TPU v7x, 128 devices: a whole 4x4x4 slice. The times are simulated.
128 devices in a mesh: panels: 128 (over x, y, z, core).
Axes of the slice: x: 4, y: 4, z: 4, core: 2. Of those that a mesh axis runs over, the one named last changes fastest.
Arguments:
- excitation: bfloat16 [64, 524288], P(None, 'panels'), may hold values from -6 to 6
- near_tiles: bfloat16 [2048, 5, 256, 256], P('panels'), may hold values from -0.15625 to 0.15625
- near_offset: int32 [2048, 5], P('panels'), may hold values from -16 to 16, as said below
- near_count: int32 [2048], P('panels'), may hold values from 1 to 5, as said below
- far_src: int32 [128, 16], replicated, may hold values from 0 to 127, as said below
- far_count: int32 [128], replicated, may hold values from 1 to 16
- source_factor: bfloat16 [16, 32, 524288], P(None, None, 'panels'), may hold values from -0.09375 to 0.09375
- target_factor: bfloat16 [16, 32, 524288], P(None, None, 'panels'), may hold values from -0.25 to 0.25
Outputs:
- krylov: float32 [5, 64, 524288], P(None, None, 'panels')
Inputs may be any that keep to these rules, and one draw needn't show every extreme that they name: `near_offset`: offsets within one leaf are distinct. `near_count`: some leaf has 5 live slots. `far_src`: within a row the entries are distinct and never the row itself. Counting live slots only, every block row is the source of at most 16 far blocks, and some block row of exactly 16.
All inputs are finite; a program needn't handle non-finite values.
Results may differ from a plain program's by a relative error of at most 0.0095.
Values may be sent and summed in bfloat16 or wider, within the bound.
No kernel may reach another device: no remote copies, remote signals or barrier semaphores. Data moves between devices by JAX's collectives and lax.ppermute only.
A program may use at most 128 MiB of HBM per device.

v0:
```python
import jax
import jax.numpy as jnp
from jax import lax
from jax.experimental import pallas as pl
from jax.experimental.pallas import tpu as pltpu
from jax.sharding import PartitionSpec as P

ITERS = 5
BATCH = 8
PARTS = 4
F32 = jnp.float32
BF16 = jnp.bfloat16
NT = (((1,), (1,)), ((), ()))
VMEM = pl.BlockSpec(memory_space=pltpu.VMEM)
SMEM = pl.BlockSpec(memory_space=pltpu.SMEM)
ANY = pl.BlockSpec(memory_space=pl.ANY)
LIMIT = 24 * 2**20


def nt(a, b):
    return lax.dot_general(a, b, NT, preferred_element_type=F32)


def pinned(x):
    return pltpu.with_memory_space_constraint(x, pltpu.VMEM)


def streamed(x):
    return pltpu.with_memory_space_constraint(x, pltpu.HBM)


def params():
    return pltpu.CompilerParams(vmem_limit_bytes=LIMIT)


def cost(flops, touched):
    return pl.CostEstimate(flops=flops, bytes_accessed=touched, transcendentals=0)


def place(dest, x, send, sem):
    slots = x.shape[0] // 16

    def copy(q):
        return pltpu.make_async_copy(x.at[pl.ds(16 * q, 16)], send.at[dest[q]], sem.at[q])

    for act in ("start", "wait"):
        for q in range(slots):

            @pl.when(dest[q] >= 0)
            def _():
                getattr(copy(q), act)()

        if act == "start":
            yield
    yield


def project(source, accs, i, leaf):
    out = []
    for h in range(2):
        part = source[h, :, :, 256 * i : 256 * i + 256]
        term = nt(part.reshape(-1, 256), leaf)
        out.append(term if accs is None else accs[h] + term)
    return out


def half_copy(factor, wide, sems, c, h):
    width = wide.shape[3] // sems.shape[0]
    cols = pl.ds(c * width, width)
    return pltpu.make_async_copy(factor.at[:, pl.ds(16 * h, 16), cols], wide.at[h, :, :, cols], sems.at[c, h])


def start_halves(factor, wide, sems):
    for c in range(sems.shape[0]):
        for h in range(2):
            half_copy(factor, wide, sems, c, h).start()


def wait_halves(factor, wide, sems, c):
    for h in range(2):
        half_copy(factor, wide, sems, c, h).wait()


def first_kernel(dest, field_in, factor, send, field, source, x, sems, psem, fsem):
    brought = pltpu.make_async_copy(field_in, field, fsem)
    brought.start()
    start_halves(factor, source, sems)
    brought.wait()
    parts = sems.shape[0]
    per = field.shape[1] // 256 // parts
    accs = None
    for c in range(parts):
        wait_halves(factor, source, sems, c)
        for i in range(c * per, c * per + per):
            accs = project(source, accs, i, field[:, 256 * i : 256 * i + 256])
    x[...] = jnp.concatenate(accs, axis=1).astype(BF16)
    for _ in place(dest, x, send, psem):
        pass


def fetch_list(lists, groups, which, base, near, tiles, sem_of):
    def body(g, carry):
        for b in range(BATCH):
            e = g * BATCH + b
            pltpu.make_async_copy(near.at[lists[which, 0, e]], tiles.at[base + e], sem_of(g)).start()
        return carry

    lax.fori_loop(0, groups, body, 0)


def arrived(near, tiles, sem, at):
    pltpu.make_async_copy(near.at[pl.ds(0, BATCH)], tiles.at[pl.ds(at, BATCH)], sem).wait()


def run_list(lists, groups, which, base, tiles, field, acc, ready=None):
    def body(g, carry):
        if ready is not None:
            ready(g)
        found = []
        for b in range(BATCH):
            e = g * BATCH + b
            at = pl.multiple_of(lists[which, 1, e], 256)
            found.append(nt(field[:, pl.ds(at, 256)], tiles[base + e]))
        for b in range(BATCH):
            e = g * BATCH + b
            acc[lists[which, 2, e]] += found[b]
        return carry

    lax.fori_loop(0, groups, body, 0)


def own_part(lists, counts, field, near, acc, others, tiles, sems, osem, also=None):
    fetch_list(lists, counts[0], 0, 0, near, tiles, lambda g: sems.at[g])
    fetch_list(lists, counts[1], 1, 0, near, others, lambda g: osem)
    fetch_list(lists, counts[2], 2, counts[1] * BATCH, near, others, lambda g: osem)
    if also is not None:
        also.start()
    acc[...] = jnp.zeros_like(acc)
    run_list(
        lists, counts[0], 0, 0, tiles, field, acc, lambda g: arrived(near, tiles, sems.at[g], g * BATCH)
    )

    def body(g, carry):
        arrived(near, others, osem, g * BATCH)
        return carry

    lax.fori_loop(0, counts[1] + counts[2], body, 0)


def setup_kernel(
    offset, count, field, near, source_factor, target_factor,
    acc, others, source, target, lists, counts, out, tiles, sems, osem, ssems, tsems,
):
    leaves = count.shape[0]
    slots = near.shape[0] // leaves

    def leaf_body(i, filled):
        def slot_body(j, filled):
            at_leaf = i + offset[j, i]
            which = jnp.where(at_leaf < 0, 1, jnp.where(at_leaf >= leaves, 2, 0))
            at = jnp.where(which == 0, filled[0], jnp.where(which == 1, filled[1], filled[2]))
            lists[which, 0, at] = i * slots + j
            lists[which, 1, at] = 256 * jnp.where(
                which == 1, at_leaf + leaves, jnp.where(which == 2, at_leaf - leaves, at_leaf)
            )
            lists[which, 2, at] = i
            return tuple(filled[w] + jnp.where(which == w, 1, 0) for w in range(3))

        return lax.fori_loop(0, count[i], slot_body, filled)

    zero = jnp.int32(0)
    filled = lax.fori_loop(0, leaves, leaf_body, (zero, zero, zero))
    for w in range(3):
        groups = (filled[w] + BATCH - 1) // BATCH

        def fill(e, carry, w=w):
            lists[w, 0, e] = 0
            lists[w, 1, e] = 0
            lists[w, 2, e] = leaves
            return carry

        lax.fori_loop(filled[w], groups * BATCH, fill, 0)
        counts[w] = groups
    start_halves(source_factor, source, ssems)
    start_halves(target_factor, target, tsems)
    own_part(lists, counts, field, near, acc, others, tiles, sems, osem)
    for c in range(ssems.shape[0]):
        wait_halves(source_factor, source, ssems, c)
        wait_halves(target_factor, target, tsems, c)


def local_kernel(step, lists, counts, field, near, done, _, acc, others, out, tiles, sems, osem, dsem):
    copy = pltpu.make_async_copy(done, out.at[step - 1], dsem)
    own_part(lists, counts, field, near, acc, others, tiles, sems, osem, copy)
    copy.wait()


def others_part(lists, counts, tiles, left, right, acc):
    run_list(lists, counts[1], 1, 0, tiles, left, acc)
    run_list(lists, counts[2], 2, counts[1] * BATCH, tiles, right, acc)


def first_others_kernel(lists, counts, tiles, left, right, source, _, acc, x):
    others_part(lists, counts, tiles, left, right, acc)
    accs = None
    for i in range(acc.shape[0] - 1):
        accs = project(source, accs, i, acc[i].astype(BF16))
    x[...] = jnp.concatenate(accs, axis=1)


def others_kernel(lists, counts, tiles, left, right, factor, _, acc, x, source, sems):
    start_halves(factor, source, sems)
    others_part(lists, counts, tiles, left, right, acc)
    parts = sems.shape[0]
    per = (acc.shape[0] - 1) // parts
    accs = None
    for c in range(parts):
        wait_halves(factor, source, sems, c)
        for i in range(c * per, c * per + per):
            accs = project(source, accs, i, acc[i].astype(BF16))
    x[...] = jnp.concatenate(accs, axis=1)


def last_others_kernel(lists, counts, tiles, left, right, _, acc):
    others_part(lists, counts, tiles, left, right, acc)


def gram_kernel(source, target, gram):
    panels = source.shape[3]
    for h in range(2):
        for g in range(2):
            gram[h, g] = nt(source[h].reshape(-1, panels), target[g].reshape(-1, panels)).astype(BF16)


def pick(far_src, far_count, received, picked):
    own = lax.axis_index("panels")
    live = far_count[own]
    for k in range(picked.shape[0] // 16):
        block = received[far_src[k, own]]
        picked[16 * k : 16 * k + 16] = jnp.where(k < live, block, jnp.zeros_like(block))


def expand(target_factor, acc, picked, wide, tsems, use, passed):
    turned = picked[...].astype(F32).T.astype(BF16)
    excite = turned.shape[0] // 2
    parts = tsems.shape[0]
    per = wide.shape[3] // 256 // parts
    for c in range(parts):
        wait_halves(target_factor, wide, tsems, c)
        for i in range(c * per, c * per + per):
            cols = slice(256 * i, 256 * i + 256)
            value = acc[i]
            for h in range(2):
                value += jnp.dot(
                    turned[excite * h : excite * h + excite],
                    wide[h, :, :, cols].reshape(-1, 256),
                    preferred_element_type=F32,
                )
            use(cols, value)
        passed(c)


def far_kernel(
    far_src, far_count, dest, received, target_factor, gram_in, acc, x, field, send, done,
    gram, picked, ready, wide, tsems, psems, gsem,
):
    brought = pltpu.make_async_copy(gram_in, gram, gsem)
    brought.start()
    start_halves(target_factor, wide, tsems)
    pick(far_src, far_count, received, picked)
    excite = picked.shape[1] // 2
    brought.wait()
    parts = []
    for h in range(2):
        part = x[:, excite * h : excite * h + excite]
        for g in range(2):
            part += jnp.dot(
                gram[h, g], picked[:, excite * g : excite * g + excite], preferred_element_type=F32
            )
        parts.append(part)
    ready[...] = jnp.concatenate(parts, axis=1).astype(BF16)
    placed = place(dest, ready, send, psems)
    next(placed)

    def use(cols, value):
        done[:, cols] = value
        field[:, cols] = value.astype(BF16)

    expand(target_factor, acc, picked, wide, tsems, use, lambda c: None)
    next(placed)


def last_kernel(step, far_src, far_count, received, target_factor, acc, _, out, picked, wide, done, tsems, osems):
    start_halves(target_factor, wide, tsems)
    pick(far_src, far_count, received, picked)
    copies = []

    def use(cols, value):
        done[:, cols] = value

    def passed(c):
        width = done.shape[1] // osems.shape[0]
        cols = pl.ds(width * c, width)
        copies.append(pltpu.make_async_copy(done.at[:, cols], out.at[step, :, cols], osems.at[c]))
        copies[-1].start()

    expand(target_factor, acc, picked, wide, tsems, use, passed)
    for copy in copies:
        copy.wait()


def far_lists(far_src, far_count, own):
    rows, slots = far_src.shape
    live = jnp.arange(slots, dtype=jnp.int32)[None, :] < far_count[:, None]
    has = jnp.any((far_src == own) & live, axis=1)
    order = jnp.arange(rows, dtype=jnp.int32)
    rank = jnp.sum((has[None, :] & (order[None, :] < order[:, None])).astype(jnp.int32), axis=1)
    hit = has[None, :] & (rank[None, :] == jnp.arange(slots, dtype=jnp.int32)[:, None])
    dest = jnp.max(jnp.where(hit, order[None, :], -1), axis=1)
    return dest


def shards(
    excitation, near_tiles, near_offset, near_count, far_src, far_count, source_factor, target_factor
):
    excite, panels = excitation.shape
    leaves, near_slots, leaf = near_tiles.shape[:3]
    rows, slots = far_src.shape
    rank = source_factor.shape[1]
    count = lax.axis_size("panels")
    dest = far_lists(far_src, far_count, lax.axis_index("panels"))

    tile_total = leaves * near_slots
    near = streamed(near_tiles.reshape(tile_total, leaf, leaf))
    source_factor, target_factor = streamed(source_factor), streamed(target_factor)
    entries = tile_total + BATCH
    half = slots * rank // 2
    send_type = pltpu.HBM((rows, rank // 2, 2 * excite), BF16)
    field_type = jax.ShapeDtypeStruct((excite, panels), BF16)
    acc_type = pltpu.VMEM((leaves + 1, excite, leaf), F32)
    out_type = pltpu.HBM((ITERS, excite, panels), F32)
    tiles_type = pltpu.VMEM((entries, leaf, leaf), BF16)
    half_type = pltpu.VMEM((2, slots, rank // 2, panels), BF16)
    done_type = pltpu.VMEM((excite, panels), F32)
    picked_type = pltpu.VMEM((half, 2 * excite), BF16)
    x_type = pltpu.VMEM((half, 2 * excite), F32)
    gram_shape = (2, 2, half, half)
    dma = pltpu.SemaphoreType.DMA
    groups = entries // BATCH
    far_flops = 2 * slots * rank * panels * excite

    def call(kernel, out_shape, in_specs, out_specs, scratch, flops, name, aliases=None):
        return pl.pallas_call(
            kernel,
            out_shape=out_shape,
            in_specs=in_specs,
            out_specs=out_specs,
            scratch_shapes=scratch,
            input_output_aliases=aliases or {},
            compiler_params=params(),
            cost_estimate=cost(flops, 2**22),
            name=name,
        )

    right_of = [(i, (i + 1) % count) for i in range(count)]
    left_of = [((i + 1) % count, i) for i in range(count)]
    field = send = lists = counts = out = gram = done = None
    turned_src = far_src.T
    for step in range(ITERS):
        if step == 0:
            send, field = call(
                first_kernel, (send_type, field_type), [SMEM, ANY, ANY], (ANY, VMEM),
                [half_type, picked_type, dma((PARTS, 2)), dma((slots,)), dma], far_flops, "first",
            )(dest, streamed(excitation), source_factor)
        left = lax.ppermute(field, "panels", right_of)
        right = lax.ppermute(field, "panels", left_of)
        received = lax.all_to_all(send, "panels", split_axis=0, concat_axis=0, tiled=True)
        own_scratch = [tiles_type, dma((groups,)), dma]
        if step == 0:
            acc, tiles, source, target, lists, counts, out = call(
                setup_kernel,
                (
                    acc_type, tiles_type, half_type, half_type,
                    jax.ShapeDtypeStruct((3, 3, entries), jnp.int32),
                    jax.ShapeDtypeStruct((3,), jnp.int32),
                    out_type,
                ),
                [SMEM, SMEM, VMEM, ANY, ANY, ANY], (VMEM, VMEM, VMEM, VMEM, SMEM, SMEM, ANY),
                [*own_scratch, dma((PARTS, 2)), dma((PARTS, 2))],
                tile_total * 2**22, "setup",
            )(near_offset.T, near_count, field, near, source_factor, target_factor)
            gram = call(
                gram_kernel, pltpu.HBM(gram_shape, BF16), [VMEM, VMEM], VMEM,
                [], 4 * half * half * panels * 2, "gram",
            )(pinned(source), pinned(target))
        else:
            acc, tiles, out = call(
                lambda *refs, step=step: local_kernel(step, *refs), (acc_type, tiles_type, out_type),
                [SMEM, SMEM, VMEM, ANY, VMEM, ANY], (VMEM, VMEM, ANY), [*own_scratch, dma],
                tile_total * 2**22, "local", {5: 2},
            )(lists, counts, field, near, pinned(done), streamed(out))
        near_operands = (lists, counts, pinned(tiles), left, right)
        if step == ITERS - 1:
            acc = call(
                last_others_kernel, acc_type, [SMEM, SMEM, VMEM, VMEM, VMEM, VMEM], VMEM,
                [], tile_total * 2**22, "others", {5: 0},
            )(*near_operands, pinned(acc))
            return call(
                lambda *refs, step=step: last_kernel(step, *refs),
                out_type, [SMEM, SMEM, VMEM, ANY, VMEM, ANY], ANY,
                [picked_type, half_type, done_type, dma((PARTS, 2)), dma((PARTS,))],
                far_flops, "last", {5: 0},
            )(turned_src, far_count, received, target_factor, pinned(acc), streamed(out))
        if step == 0:
            acc, x = call(
                first_others_kernel, (acc_type, x_type), [SMEM, SMEM, VMEM, VMEM, VMEM, VMEM, VMEM], (VMEM, VMEM),
                [], tile_total * 2**22, "others", {6: 0},
            )(*near_operands, pinned(source), pinned(acc))
        else:
            acc, x = call(
                others_kernel, (acc_type, x_type), [SMEM, SMEM, VMEM, VMEM, VMEM, ANY, VMEM], (VMEM, VMEM),
                [half_type, dma((PARTS, 2))], tile_total * 2**22, "others", {6: 0},
            )(*near_operands, source_factor, pinned(acc))
        field, send, done = call(
            far_kernel, (field_type, send_type, done_type),
            [SMEM, SMEM, SMEM, VMEM, ANY, ANY, VMEM, VMEM], (VMEM, ANY, VMEM),
            [
                pltpu.VMEM(gram_shape, BF16), picked_type, picked_type, half_type,
                dma((PARTS, 2)), dma((slots,)), dma,
            ],
            far_flops, "far",
        )(turned_src, far_count, dest, received, target_factor, streamed(gram), pinned(acc), pinned(x))


def solution(mesh):
    in_specs = (
        P(None, "panels"),
        P("panels", None, None, None),
        P("panels", None),
        P("panels"),
        P(),
        P(),
        P(None, None, "panels"),
        P(None, None, "panels"),
    )
    out_specs = P(None, None, "panels")
    return jax.shard_map(shards, mesh=mesh, in_specs=in_specs, out_specs=out_specs, check_vma=False)
```

profile of v0, /device:TPU:1, one launch (start us, length us, event | category | flops | bytes accessed | tf_op | source)
XLA Modules:
  0.0 156.1 jit_solution(371082035150888948)
XLA Ops:
  0.0 0.7 fusion.2
  1.0 4.2 %first.1 = (bf16[128,16,128]{2,1,0:T(8,128)(2,1)}, bf16[64,4096]{1,0:T(8,128)(2,1)S(1)}) custom-call(s32[16]{0:T(128)S(1)} %select_reduce_fusion.dest, bf16[64,4096]{1,0:T(8,128)(2,1)} %field_in.1, bf16[16,32,4096]{2,1,0:T(8,128)(2,1)} %factor.7), custom_call_target="tpu_custom_call" | custom-call | flops 268435456 | bytes 4194304 | tf_op jit(solution)/shard_map/first/pallas_call | solution.py:371
  5.2 3.1 %collective-permute-start = (bf16[64,4096]{1,0:T(8,128)(2,1)S(1)}, bf16[64,4096]{1,0:T(8,128)(2,1)S(1)}, u32[]{:S(2)}, u32[]{:S(2)}) collective-permute-start(bf16[64,4096]{1,0:T(8,128)(2,1)S(1)} %get-tuple-element.47.field), channel_id=1, source_target_pairs={{0,1},{1,2},{2,3},{3,4},{4,5},{5,6},{6,7},{7,8},{8,9},{9,10},{10,1... | collective-permute-start | bytes 1572872 | tf_op jit(solution)/shard_map/ppermute | solution.py:375
  8.3 10.2 %all-to-all-start = ((bf16[128,16,128]{2,1,0:T(8,128)(2,1)}), bf16[128,16,128]{2,1,0:T(8,128)(2,1)S(1)}, u32[]{:S(2)}, u32[]{:S(2)}) async-start(bf16[128,16,128]{2,1,0:T(8,128)(2,1)} %get-tuple-element.46), calls=%async_computation | async-start | bytes 1048576 | tf_op jit(solution)/shard_map/all_to_all | solution.py:377
  18.6 8.2 %setup.1 = (f32[17,64,256]{2,1,0:T(8,128)S(1)}, bf16[88,256,256]{2,1,0:T(8,128)(2,1)S(1)}, bf16[2,16,16,4096]{3,2,1,0:T(8,128)(2,1)S(1)}, bf16[2,16,16,4096]{3,2...) custom-call(s32[5,16]{1,0:T(8,128)S(1)} %bitcast.8, s32[16]{0:T(128)S(1)} %copy-done.3, ...), custom_call_target="tpu_custom_call" | custom-call | flops 335544320 | bytes 4194304 | tf_op jit(solution)/shard_map/setup/pallas_call | solution.py:380
  26.8 3.2 %gram.1.gram_in = bf16[2,2,256,256]{3,2,1,0:T(8,128)(2,1)} custom-call(bf16[2,16,16,4096]{3,2,1,0:T(8,128)(2,1)S(1)} %get-tuple-element.48.source, bf16[2,16,16,4096]{3,2,1,0:T(8,128)(2,1)S(1)} %get-tuple-element.49.target), custom_call_target="tpu_custom_call" | custom-call | flops 2147483648 | bytes 4194304 | tf_op jit(solution)/shard_map/gram/pallas_call | solution.py:392
  30.0 3.8 %others.5 = (f32[17,64,256]{2,1,0:T(8,128)S(1)}, f32[256,128]{1,0:T(8,128)S(1)}) custom-call(s32[3,3,88]{2,1,0:T(4,128)S(1)} %get-tuple-element.50.lists.refs_0_, s32[3]{0:T(128)S(1)} %get-tuple-element.51.counts.refs_1_, bf16[88,256,256]{2,1,0:T(8,128)(2,1)S(1)} %get-tuple-element.52.tiles, ...), custom_call_target="tpu_custom_call", output_to_operand_aliasing={{0}: (6, {})} | custom-call | flops 335544320 | bytes 4194304 | tf_op jit(solution)/shard_map/others/pallas_call | solution.py:415
  33.8 3.7 %far.4 = (bf16[64,4096]{1,0:T(8,128)(2,1)S(1)}, bf16[128,16,128]{2,1,0:T(8,128)(2,1)}, f32[64,4096]{1,0:T(8,128)S(1)}) custom-call(s32[16,128]{1,0:T(8,128)S(1)} %bitcast.3, s32[128]{0:T(128)S(1)} %copy-done.1, s32[16]{0:T(128)S(1)} %select_reduce_fusion.dest, bf16[128,16,128]{2,1,0:T(8,128)(2,1)S(1)} %all-to-all-done.received, ...), custom_call_target="tpu_custom_call" | custom-call | flops 268435456 | bytes 4194304 | tf_op jit(solution)/shard_map/far/pallas_call | solution.py:424
  37.5 1.9 %collective-permute-start.2 = (bf16[64,4096]{1,0:T(8,128)(2,1)S(1)}, bf16[64,4096]{1,0:T(8,128)(2,1)}, u32[]{:S(2)}, u32[]{:S(2)}) collective-permute-start(bf16[64,4096]{1,0:T(8,128)(2,1)S(1)} %get-tuple-element.57.refs_2_), channel_id=1, source_target_pairs={{0,1},{1,2},{2,3},{3,4},{4,5},{5,6},{6,7},{7,8},{8,9},{9,10},{10,1... | collective-permute-start | bytes 1572872 | tf_op jit(solution)/shard_map/ppermute | solution.py:375
  39.4 10.7 %all-to-all-start.1 = ((bf16[128,16,128]{2,1,0:T(8,128)(2,1)}), bf16[128,16,128]{2,1,0:T(8,128)(2,1)S(1)}, u32[]{:S(2)}, u32[]{:S(2)}) async-start(bf16[128,16,128]{2,1,0:T(8,128)(2,1)} %get-tuple-element.56), calls=%async_computation.1 | async-start | bytes 1048576 | tf_op jit(solution)/shard_map/all_to_all | solution.py:377
  50.1 4.6 %local.4 = (f32[17,64,256]{2,1,0:T(8,128)S(1)}, bf16[88,256,256]{2,1,0:T(8,128)(2,1)S(1)}, f32[5,64,4096]{2,1,0:T(8,128)}) custom-call(s32[3,3,88]{2,1,0:T(4,128)S(1)} %get-tuple-element.50.lists.refs_0_, s32[3]{0:T(128)S(1)} %get-tuple-element.51.counts.refs_1_, bf16[64,4096]{1,0:T(8,128)(2,1)S(1)} %get-tuple-element.57.refs_2_, ...), custom_call_target="tpu_custom_call", output_to_operand_aliasing={{2}: (5, {})} | custom-call | flops 335544320 | bytes 4194304 | tf_op jit(solution)/shard_map/local/pallas_call | solution.py:397
  54.7 4.6 %others.6 = (f32[17,64,256]{2,1,0:T(8,128)S(1)}, f32[256,128]{1,0:T(8,128)S(1)}) custom-call(s32[3,3,88]{2,1,0:T(4,128)S(1)} %get-tuple-element.50.lists.refs_0_, s32[3]{0:T(128)S(1)} %get-tuple-element.51.counts.refs_1_, bf16[88,256,256]{2,1,0:T(8,128)(2,1)S(1)} %get-tuple-element.60.tiles, ...), custom_call_target="tpu_custom_call", output_to_operand_aliasing={{0}: (6, {})} | custom-call | flops 335544320 | bytes 4194304 | tf_op jit(solution)/shard_map/others/pallas_call | solution.py:420
  59.3 4.7 %all-to-all-done.1.received = bf16[128,16,128]{2,1,0:T(8,128)(2,1)S(1)} async-done(((bf16[128,16,128]{2,1,0:T(8,128)(2,1)}), bf16[128,16,128]{2,1,0:T(8,128)(2,1)S(1)}, u32[]{:S(2)}, u32[]{:S(2)}) %all-to-all-start.1) | async-done | bytes 524320 | tf_op jit(solution)/shard_map/all_to_all | solution.py:377
  63.9 3.7 %far.5 = (bf16[64,4096]{1,0:T(8,128)(2,1)S(1)}, bf16[128,16,128]{2,1,0:T(8,128)(2,1)}, f32[64,4096]{1,0:T(8,128)S(1)}) custom-call(s32[16,128]{1,0:T(8,128)S(1)} %bitcast.4, s32[128]{0:T(128)S(1)} %copy-done.1, s32[16]{0:T(128)S(1)} %select_reduce_fusion.dest, bf16[128,16,128]{2,1,0:T(8,128)(2,1)S(1)} %all-to-all-done.1.received, ...), custom_call_target="tpu_custom_call" | custom-call | flops 268435456 | bytes 4194304 | tf_op jit(solution)/shard_map/far/pallas_call | solution.py:424
  67.6 1.2 collective-permute-start.4
  69.1 10.5 %all-to-all-start.2 = ((bf16[128,16,128]{2,1,0:T(8,128)(2,1)}), bf16[128,16,128]{2,1,0:T(8,128)(2,1)S(1)}, u32[]{:S(2)}, u32[]{:S(2)}) async-start(bf16[128,16,128]{2,1,0:T(8,128)(2,1)} %get-tuple-element.64), calls=%async_computation.2 | async-start | bytes 1048576 | tf_op jit(solution)/shard_map/all_to_all | solution.py:377
  79.6 4.6 %local.5 = (f32[17,64,256]{2,1,0:T(8,128)S(1)}, bf16[88,256,256]{2,1,0:T(8,128)(2,1)S(1)}, f32[5,64,4096]{2,1,0:T(8,128)}) custom-call(s32[3,3,88]{2,1,0:T(4,128)S(1)} %get-tuple-element.50.lists.refs_0_, s32[3]{0:T(128)S(1)} %get-tuple-element.51.counts.refs_1_, bf16[64,4096]{1,0:T(8,128)(2,1)S(1)} %get-tuple-element.65.refs_2_, ...), custom_call_target="tpu_custom_call", output_to_operand_aliasing={{2}: (5, {})} | custom-call | flops 335544320 | bytes 4194304 | tf_op jit(solution)/shard_map/local/pallas_call | solution.py:397
  84.2 4.6 %others.7 = (f32[17,64,256]{2,1,0:T(8,128)S(1)}, f32[256,128]{1,0:T(8,128)S(1)}) custom-call(s32[3,3,88]{2,1,0:T(4,128)S(1)} %get-tuple-element.50.lists.refs_0_, s32[3]{0:T(128)S(1)} %get-tuple-element.51.counts.refs_1_, bf16[88,256,256]{2,1,0:T(8,128)(2,1)S(1)} %get-tuple-element.68.tiles, ...), custom_call_target="tpu_custom_call", output_to_operand_aliasing={{0}: (6, {})} | custom-call | flops 335544320 | bytes 4194304 | tf_op jit(solution)/shard_map/others/pallas_call | solution.py:420
  88.7 4.7 %all-to-all-done.2.received = bf16[128,16,128]{2,1,0:T(8,128)(2,1)S(1)} async-done(((bf16[128,16,128]{2,1,0:T(8,128)(2,1)}), bf16[128,16,128]{2,1,0:T(8,128)(2,1)S(1)}, u32[]{:S(2)}, u32[]{:S(2)}) %all-to-all-start.2) | async-done | bytes 524320 | tf_op jit(solution)/shard_map/all_to_all | solution.py:377
  93.4 3.7 %far.6 = (bf16[64,4096]{1,0:T(8,128)(2,1)S(1)}, bf16[128,16,128]{2,1,0:T(8,128)(2,1)}, f32[64,4096]{1,0:T(8,128)S(1)}) custom-call(s32[16,128]{1,0:T(8,128)S(1)} %bitcast.5, s32[128]{0:T(128)S(1)} %copy-done.1, s32[16]{0:T(128)S(1)} %select_reduce_fusion.dest, bf16[128,16,128]{2,1,0:T(8,128)(2,1)S(1)} %all-to-all-done.2.received, ...), custom_call_target="tpu_custom_call" | custom-call | flops 268435456 | bytes 4194304 | tf_op jit(solution)/shard_map/far/pallas_call | solution.py:424
  97.1 1.0 collective-permute-start.6
  98.4 10.5 %all-to-all-start.3 = ((bf16[128,16,128]{2,1,0:T(8,128)(2,1)}), bf16[128,16,128]{2,1,0:T(8,128)(2,1)S(1)}, u32[]{:S(2)}, u32[]{:S(2)}) async-start(bf16[128,16,128]{2,1,0:T(8,128)(2,1)} %get-tuple-element.72), calls=%async_computation.3 | async-start | bytes 1048576 | tf_op jit(solution)/shard_map/all_to_all | solution.py:377
  108.9 4.6 %local.6 = (f32[17,64,256]{2,1,0:T(8,128)S(1)}, bf16[88,256,256]{2,1,0:T(8,128)(2,1)S(1)}, f32[5,64,4096]{2,1,0:T(8,128)}) custom-call(s32[3,3,88]{2,1,0:T(4,128)S(1)} %get-tuple-element.50.lists.refs_0_, s32[3]{0:T(128)S(1)} %get-tuple-element.51.counts.refs_1_, bf16[64,4096]{1,0:T(8,128)(2,1)S(1)} %get-tuple-element.73.refs_2_, ...), custom_call_target="tpu_custom_call", output_to_operand_aliasing={{2}: (5, {})} | custom-call | flops 335544320 | bytes 4194304 | tf_op jit(solution)/shard_map/local/pallas_call | solution.py:397
  113.5 4.6 %others.8 = (f32[17,64,256]{2,1,0:T(8,128)S(1)}, f32[256,128]{1,0:T(8,128)S(1)}) custom-call(s32[3,3,88]{2,1,0:T(4,128)S(1)} %get-tuple-element.50.lists.refs_0_, s32[3]{0:T(128)S(1)} %get-tuple-element.51.counts.refs_1_, bf16[88,256,256]{2,1,0:T(8,128)(2,1)S(1)} %get-tuple-element.76.tiles, ...), custom_call_target="tpu_custom_call", output_to_operand_aliasing={{0}: (6, {})} | custom-call | flops 335544320 | bytes 4194304 | tf_op jit(solution)/shard_map/others/pallas_call | solution.py:420
  118.0 4.7 %all-to-all-done.3.received = bf16[128,16,128]{2,1,0:T(8,128)(2,1)S(1)} async-done(((bf16[128,16,128]{2,1,0:T(8,128)(2,1)}), bf16[128,16,128]{2,1,0:T(8,128)(2,1)S(1)}, u32[]{:S(2)}, u32[]{:S(2)}) %all-to-all-start.3) | async-done | bytes 524320 | tf_op jit(solution)/shard_map/all_to_all | solution.py:377
  122.7 3.7 %far.7 = (bf16[64,4096]{1,0:T(8,128)(2,1)S(1)}, bf16[128,16,128]{2,1,0:T(8,128)(2,1)}, f32[64,4096]{1,0:T(8,128)S(1)}) custom-call(s32[16,128]{1,0:T(8,128)S(1)} %bitcast.6, s32[128]{0:T(128)S(1)} %copy-done.1, s32[16]{0:T(128)S(1)} %select_reduce_fusion.dest, bf16[128,16,128]{2,1,0:T(8,128)(2,1)S(1)} %all-to-all-done.3.received, ...), custom_call_target="tpu_custom_call" | custom-call | flops 268435456 | bytes 4194304 | tf_op jit(solution)/shard_map/far/pallas_call | solution.py:424
  126.4 1.0 collective-permute-start.8
  127.7 10.5 %all-to-all-start.4 = ((bf16[128,16,128]{2,1,0:T(8,128)(2,1)}), bf16[128,16,128]{2,1,0:T(8,128)(2,1)S(1)}, u32[]{:S(2)}, u32[]{:S(2)}) async-start(bf16[128,16,128]{2,1,0:T(8,128)(2,1)} %get-tuple-element.80), calls=%async_computation.4 | async-start | bytes 1048576 | tf_op jit(solution)/shard_map/all_to_all | solution.py:377
  138.2 4.6 %local.7 = (f32[17,64,256]{2,1,0:T(8,128)S(1)}, bf16[88,256,256]{2,1,0:T(8,128)(2,1)S(1)}, f32[5,64,4096]{2,1,0:T(8,128)}) custom-call(s32[3,3,88]{2,1,0:T(4,128)S(1)} %get-tuple-element.50.lists.refs_0_, s32[3]{0:T(128)S(1)} %get-tuple-element.51.counts.refs_1_, bf16[64,4096]{1,0:T(8,128)(2,1)S(1)} %get-tuple-element.81.refs_2_, ...), custom_call_target="tpu_custom_call", output_to_operand_aliasing={{2}: (5, {})} | custom-call | flops 335544320 | bytes 4194304 | tf_op jit(solution)/shard_map/local/pallas_call | solution.py:397
  142.8 3.0 %others.9.refs_4_ = f32[17,64,256]{2,1,0:T(8,128)S(1)} custom-call(s32[3,3,88]{2,1,0:T(4,128)S(1)} %get-tuple-element.50.lists.refs_0_, s32[3]{0:T(128)S(1)} %get-tuple-element.51.counts.refs_1_, bf16[88,256,256]{2,1,0:T(8,128)(2,1)S(1)} %get-tuple-element.84.tiles, bf16[64,4096]{1,0:T(8,128)(2,1)} %collective-permute-done.8.left, ...), custom_call_target="tpu_custom_call", output_to_operand_aliasing={{}: (5, {})} | custom-call | flops 335544320 | bytes 4194304 | tf_op jit(solution)/shard_map/others/pallas_call | solution.py:404
  145.8 6.2 %all-to-all-done.4.refs_2_ = bf16[128,16,128]{2,1,0:T(8,128)(2,1)S(1)} async-done(((bf16[128,16,128]{2,1,0:T(8,128)(2,1)}), bf16[128,16,128]{2,1,0:T(8,128)(2,1)S(1)}, u32[]{:S(2)}, u32[]{:S(2)}) %all-to-all-start.4) | async-done | bytes 524320 | tf_op jit(solution)/shard_map/all_to_all | solution.py:377
  152.0 3.9 %last.1 = f32[5,64,4096]{2,1,0:T(8,128)} custom-call(s32[16,128]{1,0:T(8,128)S(1)} %bitcast.7, s32[128]{0:T(128)S(1)} %copy-done.1, bf16[128,16,128]{2,1,0:T(8,128)(2,1)S(1)} %all-to-all-done.4.refs_2_, bf16[16,32,4096]{2,1,0:T(8,128)(2,1)} %refs_3_.1, f32[17,64,256]{2,1,0:T(8,128)S(1)} %others.9.refs_4_, ...), custom_call_target="tpu_custom_call", output_to_operand_aliasing={{}: (5, {})} | custom-call | flops 268435456 | bytes 4194304 | tf_op jit(solution)/shard_map/last/pallas_call | solution.py:408
  (26 shorter events, 1.2 us)
Async XLA Ops:
  0.0 18.5 %copy-start.2 = (s32[16,5]{0,1:T(8,128)S(1)}, s32[16,5]{0,1:T(8,128)}, u32[]{:S(2)}) copy-start(s32[16,5]{0,1:T(8,128)} %param.10) | copy-start | bytes 964
  0.0 18.5 %copy-start.3 = (s32[16]{0:T(128)S(1)}, s32[16]{0:T(128)}, u32[]{:S(2)}) copy-start(s32[16]{0:T(128)} %count.1) | copy-start | bytes 196
  5.2 24.8 %collective-permute-start = (bf16[64,4096]{1,0:T(8,128)(2,1)S(1)}, bf16[64,4096]{1,0:T(8,128)(2,1)S(1)}, u32[]{:S(2)}, u32[]{:S(2)}) collective-permute-start(bf16[64,4096]{1,0:T(8,128)(2,1)S(1)} %get-tuple-element.47.field), channel_id=1, source_target_pairs={{0,1},{1,2},{2,3},{3,4},{4,5},{5,6},{6,7},{7,8},{8,9},{9,10},{10,1... | collective-permute-start | bytes 1572872 | tf_op jit(solution)/shard_map/ppermute | solution.py:375
  8.3 21.7 %collective-permute-start.1 = (bf16[64,4096]{1,0:T(8,128)(2,1)S(1)}, bf16[64,4096]{1,0:T(8,128)(2,1)S(1)}, u32[]{:S(2)}, u32[]{:S(2)}) collective-permute-start(bf16[64,4096]{1,0:T(8,128)(2,1)S(1)} %get-tuple-element.47.field), channel_id=1, source_target_pairs={{1,0},{2,1},{3,2},{4,3},{5,4},{6,5},{7,6},{8,7},{9,8},{10,9},{11,1... | collective-permute-start | bytes 1572872 | tf_op jit(solution)/shard_map/ppermute | solution.py:376
  8.3 25.5 %all-to-all-start = ((bf16[128,16,128]{2,1,0:T(8,128)(2,1)}), bf16[128,16,128]{2,1,0:T(8,128)(2,1)S(1)}, u32[]{:S(2)}, u32[]{:S(2)}) async-start(bf16[128,16,128]{2,1,0:T(8,128)(2,1)} %get-tuple-element.46), calls=%async_computation | async-start | bytes 1048576 | tf_op jit(solution)/shard_map/all_to_all | solution.py:377
  30.0 3.8 %copy-start = (s32[128,16]{0,1:T(8,128)S(1)}, s32[128,16]{0,1:T(8,128)}, u32[]{:S(2)}) copy-start(s32[128,16]{0,1:T(8,128)} %param.12) | copy-start | bytes 24580
  30.0 3.8 %copy-start.1 = (s32[128]{0:T(128)S(1)}, s32[128]{0:T(128)}, u32[]{:S(2)}) copy-start(s32[128]{0:T(128)} %refs_1_.1) | copy-start | bytes 1540
  37.5 17.2 %collective-permute-start.2 = (bf16[64,4096]{1,0:T(8,128)(2,1)S(1)}, bf16[64,4096]{1,0:T(8,128)(2,1)}, u32[]{:S(2)}, u32[]{:S(2)}) collective-permute-start(bf16[64,4096]{1,0:T(8,128)(2,1)S(1)} %get-tuple-element.57.refs_2_), channel_id=1, source_target_pairs={{0,1},{1,2},{2,3},{3,4},{4,5},{5,6},{6,7},{7,8},{8,9},{9,10},{10,1... | collective-permute-start | bytes 1572872 | tf_op jit(solution)/shard_map/ppermute | solution.py:375
  39.4 15.3 %collective-permute-start.3 = (bf16[64,4096]{1,0:T(8,128)(2,1)S(1)}, bf16[64,4096]{1,0:T(8,128)(2,1)}, u32[]{:S(2)}, u32[]{:S(2)}) collective-permute-start(bf16[64,4096]{1,0:T(8,128)(2,1)S(1)} %get-tuple-element.57.refs_2_), channel_id=1, source_target_pairs={{1,0},{2,1},{3,2},{4,3},{5,4},{6,5},{7,6},{8,7},{9,8},{10,9},{11,1... | collective-permute-start | bytes 1572872 | tf_op jit(solution)/shard_map/ppermute | solution.py:376
  39.4 24.6 %all-to-all-start.1 = ((bf16[128,16,128]{2,1,0:T(8,128)(2,1)}), bf16[128,16,128]{2,1,0:T(8,128)(2,1)S(1)}, u32[]{:S(2)}, u32[]{:S(2)}) async-start(bf16[128,16,128]{2,1,0:T(8,128)(2,1)} %get-tuple-element.56), calls=%async_computation.1 | async-start | bytes 1048576 | tf_op jit(solution)/shard_map/all_to_all | solution.py:377
  67.6 16.6 %collective-permute-start.4 = (bf16[64,4096]{1,0:T(8,128)(2,1)S(1)}, bf16[64,4096]{1,0:T(8,128)(2,1)}, u32[]{:S(2)}, u32[]{:S(2)}) collective-permute-start(bf16[64,4096]{1,0:T(8,128)(2,1)S(1)} %get-tuple-element.65.refs_2_), channel_id=1, source_target_pairs={{0,1},{1,2},{2,3},{3,4},{4,5},{5,6},{6,7},{7,8},{8,9},{9,10},{10,1... | collective-permute-start | bytes 1572872 | tf_op jit(solution)/shard_map/ppermute | solution.py:375
  68.8 15.4 %collective-permute-start.5 = (bf16[64,4096]{1,0:T(8,128)(2,1)S(1)}, bf16[64,4096]{1,0:T(8,128)(2,1)}, u32[]{:S(2)}, u32[]{:S(2)}) collective-permute-start(bf16[64,4096]{1,0:T(8,128)(2,1)S(1)} %get-tuple-element.65.refs_2_), channel_id=1, source_target_pairs={{1,0},{2,1},{3,2},{4,3},{5,4},{6,5},{7,6},{8,7},{9,8},{10,9},{11,1... | collective-permute-start | bytes 1572872 | tf_op jit(solution)/shard_map/ppermute | solution.py:376
  69.1 24.3 %all-to-all-start.2 = ((bf16[128,16,128]{2,1,0:T(8,128)(2,1)}), bf16[128,16,128]{2,1,0:T(8,128)(2,1)S(1)}, u32[]{:S(2)}, u32[]{:S(2)}) async-start(bf16[128,16,128]{2,1,0:T(8,128)(2,1)} %get-tuple-element.64), calls=%async_computation.2 | async-start | bytes 1048576 | tf_op jit(solution)/shard_map/all_to_all | solution.py:377
  97.1 16.4 %collective-permute-start.6 = (bf16[64,4096]{1,0:T(8,128)(2,1)S(1)}, bf16[64,4096]{1,0:T(8,128)(2,1)}, u32[]{:S(2)}, u32[]{:S(2)}) collective-permute-start(bf16[64,4096]{1,0:T(8,128)(2,1)S(1)} %get-tuple-element.73.refs_2_), channel_id=1, source_target_pairs={{0,1},{1,2},{2,3},{3,4},{4,5},{5,6},{6,7},{7,8},{8,9},{9,10},{10,1... | collective-permute-start | bytes 1572872 | tf_op jit(solution)/shard_map/ppermute | solution.py:375
  98.1 15.4 %collective-permute-start.7 = (bf16[64,4096]{1,0:T(8,128)(2,1)S(1)}, bf16[64,4096]{1,0:T(8,128)(2,1)}, u32[]{:S(2)}, u32[]{:S(2)}) collective-permute-start(bf16[64,4096]{1,0:T(8,128)(2,1)S(1)} %get-tuple-element.73.refs_2_), channel_id=1, source_target_pairs={{1,0},{2,1},{3,2},{4,3},{5,4},{6,5},{7,6},{8,7},{9,8},{10,9},{11,1... | collective-permute-start | bytes 1572872 | tf_op jit(solution)/shard_map/ppermute | solution.py:376
  98.4 24.3 %all-to-all-start.3 = ((bf16[128,16,128]{2,1,0:T(8,128)(2,1)}), bf16[128,16,128]{2,1,0:T(8,128)(2,1)S(1)}, u32[]{:S(2)}, u32[]{:S(2)}) async-start(bf16[128,16,128]{2,1,0:T(8,128)(2,1)} %get-tuple-element.72), calls=%async_computation.3 | async-start | bytes 1048576 | tf_op jit(solution)/shard_map/all_to_all | solution.py:377
  126.4 16.4 %collective-permute-start.8 = (bf16[64,4096]{1,0:T(8,128)(2,1)S(1)}, bf16[64,4096]{1,0:T(8,128)(2,1)}, u32[]{:S(2)}, u32[]{:S(2)}) collective-permute-start(bf16[64,4096]{1,0:T(8,128)(2,1)S(1)} %get-tuple-element.81.refs_2_), channel_id=1, source_target_pairs={{0,1},{1,2},{2,3},{3,4},{4,5},{5,6},{6,7},{7,8},{8,9},{9,10},{10,1... | collective-permute-start | bytes 1572872 | tf_op jit(solution)/shard_map/ppermute | solution.py:375
  127.4 15.4 %collective-permute-start.9 = (bf16[64,4096]{1,0:T(8,128)(2,1)S(1)}, bf16[64,4096]{1,0:T(8,128)(2,1)}, u32[]{:S(2)}, u32[]{:S(2)}) collective-permute-start(bf16[64,4096]{1,0:T(8,128)(2,1)S(1)} %get-tuple-element.81.refs_2_), channel_id=1, source_target_pairs={{1,0},{2,1},{3,2},{4,3},{5,4},{6,5},{7,6},{8,7},{9,8},{10,9},{11,1... | collective-permute-start | bytes 1572872 | tf_op jit(solution)/shard_map/ppermute | solution.py:376
  127.7 24.3 %all-to-all-start.4 = ((bf16[128,16,128]{2,1,0:T(8,128)(2,1)}), bf16[128,16,128]{2,1,0:T(8,128)(2,1)S(1)}, u32[]{:S(2)}, u32[]{:S(2)}) async-start(bf16[128,16,128]{2,1,0:T(8,128)(2,1)} %get-tuple-element.80), calls=%async_computation.4 | async-start | bytes 1048576 | tf_op jit(solution)/shard_map/all_to_all | solution.py:377
where the time goes:
time: 157 us; the launch traced here: 156 us
  Pallas kernels  72.9 us (46%)
  starting transfers between devices  61.5 us (39%)
  waiting for transfers between devices  20.2 us (13%)
    all_to_all x5, starting transfers between devices, shards(): lax.all_to_all(send, 'panels', split_axis=0, concat_axis=0, tiled=True)  52.5 us
    all_to_all x5, waiting for transfers between devices, shards(): lax.all_to_all(send, 'panels', split_axis=0, concat_axis=0, tiled=True)  20.2 us
    pallas_call x4, Pallas kernels, shards(): call(lambda *refs, step=step: local_kernel(step, *refs), (acc_type, tiles...  18.2 us
    pallas_call x4, Pallas kernels, shards(): call(far_kernel, (field_type, send_type, done_type), [SMEM, SMEM, SMEM, V...  14.7 us
    pallas_call x3, Pallas kernels, shards(): call(others_kernel, (acc_type, x_type), [SMEM, SMEM, VMEM, VMEM, VMEM, AN...  13.7 us
    pallas_call x1, Pallas kernels, shards(): call(setup_kernel, (acc_type, tiles_type, half_type, half_type, jax.Shape...  8.23 us
    ppermute x5, starting transfers between devices, shards(): left = lax.ppermute(field, 'panels', right_of)  8.2 us
    pallas_call x1, Pallas kernels, shards(): call(first_kernel, (send_type, field_type), [SMEM, ANY, ANY], (ANY, VMEM)...  4.19 us
  transfers between devices with their start and end apart: 15, of which 4 were waited for; matrix products, arithmetic and copies ran while one was open for 0% of the time, Pallas kernels for 32%

commit v1 on v0

--- a/solution.py
+++ b/solution.py
@@ -129,48 +129,62 @@
     lax.fori_loop(0, groups, body, 0)
 
 
-def own_part(lists, counts, field, near, acc, others, tiles, sems, osem, also=None):
+def own_part(lists, counts, field, mate, near, acc, others, tiles, sems, osem, both, bsems, between=None):
+    panels = field.shape[1]
+    brought = [
+        pltpu.make_async_copy(part, both.at[:, pl.ds(panels * k, panels)], bsems.at[k])
+        for k, part in enumerate((field, mate))
+    ]
+    for copy in brought:
+        copy.start()
     fetch_list(lists, counts[0], 0, 0, near, tiles, lambda g: sems.at[g])
     fetch_list(lists, counts[1], 1, 0, near, others, lambda g: osem)
-    fetch_list(lists, counts[2], 2, counts[1] * BATCH, near, others, lambda g: osem)
-    if also is not None:
-        also.start()
+    if between is not None:
+        between()
     acc[...] = jnp.zeros_like(acc)
-    run_list(
-        lists, counts[0], 0, 0, tiles, field, acc, lambda g: arrived(near, tiles, sems.at[g], g * BATCH)
-    )
+    for copy in brought:
+        copy.wait()
+
+    def ready(g):
+        arrived(near, tiles, sems.at[g], g * BATCH)
+
+    run_list(lists, counts[0], 0, 0, tiles, both, acc, ready)
 
     def body(g, carry):
         arrived(near, others, osem, g * BATCH)
         return carry
 
-    lax.fori_loop(0, counts[1] + counts[2], body, 0)
+    lax.fori_loop(0, counts[1], body, 0)
 
 
 def setup_kernel(
-    offset, count, field, near, source_factor, target_factor,
-    acc, others, source, target, lists, counts, out, tiles, sems, osem, ssems, tsems,
+    offset, count, field, mate, near, source_factor, target_factor,
+    acc, others, source, gram, lists, counts, out, tiles, sems, osem, mate_here, msem, target, ssems, tsems,
 ):
+    start_halves(source_factor, source, ssems)
+    start_halves(target_factor, target, tsems)
     leaves = count.shape[0]
     slots = near.shape[0] // leaves
+    odd = lax.axis_index("panels") % 2
 
     def leaf_body(i, filled):
         def slot_body(j, filled):
             at_leaf = i + offset[j, i]
-            which = jnp.where(at_leaf < 0, 1, jnp.where(at_leaf >= leaves, 2, 0))
-            at = jnp.where(which == 0, filled[0], jnp.where(which == 1, filled[1], filled[2]))
+            outside = (at_leaf < 0) | (at_leaf >= leaves)
+            off_chip = jnp.where(odd == 1, at_leaf >= leaves, at_leaf < 0)
+            which = jnp.where(off_chip, 1, 0)
+            inside = jnp.where(at_leaf < 0, at_leaf + leaves, jnp.where(at_leaf >= leaves, at_leaf - leaves, at_leaf))
+            at = jnp.where(off_chip, filled[1], filled[0])
             lists[which, 0, at] = i * slots + j
-            lists[which, 1, at] = 256 * jnp.where(
-                which == 1, at_leaf + leaves, jnp.where(which == 2, at_leaf - leaves, at_leaf)
-            )
+            lists[which, 1, at] = 256 * (inside + jnp.where(outside & ~off_chip, leaves, 0))
             lists[which, 2, at] = i
-            return tuple(filled[w] + jnp.where(which == w, 1, 0) for w in range(3))
+            return filled[0] + 1 - which, filled[1] + which
 
         return lax.fori_loop(0, count[i], slot_body, filled)
 
     zero = jnp.int32(0)
-    filled = lax.fori_loop(0, leaves, leaf_body, (zero, zero, zero))
-    for w in range(3):
+    filled = lax.fori_loop(0, leaves, leaf_body, (zero, zero))
+    for w in range(2):
         groups = (filled[w] + BATCH - 1) // BATCH
 
         def fill(e, carry, w=w):
@@ -181,36 +195,43 @@
 
         lax.fori_loop(filled[w], groups * BATCH, fill, 0)
         counts[w] = groups
-    start_halves(source_factor, source, ssems)
-    start_halves(target_factor, target, tsems)
-    own_part(lists, counts, field, near, acc, others, tiles, sems, osem)
-    for c in range(ssems.shape[0]):
-        wait_halves(source_factor, source, ssems, c)
-        wait_halves(target_factor, target, tsems, c)
-
-
-def local_kernel(step, lists, counts, field, near, done, _, acc, others, out, tiles, sems, osem, dsem):
-    copy = pltpu.make_async_copy(done, out.at[step - 1], dsem)
-    own_part(lists, counts, field, near, acc, others, tiles, sems, osem, copy)
+
+    def couple():
+        panels = source.shape[3]
+        for c in range(ssems.shape[0]):
+            wait_halves(source_factor, source, ssems, c)
+            wait_halves(target_factor, target, tsems, c)
+        for h in range(2):
+            for g in range(2):
+                gram[h, g] = nt(source[h].reshape(-1, panels), target[g].reshape(-1, panels)).astype(BF16)
+
+    own_part(lists, counts, field, mate, near, acc, others, tiles, sems, osem, mate_here, msem, couple)
+
+
+def local_kernel(step, lists, counts, field, mate, near, tail, _, acc, others, out, *scratch):
+    *scratch, sem = scratch
+    width = tail.shape[1]
+    copy = pltpu.make_async_copy(tail, out.at[step - 1, :, pl.ds(out.shape[2] - width, width)], sem)
+    copy.start()
+    own_part(lists, counts, field, mate, near, acc, others, *scratch)
     copy.wait()
 
 
-def others_part(lists, counts, tiles, left, right, acc):
-    run_list(lists, counts[1], 1, 0, tiles, left, acc)
-    run_list(lists, counts[2], 2, counts[1] * BATCH, tiles, right, acc)
-
-
-def first_others_kernel(lists, counts, tiles, left, right, source, _, acc, x):
-    others_part(lists, counts, tiles, left, right, acc)
+def others_part(lists, counts, tiles, outer, acc):
+    run_list(lists, counts[1], 1, 0, tiles, outer, acc)
+
+
+def first_others_kernel(lists, counts, tiles, outer, source, _, acc, x):
+    others_part(lists, counts, tiles, outer, acc)
     accs = None
     for i in range(acc.shape[0] - 1):
         accs = project(source, accs, i, acc[i].astype(BF16))
     x[...] = jnp.concatenate(accs, axis=1)
 
 
-def others_kernel(lists, counts, tiles, left, right, factor, _, acc, x, source, sems):
+def others_kernel(lists, counts, tiles, outer, factor, _, acc, x, source, sems):
     start_halves(factor, source, sems)
-    others_part(lists, counts, tiles, left, right, acc)
+    others_part(lists, counts, tiles, outer, acc)
     parts = sems.shape[0]
     per = (acc.shape[0] - 1) // parts
     accs = None
@@ -221,15 +242,8 @@
     x[...] = jnp.concatenate(accs, axis=1)
 
 
-def last_others_kernel(lists, counts, tiles, left, right, _, acc):
-    others_part(lists, counts, tiles, left, right, acc)
-
-
-def gram_kernel(source, target, gram):
-    panels = source.shape[3]
-    for h in range(2):
-        for g in range(2):
-            gram[h, g] = nt(source[h].reshape(-1, panels), target[g].reshape(-1, panels)).astype(BF16)
+def last_others_kernel(lists, counts, tiles, outer, _, acc):
+    others_part(lists, counts, tiles, outer, acc)
 
 
 def pick(far_src, far_count, received, picked):
@@ -261,8 +275,8 @@
 
 
 def far_kernel(
-    far_src, far_count, dest, received, target_factor, gram_in, acc, x, field, send, done,
-    gram, picked, ready, wide, tsems, psems, gsem,
+    step, far_src, far_count, dest, received, target_factor, gram_in, acc, x, _, field, send, out, tail,
+    gram, picked, ready, wide, done, tsems, psems, gsem, osems,
 ):
     brought = pltpu.make_async_copy(gram_in, gram, gsem)
     brought.start()
@@ -282,12 +296,32 @@
     placed = place(dest, ready, send, psems)
     next(placed)
 
+    kept = done.shape[1]
+
     def use(cols, value):
-        done[:, cols] = value
+        if cols.start < kept:
+            done[:, cols] = value
+        else:
+            tail[:, cols.start - kept : cols.stop - kept] = value
         field[:, cols] = value.astype(BF16)
 
-    expand(target_factor, acc, picked, wide, tsems, use, lambda c: None)
+    copies = []
+
+    def passed(c):
+        if c < osems.shape[0]:
+            store_part(step, c, done, out, osems, copies)
+
+    expand(target_factor, acc, picked, wide, tsems, use, passed)
     next(placed)
+    for copy in copies:
+        copy.wait()
+
+
+def store_part(step, c, done, out, osems, copies):
+    width = done.shape[1] // osems.shape[0]
+    cols = pl.ds(width * c, width)
+    copies.append(pltpu.make_async_copy(done.at[:, cols], out.at[step, :, cols], osems.at[c]))
+    copies[-1].start()
 
 
 def last_kernel(step, far_src, far_count, received, target_factor, acc, _, out, picked, wide, done, tsems, osems):
@@ -298,13 +332,7 @@
     def use(cols, value):
         done[:, cols] = value
 
-    def passed(c):
-        width = done.shape[1] // osems.shape[0]
-        cols = pl.ds(width * c, width)
-        copies.append(pltpu.make_async_copy(done.at[:, cols], out.at[step, :, cols], osems.at[c]))
-        copies[-1].start()
-
-    expand(target_factor, acc, picked, wide, tsems, use, passed)
+    expand(target_factor, acc, picked, wide, tsems, use, lambda c: store_part(step, c, done, out, osems, copies))
     for copy in copies:
         copy.wait()
 
@@ -362,9 +390,9 @@
             name=name,
         )
 
-    right_of = [(i, (i + 1) % count) for i in range(count)]
-    left_of = [((i + 1) % count, i) for i in range(count)]
-    field = send = lists = counts = out = gram = done = None
+    outward = [(i, (i + 2 * (i % 2) - 1) % count) for i in range(count)]
+    inward = [(i, i + 1 - 2 * (i % 2)) for i in range(count)]
+    field = send = lists = counts = out = gram = None
     turned_src = far_src.T
     for step in range(ITERS):
         if step == 0:
@@ -372,38 +400,34 @@
                 first_kernel, (send_type, field_type), [SMEM, ANY, ANY], (ANY, VMEM),
                 [half_type, picked_type, dma((PARTS, 2)), dma((slots,)), dma], far_flops, "first",
             )(dest, streamed(excitation), source_factor)
-        left = lax.ppermute(field, "panels", right_of)
-        right = lax.ppermute(field, "panels", left_of)
+        outer = lax.ppermute(field, "panels", outward)
+        mate = lax.ppermute(field, "panels", inward)
         received = lax.all_to_all(send, "panels", split_axis=0, concat_axis=0, tiled=True)
-        own_scratch = [tiles_type, dma((groups,)), dma]
+        own_scratch = [tiles_type, dma((groups,)), dma, pltpu.VMEM((excite, 2 * panels), BF16), dma((2,))]
         if step == 0:
-            acc, tiles, source, target, lists, counts, out = call(
+            acc, tiles, source, gram, lists, counts, out = call(
                 setup_kernel,
                 (
-                    acc_type, tiles_type, half_type, half_type,
-                    jax.ShapeDtypeStruct((3, 3, entries), jnp.int32),
-                    jax.ShapeDtypeStruct((3,), jnp.int32),
+                    acc_type, tiles_type, half_type, pltpu.HBM(gram_shape, BF16),
+                    jax.ShapeDtypeStruct((2, 3, entries), jnp.int32),
+                    jax.ShapeDtypeStruct((2,), jnp.int32),
                     out_type,
                 ),
-                [SMEM, SMEM, VMEM, ANY, ANY, ANY], (VMEM, VMEM, VMEM, VMEM, SMEM, SMEM, ANY),
-                [*own_scratch, dma((PARTS, 2)), dma((PARTS, 2))],
+                [SMEM, SMEM, ANY, ANY, ANY, ANY, ANY], (VMEM, VMEM, VMEM, VMEM, SMEM, SMEM, ANY),
+                [*own_scratch, half_type, dma((PARTS, 2)), dma((PARTS, 2))],
                 tile_total * 2**22, "setup",
-            )(near_offset.T, near_count, field, near, source_factor, target_factor)
-            gram = call(
-                gram_kernel, pltpu.HBM(gram_shape, BF16), [VMEM, VMEM], VMEM,
-                [], 4 * half * half * panels * 2, "gram",
-            )(pinned(source), pinned(target))
+            )(near_offset.T, near_count, field, mate, near, source_factor, target_factor)
         else:
             acc, tiles, out = call(
                 lambda *refs, step=step: local_kernel(step, *refs), (acc_type, tiles_type, out_type),
-                [SMEM, SMEM, VMEM, ANY, VMEM, ANY], (VMEM, VMEM, ANY), [*own_scratch, dma],
-                tile_total * 2**22, "local", {5: 2},
-            )(lists, counts, field, near, pinned(done), streamed(out))
-        near_operands = (lists, counts, pinned(tiles), left, right)
+                [SMEM, SMEM, ANY, ANY, ANY, VMEM, ANY], (VMEM, VMEM, ANY), [*own_scratch, dma],
+                tile_total * 2**22, "local", {6: 2},
+            )(lists, counts, field, mate, near, pinned(tail), streamed(out))
+        near_operands = (lists, counts, pinned(tiles), outer)
         if step == ITERS - 1:
             acc = call(
-                last_others_kernel, acc_type, [SMEM, SMEM, VMEM, VMEM, VMEM, VMEM], VMEM,
-                [], tile_total * 2**22, "others", {5: 0},
+                last_others_kernel, acc_type, [SMEM, SMEM, VMEM, VMEM, VMEM], VMEM,
+                [], tile_total * 2**22, "others", {4: 0},
             )(*near_operands, pinned(acc))
             return call(
                 lambda *refs, step=step: last_kernel(step, *refs),
@@ -413,23 +437,29 @@
             )(turned_src, far_count, received, target_factor, pinned(acc), streamed(out))
         if step == 0:
             acc, x = call(
-                first_others_kernel, (acc_type, x_type), [SMEM, SMEM, VMEM, VMEM, VMEM, VMEM, VMEM], (VMEM, VMEM),
-                [], tile_total * 2**22, "others", {6: 0},
+                first_others_kernel, (acc_type, x_type), [SMEM, SMEM, VMEM, VMEM, VMEM, VMEM], (VMEM, VMEM),
+                [], tile_total * 2**22, "others", {5: 0},
             )(*near_operands, pinned(source), pinned(acc))
         else:
             acc, x = call(
-                others_kernel, (acc_type, x_type), [SMEM, SMEM, VMEM, VMEM, VMEM, ANY, VMEM], (VMEM, VMEM),
-                [half_type, dma((PARTS, 2))], tile_total * 2**22, "others", {6: 0},
+                others_kernel, (acc_type, x_type), [SMEM, SMEM, VMEM, VMEM, ANY, VMEM], (VMEM, VMEM),
+                [half_type, dma((PARTS, 2))], tile_total * 2**22, "others", {5: 0},
             )(*near_operands, source_factor, pinned(acc))
-        field, send, done = call(
-            far_kernel, (field_type, send_type, done_type),
-            [SMEM, SMEM, SMEM, VMEM, ANY, ANY, VMEM, VMEM], (VMEM, ANY, VMEM),
+        width = panels // PARTS
+        field, send, out, tail = call(
+            lambda *refs, step=step: far_kernel(step, *refs),
+            (field_type, send_type, out_type, pltpu.VMEM((excite, width), F32)),
+            [SMEM, SMEM, SMEM, VMEM, ANY, ANY, VMEM, VMEM, ANY], (VMEM, ANY, ANY, VMEM),
             [
                 pltpu.VMEM(gram_shape, BF16), picked_type, picked_type, half_type,
-                dma((PARTS, 2)), dma((slots,)), dma,
+                pltpu.VMEM((excite, panels - width), F32),
+                dma((PARTS, 2)), dma((slots,)), dma, dma((PARTS - 1,)),
             ],
-            far_flops, "far",
-        )(turned_src, far_count, dest, received, target_factor, streamed(gram), pinned(acc), pinned(x))
+            far_flops, "far", {8: 2},
+        )(
+            turned_src, far_count, dest, received, target_factor, streamed(gram), pinned(acc), pinned(x),
+            streamed(out),
+        )
 
 
 def solution(mesh):

time: 157 us -> 148 us (0.943)
  starting transfers between devices: 61.5 us -> 54 us
  waiting for transfers between devices: 20.2 us -> 24.9 us
  Pallas kernels: 72.9 us -> 68.3 us
    all_to_all x5, starting transfers between devices: 52.5 us -> 45.7 us  [shards(): lax.all_to_all(send, 'panels', split_axis=0, concat_axis=0, tiled=True)]
    pallas_call x10 -> x9, Pallas kernels: 42.8 us -> 37.9 us  [the longest x4 16.1 us: shards(): call(lambda *refs, step=step: far_kernel(step, *refs), (field_type, send_...]
    all_to_all x5, waiting for transfers between devices: 20.2 us -> 24.9 us  [shards(): lax.all_to_all(send, 'panels', split_axis=0, concat_axis=0, tiled=True)]
  transfers between devices with their start and end apart: 15 -> 15, of which waited for: 4 -> 5; matrix products, arithmetic and copies ran while one was open for 0% -> 0% of each run, Pallas kernels for 32% -> 30%
where the time goes in v1:
time: 148 us; the launch traced here: 149 us
  Pallas kernels  68.3 us (46%)
  starting transfers between devices  54 us (36%)
  waiting for transfers between devices  24.9 us (17%)
    all_to_all x5, starting transfers between devices, shards(): lax.all_to_all(send, 'panels', split_axis=0, concat_axis=0, tiled=True)  45.7 us
    all_to_all x5, waiting for transfers between devices, shards(): lax.all_to_all(send, 'panels', split_axis=0, concat_axis=0, tiled=True)  24.9 us
    pallas_call x4, Pallas kernels, shards(): call(lambda *refs, step=step: local_kernel(step, *refs), (acc_type, tiles...  19.4 us
    pallas_call x4, Pallas kernels, shards(): call(lambda *refs, step=step: far_kernel(step, *refs), (field_type, send_...  16.1 us
    pallas_call x1, Pallas kernels, shards(): call(setup_kernel, (acc_type, tiles_type, half_type, pltpu.HBM(gram_shape...  10.2 us
    pallas_call x3, Pallas kernels, shards(): call(others_kernel, (acc_type, x_type), [SMEM, SMEM, VMEM, VMEM, ANY, VME...  9.99 us
    ppermute x5, starting transfers between devices, shards(): mate = lax.ppermute(field, 'panels', inward)  6.4 us
    pallas_call x1, Pallas kernels, shards(): call(first_kernel, (send_type, field_type), [SMEM, ANY, ANY], (ANY, VMEM)...  4.2 us
  transfers between devices with their start and end apart: 15, of which 5 were waited for; matrix products, arithmetic and copies ran while one was open for 0% of the time, Pallas kernels for 30%

profile of v1, /device:TPU:1, one launch (start us, length us, event | category | flops | bytes accessed | tf_op | source)
XLA Modules:
  0.0 148.6 jit_solution(4271004352334361722)
XLA Ops:
  0.0 0.7 fusion.2
  1.0 4.2 %first.1 = (bf16[128,16,128]{2,1,0:T(8,128)(2,1)}, bf16[64,4096]{1,0:T(8,128)(2,1)S(1)}) custom-call(s32[16]{0:T(128)S(1)} %select_reduce_fusion.dest.refs_2_, bf16[64,4096]{1,0:T(8,128)(2,1)} %field_in.1, bf16[16,32,4096]{2,1,0:T(8,128)(2,1)} %factor.7), custom_call_target="tpu_custom_call" | custom-call | flops 268435456 | bytes 4194304 | tf_op jit(solution)/shard_map/first/pallas_call | solution.py:399
  5.2 1.5 %collective-permute-start = (bf16[64,4096]{1,0:T(8,128)(2,1)S(1)}, bf16[64,4096]{1,0:T(8,128)(2,1)S(1)}, u32[]{:S(2)}, u32[]{:S(2)}) collective-permute-start(bf16[64,4096]{1,0:T(8,128)(2,1)S(1)} %get-tuple-element.51.field), channel_id=1, source_target_pairs={{0,1},{1,0},{2,3},{3,2},{4,5},{5,4},{6,7},{7,6},{8,9},{9,8},{10,11... | collective-permute-start | bytes 1572872 | tf_op jit(solution)/shard_map/ppermute | solution.py:404
  6.7 1.7 %collective-permute-start.1 = (bf16[64,4096]{1,0:T(8,128)(2,1)S(1)}, bf16[64,4096]{1,0:T(8,128)(2,1)S(1)}, u32[]{:S(2)}, u32[]{:S(2)}) collective-permute-start(bf16[64,4096]{1,0:T(8,128)(2,1)S(1)} %get-tuple-element.51.field), channel_id=1, source_target_pairs={{0,127},{1,2},{2,1},{3,4},{4,3},{5,6},{6,5},{7,8},{8,7},{9,10},{10... | collective-permute-start | bytes 1572872 | tf_op jit(solution)/shard_map/ppermute | solution.py:403
  8.4 10.6 %all-to-all-start = ((bf16[128,16,128]{2,1,0:T(8,128)(2,1)}), bf16[128,16,128]{2,1,0:T(8,128)(2,1)S(1)}, u32[]{:S(2)}, u32[]{:S(2)}) async-start(bf16[128,16,128]{2,1,0:T(8,128)(2,1)} %get-tuple-element.50), calls=%async_computation | async-start | bytes 1048576 | tf_op jit(solution)/shard_map/all_to_all | solution.py:405
  19.0 10.2 %setup.1 = (f32[17,64,256]{2,1,0:T(8,128)S(1)}, bf16[88,256,256]{2,1,0:T(8,128)(2,1)S(1)}, bf16[2,16,16,4096]{3,2,1,0:T(8,128)(2,1)S(1)}, bf16[2,2,256,256]{3,2,...) custom-call(s32[5,16]{1,0:T(8,128)S(1)} %bitcast.8, s32[16]{0:T(128)S(1)} %copy-done.3, ...), custom_call_target="tpu_custom_call" | custom-call | flops 335544320 | bytes 4194304 | tf_op jit(solution)/shard_map/setup/pallas_call | solution.py:408
  29.3 2.8 %others.5 = (f32[17,64,256]{2,1,0:T(8,128)S(1)}, f32[256,128]{1,0:T(8,128)S(1)}) custom-call(s32[2,3,88]{2,1,0:T(4,128)S(1)} %get-tuple-element.53.lists.refs_0_, s32[2]{0:T(128)S(1)} %get-tuple-element.54.counts.refs_1_, bf16[88,256,256]{2,1,0:T(8,128)(2,1)S(1)} %get-tuple-element.55.tiles, ...), custom_call_target="tpu_custom_call", output_to_operand_aliasing={{0}: (5, {})} | custom-call | flops 335544320 | bytes 4194304 | tf_op jit(solution)/shard_map/others/pallas_call | solution.py:439
  32.8 4.0 %far.4 = (bf16[64,4096]{1,0:T(8,128)(2,1)S(1)}, bf16[128,16,128]{2,1,0:T(8,128)(2,1)}, f32[5,64,4096]{2,1,0:T(8,128)}, f32[64,1024]{1,0:T(8,128)S(1)}) custom-call(s32[16,128]{1,0:T(8,128)S(1)} %bitcast.3, s32[128]{0:T(128)S(1)} %copy-done.1, s32[16]{0:T(128)S(1)} %select_reduce_fusion.dest.refs_2_, ...), custom_call_target="tpu_custom_call", output_to_operand_aliasing={{2}: (8, {})} | custom-call | flops 268435456 | bytes 4194304 | tf_op jit(solution)/shard_map/far/pallas_call | solution.py:449
  36.9 1.2 collective-permute-start.2
  38.3 9.8 %all-to-all-start.1 = ((bf16[128,16,128]{2,1,0:T(8,128)(2,1)}), bf16[128,16,128]{2,1,0:T(8,128)(2,1)S(1)}, u32[]{:S(2)}, u32[]{:S(2)}) async-start(bf16[128,16,128]{2,1,0:T(8,128)(2,1)} %get-tuple-element.61), calls=%async_computation.1 | async-start | bytes 1048576 | tf_op jit(solution)/shard_map/all_to_all | solution.py:405
  48.1 4.9 %local.4 = (f32[17,64,256]{2,1,0:T(8,128)S(1)}, bf16[88,256,256]{2,1,0:T(8,128)(2,1)S(1)}, f32[5,64,4096]{2,1,0:T(8,128)}) custom-call(s32[2,3,88]{2,1,0:T(4,128)S(1)} %get-tuple-element.53.lists.refs_0_, s32[2]{0:T(128)S(1)} %get-tuple-element.54.counts.refs_1_, bf16[64,4096]{1,0:T(8,128)(2,1)S(1)} %get-tuple-element.62.refs_2_, ...), custom_call_target="tpu_custom_call", output_to_operand_aliasing={{2}: (6, {})} | custom-call | flops 335544320 | bytes 4194304 | tf_op jit(solution)/shard_map/local/pallas_call | solution.py:421
  52.9 3.3 %others.6 = (f32[17,64,256]{2,1,0:T(8,128)S(1)}, f32[256,128]{1,0:T(8,128)S(1)}) custom-call(s32[2,3,88]{2,1,0:T(4,128)S(1)} %get-tuple-element.53.lists.refs_0_, s32[2]{0:T(128)S(1)} %get-tuple-element.54.counts.refs_1_, bf16[88,256,256]{2,1,0:T(8,128)(2,1)S(1)} %get-tuple-element.65.tiles, ...), custom_call_target="tpu_custom_call", output_to_operand_aliasing={{0}: (5, {})} | custom-call | flops 335544320 | bytes 4194304 | tf_op jit(solution)/shard_map/others/pallas_call | solution.py:444
  56.3 5.6 %all-to-all-done.1.refs_3_ = bf16[128,16,128]{2,1,0:T(8,128)(2,1)S(1)} async-done(((bf16[128,16,128]{2,1,0:T(8,128)(2,1)}), bf16[128,16,128]{2,1,0:T(8,128)(2,1)S(1)}, u32[]{:S(2)}, u32[]{:S(2)}) %all-to-all-start.1) | async-done | bytes 524320 | tf_op jit(solution)/shard_map/all_to_all | solution.py:405
  61.9 4.0 %far.5 = (bf16[64,4096]{1,0:T(8,128)(2,1)S(1)}, bf16[128,16,128]{2,1,0:T(8,128)(2,1)}, f32[5,64,4096]{2,1,0:T(8,128)}, f32[64,1024]{1,0:T(8,128)S(1)}) custom-call(s32[16,128]{1,0:T(8,128)S(1)} %bitcast.4, s32[128]{0:T(128)S(1)} %copy-done.1, s32[16]{0:T(128)S(1)} %select_reduce_fusion.dest.refs_2_, ...), custom_call_target="tpu_custom_call", output_to_operand_aliasing={{2}: (8, {})} | custom-call | flops 268435456 | bytes 4194304 | tf_op jit(solution)/shard_map/far/pallas_call | solution.py:449
  65.9 1.2 collective-permute-start.4
  67.1 8.6 %all-to-all-start.2 = ((bf16[128,16,128]{2,1,0:T(8,128)(2,1)}), bf16[128,16,128]{2,1,0:T(8,128)(2,1)S(1)}, u32[]{:S(2)}, u32[]{:S(2)}) async-start(bf16[128,16,128]{2,1,0:T(8,128)(2,1)} %get-tuple-element.70), calls=%async_computation.2 | async-start | bytes 1048576 | tf_op jit(solution)/shard_map/all_to_all | solution.py:405
  75.8 4.9 %local.5 = (f32[17,64,256]{2,1,0:T(8,128)S(1)}, bf16[88,256,256]{2,1,0:T(8,128)(2,1)S(1)}, f32[5,64,4096]{2,1,0:T(8,128)}) custom-call(s32[2,3,88]{2,1,0:T(4,128)S(1)} %get-tuple-element.53.lists.refs_0_, s32[2]{0:T(128)S(1)} %get-tuple-element.54.counts.refs_1_, bf16[64,4096]{1,0:T(8,128)(2,1)S(1)} %get-tuple-element.71.refs_2_, ...), custom_call_target="tpu_custom_call", output_to_operand_aliasing={{2}: (6, {})} | custom-call | flops 335544320 | bytes 4194304 | tf_op jit(solution)/shard_map/local/pallas_call | solution.py:421
  80.6 3.3 %others.7 = (f32[17,64,256]{2,1,0:T(8,128)S(1)}, f32[256,128]{1,0:T(8,128)S(1)}) custom-call(s32[2,3,88]{2,1,0:T(4,128)S(1)} %get-tuple-element.53.lists.refs_0_, s32[2]{0:T(128)S(1)} %get-tuple-element.54.counts.refs_1_, bf16[88,256,256]{2,1,0:T(8,128)(2,1)S(1)} %get-tuple-element.74.tiles, ...), custom_call_target="tpu_custom_call", output_to_operand_aliasing={{0}: (5, {})} | custom-call | flops 335544320 | bytes 4194304 | tf_op jit(solution)/shard_map/others/pallas_call | solution.py:444
  84.0 5.6 %all-to-all-done.2.refs_3_ = bf16[128,16,128]{2,1,0:T(8,128)(2,1)S(1)} async-done(((bf16[128,16,128]{2,1,0:T(8,128)(2,1)}), bf16[128,16,128]{2,1,0:T(8,128)(2,1)S(1)}, u32[]{:S(2)}, u32[]{:S(2)}) %all-to-all-start.2) | async-done | bytes 524320 | tf_op jit(solution)/shard_map/all_to_all | solution.py:405
  89.6 4.0 %far.6 = (bf16[64,4096]{1,0:T(8,128)(2,1)S(1)}, bf16[128,16,128]{2,1,0:T(8,128)(2,1)}, f32[5,64,4096]{2,1,0:T(8,128)}, f32[64,1024]{1,0:T(8,128)S(1)}) custom-call(s32[16,128]{1,0:T(8,128)S(1)} %bitcast.5, s32[128]{0:T(128)S(1)} %copy-done.1, s32[16]{0:T(128)S(1)} %select_reduce_fusion.dest.refs_2_, ...), custom_call_target="tpu_custom_call", output_to_operand_aliasing={{2}: (8, {})} | custom-call | flops 268435456 | bytes 4194304 | tf_op jit(solution)/shard_map/far/pallas_call | solution.py:449
  93.6 1.2 collective-permute-start.6
  94.9 8.2 %all-to-all-start.3 = ((bf16[128,16,128]{2,1,0:T(8,128)(2,1)}), bf16[128,16,128]{2,1,0:T(8,128)(2,1)S(1)}, u32[]{:S(2)}, u32[]{:S(2)}) async-start(bf16[128,16,128]{2,1,0:T(8,128)(2,1)} %get-tuple-element.79), calls=%async_computation.3 | async-start | bytes 1048576 | tf_op jit(solution)/shard_map/all_to_all | solution.py:405
  103.1 4.9 %local.6 = (f32[17,64,256]{2,1,0:T(8,128)S(1)}, bf16[88,256,256]{2,1,0:T(8,128)(2,1)S(1)}, f32[5,64,4096]{2,1,0:T(8,128)}) custom-call(s32[2,3,88]{2,1,0:T(4,128)S(1)} %get-tuple-element.53.lists.refs_0_, s32[2]{0:T(128)S(1)} %get-tuple-element.54.counts.refs_1_, bf16[64,4096]{1,0:T(8,128)(2,1)S(1)} %get-tuple-element.80.refs_2_, ...), custom_call_target="tpu_custom_call", output_to_operand_aliasing={{2}: (6, {})} | custom-call | flops 335544320 | bytes 4194304 | tf_op jit(solution)/shard_map/local/pallas_call | solution.py:421
  108.0 3.3 %others.8 = (f32[17,64,256]{2,1,0:T(8,128)S(1)}, f32[256,128]{1,0:T(8,128)S(1)}) custom-call(s32[2,3,88]{2,1,0:T(4,128)S(1)} %get-tuple-element.53.lists.refs_0_, s32[2]{0:T(128)S(1)} %get-tuple-element.54.counts.refs_1_, bf16[88,256,256]{2,1,0:T(8,128)(2,1)S(1)} %get-tuple-element.83.tiles, ...), custom_call_target="tpu_custom_call", output_to_operand_aliasing={{0}: (5, {})} | custom-call | flops 335544320 | bytes 4194304 | tf_op jit(solution)/shard_map/others/pallas_call | solution.py:444
  111.3 5.6 %all-to-all-done.3.refs_3_ = bf16[128,16,128]{2,1,0:T(8,128)(2,1)S(1)} async-done(((bf16[128,16,128]{2,1,0:T(8,128)(2,1)}), bf16[128,16,128]{2,1,0:T(8,128)(2,1)S(1)}, u32[]{:S(2)}, u32[]{:S(2)}) %all-to-all-start.3) | async-done | bytes 524320 | tf_op jit(solution)/shard_map/all_to_all | solution.py:405
  116.9 4.0 %far.7 = (bf16[64,4096]{1,0:T(8,128)(2,1)S(1)}, bf16[128,16,128]{2,1,0:T(8,128)(2,1)}, f32[5,64,4096]{2,1,0:T(8,128)}, f32[64,1024]{1,0:T(8,128)S(1)}) custom-call(s32[16,128]{1,0:T(8,128)S(1)} %bitcast.6, s32[128]{0:T(128)S(1)} %copy-done.1, s32[16]{0:T(128)S(1)} %select_reduce_fusion.dest.refs_2_, ...), custom_call_target="tpu_custom_call", output_to_operand_aliasing={{2}: (8, {})} | custom-call | flops 268435456 | bytes 4194304 | tf_op jit(solution)/shard_map/far/pallas_call | solution.py:449
  120.9 1.2 collective-permute-start.8
  122.2 8.5 %all-to-all-start.4 = ((bf16[128,16,128]{2,1,0:T(8,128)(2,1)}), bf16[128,16,128]{2,1,0:T(8,128)(2,1)S(1)}, u32[]{:S(2)}, u32[]{:S(2)}) async-start(bf16[128,16,128]{2,1,0:T(8,128)(2,1)} %get-tuple-element.88), calls=%async_computation.4 | async-start | bytes 1048576 | tf_op jit(solution)/shard_map/all_to_all | solution.py:405
  130.7 4.9 %local.7 = (f32[17,64,256]{2,1,0:T(8,128)S(1)}, bf16[88,256,256]{2,1,0:T(8,128)(2,1)S(1)}, f32[5,64,4096]{2,1,0:T(8,128)}) custom-call(s32[2,3,88]{2,1,0:T(4,128)S(1)} %get-tuple-element.53.lists.refs_0_, s32[2]{0:T(128)S(1)} %get-tuple-element.54.counts.refs_1_, bf16[64,4096]{1,0:T(8,128)(2,1)S(1)} %get-tuple-element.89.refs_2_, ...), custom_call_target="tpu_custom_call", output_to_operand_aliasing={{2}: (6, {})} | custom-call | flops 335544320 | bytes 4194304 | tf_op jit(solution)/shard_map/local/pallas_call | solution.py:421
  135.6 1.5 %others.9.refs_4_ = f32[17,64,256]{2,1,0:T(8,128)S(1)} custom-call(s32[2,3,88]{2,1,0:T(4,128)S(1)} %get-tuple-element.53.lists.refs_0_, s32[2]{0:T(128)S(1)} %get-tuple-element.54.counts.refs_1_, bf16[88,256,256]{2,1,0:T(8,128)(2,1)S(1)} %get-tuple-element.92.tiles, ...), custom_call_target="tpu_custom_call", output_to_operand_aliasing={{}: (4, {})} | custom-call | flops 335544320 | bytes 4194304 | tf_op jit(solution)/shard_map/others/pallas_call | solution.py:428
  137.1 7.4 %all-to-all-done.4.refs_2_ = bf16[128,16,128]{2,1,0:T(8,128)(2,1)S(1)} async-done(((bf16[128,16,128]{2,1,0:T(8,128)(2,1)}), bf16[128,16,128]{2,1,0:T(8,128)(2,1)S(1)}, u32[]{:S(2)}, u32[]{:S(2)}) %all-to-all-start.4) | async-done | bytes 524320 | tf_op jit(solution)/shard_map/all_to_all | solution.py:405
  144.5 3.9 %last.1 = f32[5,64,4096]{2,1,0:T(8,128)} custom-call(s32[16,128]{1,0:T(8,128)S(1)} %bitcast.7, s32[128]{0:T(128)S(1)} %copy-done.1, bf16[128,16,128]{2,1,0:T(8,128)(2,1)S(1)} %all-to-all-done.4.refs_2_, bf16[16,32,4096]{2,1,0:T(8,128)(2,1)} %refs_3_.1, f32[17,64,256]{2,1,0:T(8,128)S(1)} %others.9.refs_4_, ...), custom_call_target="tpu_custom_call", output_to_operand_aliasing={{}: (5, {})} | custom-call | flops 268435456 | bytes 4194304 | tf_op jit(solution)/shard_map/last/pallas_call | solution.py:432
  (25 shorter events, 1.2 us)
Async XLA Ops:
  0.0 19.0 %copy-start.2 = (s32[16,5]{0,1:T(8,128)S(1)}, s32[16,5]{0,1:T(8,128)}, u32[]{:S(2)}) copy-start(s32[16,5]{0,1:T(8,128)} %param.10) | copy-start | bytes 964
  0.0 19.0 %copy-start.3 = (s32[16]{0:T(128)S(1)}, s32[16]{0:T(128)}, u32[]{:S(2)}) copy-start(s32[16]{0:T(128)} %count.1) | copy-start | bytes 196
  5.2 13.8 %collective-permute-start = (bf16[64,4096]{1,0:T(8,128)(2,1)S(1)}, bf16[64,4096]{1,0:T(8,128)(2,1)S(1)}, u32[]{:S(2)}, u32[]{:S(2)}) collective-permute-start(bf16[64,4096]{1,0:T(8,128)(2,1)S(1)} %get-tuple-element.51.field), channel_id=1, source_target_pairs={{0,1},{1,0},{2,3},{3,2},{4,5},{5,4},{6,7},{7,6},{8,9},{9,8},{10,11... | collective-permute-start | bytes 1572872 | tf_op jit(solution)/shard_map/ppermute | solution.py:404
  6.7 22.6 %collective-permute-start.1 = (bf16[64,4096]{1,0:T(8,128)(2,1)S(1)}, bf16[64,4096]{1,0:T(8,128)(2,1)S(1)}, u32[]{:S(2)}, u32[]{:S(2)}) collective-permute-start(bf16[64,4096]{1,0:T(8,128)(2,1)S(1)} %get-tuple-element.51.field), channel_id=1, source_target_pairs={{0,127},{1,2},{2,1},{3,4},{4,3},{5,6},{6,5},{7,8},{8,7},{9,10},{10... | collective-permute-start | bytes 1572872 | tf_op jit(solution)/shard_map/ppermute | solution.py:403
  8.4 24.4 %all-to-all-start = ((bf16[128,16,128]{2,1,0:T(8,128)(2,1)}), bf16[128,16,128]{2,1,0:T(8,128)(2,1)S(1)}, u32[]{:S(2)}, u32[]{:S(2)}) async-start(bf16[128,16,128]{2,1,0:T(8,128)(2,1)} %get-tuple-element.50), calls=%async_computation | async-start | bytes 1048576 | tf_op jit(solution)/shard_map/all_to_all | solution.py:405
  29.3 3.5 %copy-start = (s32[128,16]{0,1:T(8,128)S(1)}, s32[128,16]{0,1:T(8,128)}, u32[]{:S(2)}) copy-start(s32[128,16]{0,1:T(8,128)} %param.12) | copy-start | bytes 24580
  29.3 3.5 %copy-start.1 = (s32[128]{0:T(128)S(1)}, s32[128]{0:T(128)}, u32[]{:S(2)}) copy-start(s32[128]{0:T(128)} %refs_1_.9) | copy-start | bytes 1540
  36.9 11.2 %collective-permute-start.2 = (bf16[64,4096]{1,0:T(8,128)(2,1)S(1)}, bf16[64,4096]{1,0:T(8,128)(2,1)S(1)}, u32[]{:S(2)}, u32[]{:S(2)}) collective-permute-start(bf16[64,4096]{1,0:T(8,128)(2,1)S(1)} %get-tuple-element.62.refs_2_), channel_id=1, source_target_pairs={{0,1},{1,0},{2,3},{3,2},{4,5},{5,4},{6,7},{7,6},{8,9},{9,8},{10,11... | collective-permute-start | bytes 1572872 | tf_op jit(solution)/shard_map/ppermute | solution.py:404
  38.1 14.9 %collective-permute-start.3 = (bf16[64,4096]{1,0:T(8,128)(2,1)S(1)}, bf16[64,4096]{1,0:T(8,128)(2,1)S(1)}, u32[]{:S(2)}, u32[]{:S(2)}) collective-permute-start(bf16[64,4096]{1,0:T(8,128)(2,1)S(1)} %get-tuple-element.62.refs_2_), channel_id=1, source_target_pairs={{0,127},{1,2},{2,1},{3,4},{4,3},{5,6},{6,5},{7,8},{8,7},{9,10},{10... | collective-permute-start | bytes 1572872 | tf_op jit(solution)/shard_map/ppermute | solution.py:403
  38.3 23.6 %all-to-all-start.1 = ((bf16[128,16,128]{2,1,0:T(8,128)(2,1)}), bf16[128,16,128]{2,1,0:T(8,128)(2,1)S(1)}, u32[]{:S(2)}, u32[]{:S(2)}) async-start(bf16[128,16,128]{2,1,0:T(8,128)(2,1)} %get-tuple-element.61), calls=%async_computation.1 | async-start | bytes 1048576 | tf_op jit(solution)/shard_map/all_to_all | solution.py:405
  65.9 9.8 %collective-permute-start.4 = (bf16[64,4096]{1,0:T(8,128)(2,1)S(1)}, bf16[64,4096]{1,0:T(8,128)(2,1)S(1)}, u32[]{:S(2)}, u32[]{:S(2)}) collective-permute-start(bf16[64,4096]{1,0:T(8,128)(2,1)S(1)} %get-tuple-element.71.refs_2_), channel_id=1, source_target_pairs={{0,1},{1,0},{2,3},{3,2},{4,5},{5,4},{6,7},{7,6},{8,9},{9,8},{10,11... | collective-permute-start | bytes 1572872 | tf_op jit(solution)/shard_map/ppermute | solution.py:404
  67.1 13.5 %collective-permute-start.5 = (bf16[64,4096]{1,0:T(8,128)(2,1)S(1)}, bf16[64,4096]{1,0:T(8,128)(2,1)S(1)}, u32[]{:S(2)}, u32[]{:S(2)}) collective-permute-start(bf16[64,4096]{1,0:T(8,128)(2,1)S(1)} %get-tuple-element.71.refs_2_), channel_id=1, source_target_pairs={{0,127},{1,2},{2,1},{3,4},{4,3},{5,6},{6,5},{7,8},{8,7},{9,10},{10... | collective-permute-start | bytes 1572872 | tf_op jit(solution)/shard_map/ppermute | solution.py:403
  67.1 22.4 %all-to-all-start.2 = ((bf16[128,16,128]{2,1,0:T(8,128)(2,1)}), bf16[128,16,128]{2,1,0:T(8,128)(2,1)S(1)}, u32[]{:S(2)}, u32[]{:S(2)}) async-start(bf16[128,16,128]{2,1,0:T(8,128)(2,1)} %get-tuple-element.70), calls=%async_computation.2 | async-start | bytes 1048576 | tf_op jit(solution)/shard_map/all_to_all | solution.py:405
  93.6 9.5 %collective-permute-start.6 = (bf16[64,4096]{1,0:T(8,128)(2,1)S(1)}, bf16[64,4096]{1,0:T(8,128)(2,1)S(1)}, u32[]{:S(2)}, u32[]{:S(2)}) collective-permute-start(bf16[64,4096]{1,0:T(8,128)(2,1)S(1)} %get-tuple-element.80.refs_2_), channel_id=1, source_target_pairs={{0,1},{1,0},{2,3},{3,2},{4,5},{5,4},{6,7},{7,6},{8,9},{9,8},{10,11... | collective-permute-start | bytes 1572872 | tf_op jit(solution)/shard_map/ppermute | solution.py:404
  94.8 13.1 %collective-permute-start.7 = (bf16[64,4096]{1,0:T(8,128)(2,1)S(1)}, bf16[64,4096]{1,0:T(8,128)(2,1)S(1)}, u32[]{:S(2)}, u32[]{:S(2)}) collective-permute-start(bf16[64,4096]{1,0:T(8,128)(2,1)S(1)} %get-tuple-element.80.refs_2_), channel_id=1, source_target_pairs={{0,127},{1,2},{2,1},{3,4},{4,3},{5,6},{6,5},{7,8},{8,7},{9,10},{10... | collective-permute-start | bytes 1572872 | tf_op jit(solution)/shard_map/ppermute | solution.py:403
  94.9 22.0 %all-to-all-start.3 = ((bf16[128,16,128]{2,1,0:T(8,128)(2,1)}), bf16[128,16,128]{2,1,0:T(8,128)(2,1)S(1)}, u32[]{:S(2)}, u32[]{:S(2)}) async-start(bf16[128,16,128]{2,1,0:T(8,128)(2,1)} %get-tuple-element.79), calls=%async_computation.3 | async-start | bytes 1048576 | tf_op jit(solution)/shard_map/all_to_all | solution.py:405
  120.9 9.8 %collective-permute-start.8 = (bf16[64,4096]{1,0:T(8,128)(2,1)S(1)}, bf16[64,4096]{1,0:T(8,128)(2,1)S(1)}, u32[]{:S(2)}, u32[]{:S(2)}) collective-permute-start(bf16[64,4096]{1,0:T(8,128)(2,1)S(1)} %get-tuple-element.89.refs_2_), channel_id=1, source_target_pairs={{0,1},{1,0},{2,3},{3,2},{4,5},{5,4},{6,7},{7,6},{8,9},{9,8},{10,11... | collective-permute-start | bytes 1572872 | tf_op jit(solution)/shard_map/ppermute | solution.py:404
  122.2 13.4 %collective-permute-start.9 = (bf16[64,4096]{1,0:T(8,128)(2,1)S(1)}, bf16[64,4096]{1,0:T(8,128)(2,1)S(1)}, u32[]{:S(2)}, u32[]{:S(2)}) collective-permute-start(bf16[64,4096]{1,0:T(8,128)(2,1)S(1)} %get-tuple-element.89.refs_2_), channel_id=1, source_target_pairs={{0,127},{1,2},{2,1},{3,4},{4,3},{5,6},{6,5},{7,8},{8,7},{9,10},{10... | collective-permute-start | bytes 1572872 | tf_op jit(solution)/shard_map/ppermute | solution.py:403
  122.2 22.4 %all-to-all-start.4 = ((bf16[128,16,128]{2,1,0:T(8,128)(2,1)}), bf16[128,16,128]{2,1,0:T(8,128)(2,1)S(1)}, u32[]{:S(2)}, u32[]{:S(2)}) async-start(bf16[128,16,128]{2,1,0:T(8,128)(2,1)} %get-tuple-element.88), calls=%async_computation.4 | async-start | bytes 1048576 | tf_op jit(solution)/shard_map/all_to_all | solution.py:405

commit v2 on v1

--- a/solution.py
+++ b/solution.py
@@ -8,6 +8,7 @@
 ITERS = 5
 BATCH = 8
 PARTS = 4
+KEPT = 2
 F32 = jnp.float32
 BF16 = jnp.bfloat16
 NT = (((1,), (1,)), ((), ()))
@@ -161,8 +162,6 @@
     offset, count, field, mate, near, source_factor, target_factor,
     acc, others, source, gram, lists, counts, out, tiles, sems, osem, mate_here, msem, target, ssems, tsems,
 ):
-    start_halves(source_factor, source, ssems)
-    start_halves(target_factor, target, tsems)
     leaves = count.shape[0]
     slots = near.shape[0] // leaves
     odd = lax.axis_index("panels") % 2
@@ -196,22 +195,43 @@
         lax.fori_loop(filled[w], groups * BATCH, fill, 0)
         counts[w] = groups
 
-    def couple():
-        panels = source.shape[3]
-        for c in range(ssems.shape[0]):
-            wait_halves(source_factor, source, ssems, c)
-            wait_halves(target_factor, target, tsems, c)
-        for h in range(2):
-            for g in range(2):
-                gram[h, g] = nt(source[h].reshape(-1, panels), target[g].reshape(-1, panels)).astype(BF16)
-
-    own_part(lists, counts, field, mate, near, acc, others, tiles, sems, osem, mate_here, msem, couple)
-
-
-def local_kernel(step, lists, counts, field, mate, near, tail, _, acc, others, out, *scratch):
+    def start_factors():
+        start_halves(source_factor, source, ssems)
+        start_halves(target_factor, target, tsems)
+
+    own_part(lists, counts, field, mate, near, acc, others, tiles, sems, osem, mate_here, msem, start_factors)
+    panels = source.shape[3]
+    for c in range(ssems.shape[0]):
+        wait_halves(source_factor, source, ssems, c)
+        wait_halves(target_factor, target, tsems, c)
+    for h in range(2):
+        for g in range(2):
+            gram[h, g] = nt(source[h].reshape(-1, panels), target[g].reshape(-1, panels)).astype(BF16)
+
+
+def store_tail(step, tail, out, sem):
+    width = tail.shape[1]
+    return pltpu.make_async_copy(tail, out.at[step - 1, :, pl.ds(out.shape[2] - width, width)], sem)
+
+
+def local_kernel(
+    step, lists, counts, field, mate, near, factor, tail, _, acc, others, source, out,
+    tiles, sems, osem, both, bsems, sem, ssems,
+):
+    copy = store_tail(step, tail, out, sem)
+    copy.start()
+    own_part(
+        lists, counts, field, mate, near, acc, others, tiles, sems, osem, both, bsems,
+        lambda: start_halves(factor, source, ssems),
+    )
+    for c in range(ssems.shape[0]):
+        wait_halves(factor, source, ssems, c)
+    copy.wait()
+
+
+def last_local_kernel(step, lists, counts, field, mate, near, tail, _, acc, others, out, *scratch):
     *scratch, sem = scratch
-    width = tail.shape[1]
-    copy = pltpu.make_async_copy(tail, out.at[step - 1, :, pl.ds(out.shape[2] - width, width)], sem)
+    copy = store_tail(step, tail, out, sem)
     copy.start()
     own_part(lists, counts, field, mate, near, acc, others, *scratch)
     copy.wait()
@@ -221,24 +241,11 @@
     run_list(lists, counts[1], 1, 0, tiles, outer, acc)
 
 
-def first_others_kernel(lists, counts, tiles, outer, source, _, acc, x):
+def others_kernel(lists, counts, tiles, outer, source, _, acc, x):
     others_part(lists, counts, tiles, outer, acc)
     accs = None
     for i in range(acc.shape[0] - 1):
         accs = project(source, accs, i, acc[i].astype(BF16))
-    x[...] = jnp.concatenate(accs, axis=1)
-
-
-def others_kernel(lists, counts, tiles, outer, factor, _, acc, x, source, sems):
-    start_halves(factor, source, sems)
-    others_part(lists, counts, tiles, outer, acc)
-    parts = sems.shape[0]
-    per = (acc.shape[0] - 1) // parts
-    accs = None
-    for c in range(parts):
-        wait_halves(factor, source, sems, c)
-        for i in range(c * per, c * per + per):
-            accs = project(source, accs, i, acc[i].astype(BF16))
     x[...] = jnp.concatenate(accs, axis=1)
 
 
@@ -418,11 +425,19 @@
                 tile_total * 2**22, "setup",
             )(near_offset.T, near_count, field, mate, near, source_factor, target_factor)
         else:
-            acc, tiles, out = call(
-                lambda *refs, step=step: local_kernel(step, *refs), (acc_type, tiles_type, out_type),
-                [SMEM, SMEM, ANY, ANY, ANY, VMEM, ANY], (VMEM, VMEM, ANY), [*own_scratch, dma],
-                tile_total * 2**22, "local", {6: 2},
-            )(lists, counts, field, mate, near, pinned(tail), streamed(out))
+            last = step == ITERS - 1
+            acc, tiles, *source, out = call(
+                lambda *refs, step=step, last=last: (last_local_kernel if last else local_kernel)(step, *refs),
+                (acc_type, tiles_type, *([] if last else [half_type]), out_type),
+                [SMEM, SMEM, ANY, ANY, ANY, *([] if last else [ANY]), VMEM, ANY],
+                (VMEM, VMEM, *([] if last else [VMEM]), ANY),
+                [*own_scratch, dma, *([] if last else [dma((PARTS, 2))])],
+                tile_total * 2**22, "local", {6: 2} if last else {7: 3},
+            )(
+                lists, counts, field, mate, near, *([] if last else [source_factor]),
+                pinned(tail), streamed(out),
+            )
+            source = None if last else source[0]
         near_operands = (lists, counts, pinned(tiles), outer)
         if step == ITERS - 1:
             acc = call(
@@ -435,17 +450,11 @@
                 [picked_type, half_type, done_type, dma((PARTS, 2)), dma((PARTS,))],
                 far_flops, "last", {5: 0},
             )(turned_src, far_count, received, target_factor, pinned(acc), streamed(out))
-        if step == 0:
-            acc, x = call(
-                first_others_kernel, (acc_type, x_type), [SMEM, SMEM, VMEM, VMEM, VMEM, VMEM], (VMEM, VMEM),
-                [], tile_total * 2**22, "others", {5: 0},
-            )(*near_operands, pinned(source), pinned(acc))
-        else:
-            acc, x = call(
-                others_kernel, (acc_type, x_type), [SMEM, SMEM, VMEM, VMEM, ANY, VMEM], (VMEM, VMEM),
-                [half_type, dma((PARTS, 2))], tile_total * 2**22, "others", {5: 0},
-            )(*near_operands, source_factor, pinned(acc))
-        width = panels // PARTS
+        acc, x = call(
+            others_kernel, (acc_type, x_type), [SMEM, SMEM, VMEM, VMEM, VMEM, VMEM], (VMEM, VMEM),
+            [], tile_total * 2**22, "others", {5: 0},
+        )(*near_operands, pinned(source), pinned(acc))
+        width = panels // PARTS * KEPT
         field, send, out, tail = call(
             lambda *refs, step=step: far_kernel(step, *refs),
             (field_type, send_type, out_type, pltpu.VMEM((excite, width), F32)),
@@ -453,7 +462,7 @@
             [
                 pltpu.VMEM(gram_shape, BF16), picked_type, picked_type, half_type,
                 pltpu.VMEM((excite, panels - width), F32),
-                dma((PARTS, 2)), dma((slots,)), dma, dma((PARTS - 1,)),
+                dma((PARTS, 2)), dma((slots,)), dma, dma((PARTS - KEPT,)),
             ],
             far_flops, "far", {8: 2},
         )(

time: 148 us -> 148 us (level)
  local copies, waits for them, and re-layouts: 0.02 us -> 7.31 us
  Pallas kernels: 68.3 us -> 63.8 us
  waiting for transfers between devices: 24.9 us -> 20.5 us
    unnamed x8 -> x24, local copies, waits for them, and re-layouts: 0.02 us -> 7.31 us
    all_to_all x5, waiting for transfers between devices: 24.9 us -> 20.5 us  [shards(): lax.all_to_all(send, 'panels', split_axis=0, concat_axis=0, tiled=True)]
    pallas_call x8, Pallas kernels: 32.2 us -> 29.2 us  [the longest x4 19.8 us: shards(): call(lambda *refs, step=step, last=last: (last_local_kernel if last else...]
  transfers between devices with their start and end apart: 15 -> 15, of which waited for: 5 -> 5; matrix products, arithmetic and copies ran while one was open for 0% -> 0% of each run, Pallas kernels for 30% -> 28%
where the time goes in v2:
time: 148 us
  Pallas kernels  63.8 us (43%)
  starting transfers between devices  54.9 us (37%)
  waiting for transfers between devices  20.5 us (14%)
  local copies, waits for them, and re-layouts  7.31 us (5%)
    all_to_all x5, starting transfers between devices, shards(): lax.all_to_all(send, 'panels', split_axis=0, concat_axis=0, tiled=True)  45.9 us
    all_to_all x5, waiting for transfers between devices, shards(): lax.all_to_all(send, 'panels', split_axis=0, concat_axis=0, tiled=True)  20.5 us
    pallas_call x4, Pallas kernels, shards(): call(lambda *refs, step=step, last=last: (last_local_kernel if last else...  19.8 us
    pallas_call x4, Pallas kernels, shards(): call(lambda *refs, step=step: far_kernel(step, *refs), (field_type, send_...  14.9 us
    pallas_call x1, Pallas kernels, shards(): call(setup_kernel, (acc_type, tiles_type, half_type, pltpu.HBM(gram_shape...  10.5 us
    pallas_call x4, Pallas kernels, shards(): call(others_kernel, (acc_type, x_type), [SMEM, SMEM, VMEM, VMEM, VMEM, VM...  9.43 us
    unnamed x24, local copies, waits for them, and re-layouts  7.31 us
    ppermute x5, starting transfers between devices, shards(): mate = lax.ppermute(field, 'panels', inward)  6.5 us
  transfers between devices with their start and end apart: 15, of which 5 were waited for; matrix products, arithmetic and copies ran while one was open for 0% of the time, Pallas kernels for 28%

profile of v2, /device:TPU:1, one launch (start us, length us, event | category | flops | bytes accessed | tf_op | source)
XLA Modules:
  0.0 147.9 jit_solution(5370795380514220028)
XLA Ops:
  1.0 4.2 %first.1 = (bf16[128,16,128]{2,1,0:T(8,128)(2,1)}, bf16[64,4096]{1,0:T(8,128)(2,1)S(1)}) custom-call(s32[16]{0:T(128)S(1)} %select_reduce_fusion.dest.refs_2_, bf16[64,4096]{1,0:T(8,128)(2,1)} %field_in.1, bf16[16,32,4096]{2,1,0:T(8,128)(2,1)} %refs_5_.5), custom_call_target="tpu_custom_call" | custom-call | flops 268435456 | bytes 4194304 | tf_op jit(solution)/shard_map/first/pallas_call | solution.py:406
  5.2 1.5 %collective-permute-start = (bf16[64,4096]{1,0:T(8,128)(2,1)S(1)}, bf16[64,4096]{1,0:T(8,128)(2,1)S(1)}, u32[]{:S(2)}, u32[]{:S(2)}) collective-permute-start(bf16[64,4096]{1,0:T(8,128)(2,1)S(1)} %get-tuple-element.54.field), channel_id=1, source_target_pairs={{0,1},{1,0},{2,3},{3,2},{4,5},{5,4},{6,7},{7,6},{8,9},{9,8},{10,11... | collective-permute-start | bytes 1572872 | tf_op jit(solution)/shard_map/ppermute | solution.py:411
  6.7 1.7 %collective-permute-start.1 = (bf16[64,4096]{1,0:T(8,128)(2,1)S(1)}, bf16[64,4096]{1,0:T(8,128)(2,1)S(1)}, u32[]{:S(2)}, u32[]{:S(2)}) collective-permute-start(bf16[64,4096]{1,0:T(8,128)(2,1)S(1)} %get-tuple-element.54.field), channel_id=1, source_target_pairs={{0,127},{1,2},{2,1},{3,4},{4,3},{5,6},{6,5},{7,8},{8,7},{9,10},{10... | collective-permute-start | bytes 1572872 | tf_op jit(solution)/shard_map/ppermute | solution.py:410
  8.4 10.6 %all-to-all-start = ((bf16[128,16,128]{2,1,0:T(8,128)(2,1)}), bf16[128,16,128]{2,1,0:T(8,128)(2,1)S(1)}, u32[]{:S(2)}, u32[]{:S(2)}) async-start(bf16[128,16,128]{2,1,0:T(8,128)(2,1)} %get-tuple-element.53), calls=%async_computation | async-start | bytes 1048576 | tf_op jit(solution)/shard_map/all_to_all | solution.py:412
  19.0 10.5 %setup.1 = (f32[17,64,256]{2,1,0:T(8,128)S(1)}, bf16[88,256,256]{2,1,0:T(8,128)(2,1)S(1)}, bf16[2,16,16,4096]{3,2,1,0:T(8,128)(2,1)S(1)}, bf16[2,2,256,256]{3,2,...) custom-call(s32[5,16]{1,0:T(8,128)S(1)} %bitcast.8, s32[16]{0:T(128)S(1)} %copy-done.11, ...), custom_call_target="tpu_custom_call" | custom-call | flops 335544320 | bytes 4194304 | tf_op jit(solution)/shard_map/setup/pallas_call | solution.py:415
  29.5 2.4 %others.5 = (f32[17,64,256]{2,1,0:T(8,128)S(1)}, f32[256,128]{1,0:T(8,128)S(1)}) custom-call(s32[2,3,88]{2,1,0:T(4,128)S(1)} %get-tuple-element.56.lists.refs_0_, s32[2]{0:T(128)S(1)} %get-tuple-element.57.counts.refs_1_, bf16[88,256,256]{2,1,0:T(8,128)(2,1)S(1)} %get-tuple-element.58.tiles, ...), custom_call_target="tpu_custom_call", output_to_operand_aliasing={{0}: (5, {})} | custom-call | flops 335544320 | bytes 4194304 | tf_op jit(solution)/shard_map/others/pallas_call | solution.py:453
  32.8 3.7 %far.4 = (bf16[64,4096]{1,0:T(8,128)(2,1)S(1)}, bf16[128,16,128]{2,1,0:T(8,128)(2,1)}, f32[5,64,4096]{2,1,0:T(8,128)}, f32[64,2048]{1,0:T(8,128)S(1)}) custom-call(s32[16,128]{1,0:T(8,128)S(1)} %bitcast.3, s32[128]{0:T(128)S(1)} %copy-done.9, s32[16]{0:T(128)S(1)} %select_reduce_fusion.dest.refs_2_, ...), custom_call_target="tpu_custom_call", output_to_operand_aliasing={{2}: (8, {})} | custom-call | flops 268435456 | bytes 4194304 | tf_op jit(solution)/shard_map/far/pallas_call | solution.py:458
  36.6 1.3 collective-permute-start.2
  38.7 10.9 %all-to-all-start.1 = ((bf16[128,16,128]{2,1,0:T(8,128)(2,1)}), bf16[128,16,128]{2,1,0:T(8,128)(2,1)S(1)}, u32[]{:S(2)}, u32[]{:S(2)}) async-start(bf16[128,16,128]{2,1,0:T(8,128)(2,1)} %get-tuple-element.64), calls=%async_computation.1 | async-start | bytes 1048576 | tf_op jit(solution)/shard_map/all_to_all | solution.py:412
  50.4 1.0 copy-done.1
  51.4 5.1 %local.4 = (f32[17,64,256]{2,1,0:T(8,128)S(1)}, bf16[88,256,256]{2,1,0:T(8,128)(2,1)S(1)}, bf16[2,16,16,4096]{3,2,1,0:T(8,128)(2,1)S(1)}, f32[5,64,4096]{2,1,0:T(8,128)}) custom-call(s32[2,3,88]{2,1,0:T(4,128)S(1)} %get-tuple-element.56.lists.refs_0_, s32[2]{0:T(128)S(1)} %get-tuple-element.57.counts.refs_1_, ...), custom_call_target="tpu_custom_call", output_to_operand_aliasing={{3}: (7, {})} | custom-call | flops 335544320 | bytes 4194304 | tf_op jit(solution)/shard_map/local/pallas_call | solution.py:429
  56.5 2.4 %others.6 = (f32[17,64,256]{2,1,0:T(8,128)S(1)}, f32[256,128]{1,0:T(8,128)S(1)}) custom-call(s32[2,3,88]{2,1,0:T(4,128)S(1)} %get-tuple-element.56.lists.refs_0_, s32[2]{0:T(128)S(1)} %get-tuple-element.57.counts.refs_1_, bf16[88,256,256]{2,1,0:T(8,128)(2,1)S(1)} %get-tuple-element.68.tiles, ...), custom_call_target="tpu_custom_call", output_to_operand_aliasing={{0}: (5, {})} | custom-call | flops 335544320 | bytes 4194304 | tf_op jit(solution)/shard_map/others/pallas_call | solution.py:453
  58.9 4.5 %all-to-all-done.1.refs_3_ = bf16[128,16,128]{2,1,0:T(8,128)(2,1)S(1)} async-done(((bf16[128,16,128]{2,1,0:T(8,128)(2,1)}), bf16[128,16,128]{2,1,0:T(8,128)(2,1)S(1)}, u32[]{:S(2)}, u32[]{:S(2)}) %all-to-all-start.1) | async-done | bytes 524320 | tf_op jit(solution)/shard_map/all_to_all | solution.py:412
  63.4 3.7 %far.5 = (bf16[64,4096]{1,0:T(8,128)(2,1)S(1)}, bf16[128,16,128]{2,1,0:T(8,128)(2,1)}, f32[5,64,4096]{2,1,0:T(8,128)}, f32[64,2048]{1,0:T(8,128)S(1)}) custom-call(s32[16,128]{1,0:T(8,128)S(1)} %bitcast.4, s32[128]{0:T(128)S(1)} %copy-done.9, s32[16]{0:T(128)S(1)} %select_reduce_fusion.dest.refs_2_, ...), custom_call_target="tpu_custom_call", output_to_operand_aliasing={{2}: (8, {})} | custom-call | flops 268435456 | bytes 4194304 | tf_op jit(solution)/shard_map/far/pallas_call | solution.py:458
  67.1 1.2 collective-permute-start.4
  68.4 8.1 %all-to-all-start.2 = ((bf16[128,16,128]{2,1,0:T(8,128)(2,1)}), bf16[128,16,128]{2,1,0:T(8,128)(2,1)S(1)}, u32[]{:S(2)}, u32[]{:S(2)}) async-start(bf16[128,16,128]{2,1,0:T(8,128)(2,1)} %get-tuple-element.74), calls=%async_computation.2 | async-start | bytes 1048576 | tf_op jit(solution)/shard_map/all_to_all | solution.py:412
  78.3 5.1 %local.5 = (f32[17,64,256]{2,1,0:T(8,128)S(1)}, bf16[88,256,256]{2,1,0:T(8,128)(2,1)S(1)}, bf16[2,16,16,4096]{3,2,1,0:T(8,128)(2,1)S(1)}, f32[5,64,4096]{2,1,0:T(8,128)}) custom-call(s32[2,3,88]{2,1,0:T(4,128)S(1)} %get-tuple-element.56.lists.refs_0_, s32[2]{0:T(128)S(1)} %get-tuple-element.57.counts.refs_1_, ...), custom_call_target="tpu_custom_call", output_to_operand_aliasing={{3}: (7, {})} | custom-call | flops 335544320 | bytes 4194304 | tf_op jit(solution)/shard_map/local/pallas_call | solution.py:429
  83.5 2.4 %others.7 = (f32[17,64,256]{2,1,0:T(8,128)S(1)}, f32[256,128]{1,0:T(8,128)S(1)}) custom-call(s32[2,3,88]{2,1,0:T(4,128)S(1)} %get-tuple-element.56.lists.refs_0_, s32[2]{0:T(128)S(1)} %get-tuple-element.57.counts.refs_1_, bf16[88,256,256]{2,1,0:T(8,128)(2,1)S(1)} %get-tuple-element.78.tiles, ...), custom_call_target="tpu_custom_call", output_to_operand_aliasing={{0}: (5, {})} | custom-call | flops 335544320 | bytes 4194304 | tf_op jit(solution)/shard_map/others/pallas_call | solution.py:453
  85.8 4.5 %all-to-all-done.2.refs_3_ = bf16[128,16,128]{2,1,0:T(8,128)(2,1)S(1)} async-done(((bf16[128,16,128]{2,1,0:T(8,128)(2,1)}), bf16[128,16,128]{2,1,0:T(8,128)(2,1)S(1)}, u32[]{:S(2)}, u32[]{:S(2)}) %all-to-all-start.2) | async-done | bytes 524320 | tf_op jit(solution)/shard_map/all_to_all | solution.py:412
  90.3 3.7 %far.6 = (bf16[64,4096]{1,0:T(8,128)(2,1)S(1)}, bf16[128,16,128]{2,1,0:T(8,128)(2,1)}, f32[5,64,4096]{2,1,0:T(8,128)}, f32[64,2048]{1,0:T(8,128)S(1)}) custom-call(s32[16,128]{1,0:T(8,128)S(1)} %bitcast.5, s32[128]{0:T(128)S(1)} %copy-done.9, s32[16]{0:T(128)S(1)} %select_reduce_fusion.dest.refs_2_, ...), custom_call_target="tpu_custom_call", output_to_operand_aliasing={{2}: (8, {})} | custom-call | flops 268435456 | bytes 4194304 | tf_op jit(solution)/shard_map/far/pallas_call | solution.py:458
  94.0 1.2 collective-permute-start.6
  95.2 8.1 %all-to-all-start.3 = ((bf16[128,16,128]{2,1,0:T(8,128)(2,1)}), bf16[128,16,128]{2,1,0:T(8,128)(2,1)S(1)}, u32[]{:S(2)}, u32[]{:S(2)}) async-start(bf16[128,16,128]{2,1,0:T(8,128)(2,1)} %get-tuple-element.84), calls=%async_computation.3 | async-start | bytes 1048576 | tf_op jit(solution)/shard_map/all_to_all | solution.py:412
  105.2 5.1 %local.6 = (f32[17,64,256]{2,1,0:T(8,128)S(1)}, bf16[88,256,256]{2,1,0:T(8,128)(2,1)S(1)}, bf16[2,16,16,4096]{3,2,1,0:T(8,128)(2,1)S(1)}, f32[5,64,4096]{2,1,0:T(8,128)}) custom-call(s32[2,3,88]{2,1,0:T(4,128)S(1)} %get-tuple-element.56.lists.refs_0_, s32[2]{0:T(128)S(1)} %get-tuple-element.57.counts.refs_1_, ...), custom_call_target="tpu_custom_call", output_to_operand_aliasing={{3}: (7, {})} | custom-call | flops 335544320 | bytes 4194304 | tf_op jit(solution)/shard_map/local/pallas_call | solution.py:429
  110.3 2.4 %others.8 = (f32[17,64,256]{2,1,0:T(8,128)S(1)}, f32[256,128]{1,0:T(8,128)S(1)}) custom-call(s32[2,3,88]{2,1,0:T(4,128)S(1)} %get-tuple-element.56.lists.refs_0_, s32[2]{0:T(128)S(1)} %get-tuple-element.57.counts.refs_1_, bf16[88,256,256]{2,1,0:T(8,128)(2,1)S(1)} %get-tuple-element.88.tiles, ...), custom_call_target="tpu_custom_call", output_to_operand_aliasing={{0}: (5, {})} | custom-call | flops 335544320 | bytes 4194304 | tf_op jit(solution)/shard_map/others/pallas_call | solution.py:453
  112.7 4.4 %all-to-all-done.3.refs_3_ = bf16[128,16,128]{2,1,0:T(8,128)(2,1)S(1)} async-done(((bf16[128,16,128]{2,1,0:T(8,128)(2,1)}), bf16[128,16,128]{2,1,0:T(8,128)(2,1)S(1)}, u32[]{:S(2)}, u32[]{:S(2)}) %all-to-all-start.3) | async-done | bytes 524320 | tf_op jit(solution)/shard_map/all_to_all | solution.py:412
  117.1 3.7 %far.7 = (bf16[64,4096]{1,0:T(8,128)(2,1)S(1)}, bf16[128,16,128]{2,1,0:T(8,128)(2,1)}, f32[5,64,4096]{2,1,0:T(8,128)}, f32[64,2048]{1,0:T(8,128)S(1)}) custom-call(s32[16,128]{1,0:T(8,128)S(1)} %bitcast.6, s32[128]{0:T(128)S(1)} %copy-done.9, s32[16]{0:T(128)S(1)} %select_reduce_fusion.dest.refs_2_, ...), custom_call_target="tpu_custom_call", output_to_operand_aliasing={{2}: (8, {})} | custom-call | flops 268435456 | bytes 4194304 | tf_op jit(solution)/shard_map/far/pallas_call | solution.py:458
  120.8 1.2 collective-permute-start.8
  122.0 8.1 %all-to-all-start.4 = ((bf16[128,16,128]{2,1,0:T(8,128)(2,1)}), bf16[128,16,128]{2,1,0:T(8,128)(2,1)S(1)}, u32[]{:S(2)}, u32[]{:S(2)}) async-start(bf16[128,16,128]{2,1,0:T(8,128)(2,1)} %get-tuple-element.94), calls=%async_computation.4 | async-start | bytes 1048576 | tf_op jit(solution)/shard_map/all_to_all | solution.py:412
  132.0 4.5 %local.7 = (f32[17,64,256]{2,1,0:T(8,128)S(1)}, bf16[88,256,256]{2,1,0:T(8,128)(2,1)S(1)}, f32[5,64,4096]{2,1,0:T(8,128)}) custom-call(s32[2,3,88]{2,1,0:T(4,128)S(1)} %get-tuple-element.56.lists.refs_0_, s32[2]{0:T(128)S(1)} %get-tuple-element.57.counts.refs_1_, bf16[64,4096]{1,0:T(8,128)(2,1)S(1)} %get-tuple-element.95.refs_2_, ...), custom_call_target="tpu_custom_call", output_to_operand_aliasing={{2}: (6, {})} | custom-call | flops 335544320 | bytes 4194304 | tf_op jit(solution)/shard_map/local/pallas_call | solution.py:429
  136.5 1.1 others.9.refs_4_
  137.6 6.3 %all-to-all-done.4.refs_2_ = bf16[128,16,128]{2,1,0:T(8,128)(2,1)S(1)} async-done(((bf16[128,16,128]{2,1,0:T(8,128)(2,1)}), bf16[128,16,128]{2,1,0:T(8,128)(2,1)S(1)}, u32[]{:S(2)}, u32[]{:S(2)}) %all-to-all-start.4) | async-done | bytes 524320 | tf_op jit(solution)/shard_map/all_to_all | solution.py:412
  143.8 3.9 %last.1 = f32[5,64,4096]{2,1,0:T(8,128)} custom-call(s32[16,128]{1,0:T(8,128)S(1)} %bitcast.7, s32[128]{0:T(128)S(1)} %copy-done.9, bf16[128,16,128]{2,1,0:T(8,128)(2,1)S(1)} %all-to-all-done.4.refs_2_, bf16[16,32,4096]{2,1,0:T(8,128)(2,1)} %refs_3_.1, f32[17,64,256]{2,1,0:T(8,128)S(1)} %others.9.refs_4_, ...), custom_call_target="tpu_custom_call", output_to_operand_aliasing={{}: (5, {})} | custom-call | flops 268435456 | bytes 4194304 | tf_op jit(solution)/shard_map/last/pallas_call | solution.py:447
  (41 shorter events, 9.0 us)
Async XLA Ops:
  0.0 19.0 %copy-start.10 = (s32[16,5]{0,1:T(8,128)S(1)}, s32[16,5]{0,1:T(8,128)}, u32[]{:S(2)}) copy-start(s32[16,5]{0,1:T(8,128)} %param.10) | copy-start | bytes 964
  0.0 19.0 %copy-start.11 = (s32[16]{0:T(128)S(1)}, s32[16]{0:T(128)}, u32[]{:S(2)}) copy-start(s32[16]{0:T(128)} %count.1) | copy-start | bytes 196
  5.2 13.8 %collective-permute-start = (bf16[64,4096]{1,0:T(8,128)(2,1)S(1)}, bf16[64,4096]{1,0:T(8,128)(2,1)S(1)}, u32[]{:S(2)}, u32[]{:S(2)}) collective-permute-start(bf16[64,4096]{1,0:T(8,128)(2,1)S(1)} %get-tuple-element.54.field), channel_id=1, source_target_pairs={{0,1},{1,0},{2,3},{3,2},{4,5},{5,4},{6,7},{7,6},{8,9},{9,8},{10,11... | collective-permute-start | bytes 1572872 | tf_op jit(solution)/shard_map/ppermute | solution.py:411
  6.7 22.8 %collective-permute-start.1 = (bf16[64,4096]{1,0:T(8,128)(2,1)S(1)}, bf16[64,4096]{1,0:T(8,128)(2,1)S(1)}, u32[]{:S(2)}, u32[]{:S(2)}) collective-permute-start(bf16[64,4096]{1,0:T(8,128)(2,1)S(1)} %get-tuple-element.54.field), channel_id=1, source_target_pairs={{0,127},{1,2},{2,1},{3,4},{4,3},{5,6},{6,5},{7,8},{8,7},{9,10},{10... | collective-permute-start | bytes 1572872 | tf_op jit(solution)/shard_map/ppermute | solution.py:410
  8.4 24.4 %all-to-all-start = ((bf16[128,16,128]{2,1,0:T(8,128)(2,1)}), bf16[128,16,128]{2,1,0:T(8,128)(2,1)S(1)}, u32[]{:S(2)}, u32[]{:S(2)}) async-start(bf16[128,16,128]{2,1,0:T(8,128)(2,1)} %get-tuple-element.53), calls=%async_computation | async-start | bytes 1048576 | tf_op jit(solution)/shard_map/all_to_all | solution.py:412
  29.5 3.3 %copy-start.8 = (s32[128,16]{0,1:T(8,128)S(1)}, s32[128,16]{0,1:T(8,128)}, u32[]{:S(2)}) copy-start(s32[128,16]{0,1:T(8,128)} %param.12) | copy-start | bytes 24580
  29.5 3.3 %copy-start.9 = (s32[128]{0:T(128)S(1)}, s32[128]{0:T(128)}, u32[]{:S(2)}) copy-start(s32[128]{0:T(128)} %refs_1_.9) | copy-start | bytes 1540
  36.6 13.0 %collective-permute-start.2 = (bf16[64,4096]{1,0:T(8,128)(2,1)S(1)}, bf16[64,4096]{1,0:T(8,128)(2,1)S(1)}, u32[]{:S(2)}, u32[]{:S(2)}) collective-permute-start(bf16[64,4096]{1,0:T(8,128)(2,1)S(1)} %get-tuple-element.65.refs_2_), channel_id=1, source_target_pairs={{0,1},{1,0},{2,3},{3,2},{4,5},{5,4},{6,7},{7,6},{8,9},{9,8},{10,11... | collective-permute-start | bytes 1572872 | tf_op jit(solution)/shard_map/ppermute | solution.py:411
  37.9 18.7 %collective-permute-start.3 = (bf16[64,4096]{1,0:T(8,128)(2,1)S(1)}, bf16[64,4096]{1,0:T(8,128)(2,1)S(1)}, u32[]{:S(2)}, u32[]{:S(2)}) collective-permute-start(bf16[64,4096]{1,0:T(8,128)(2,1)S(1)} %get-tuple-element.65.refs_2_), channel_id=1, source_target_pairs={{0,127},{1,2},{2,1},{3,4},{4,3},{5,6},{6,5},{7,8},{8,7},{9,10},{10... | collective-permute-start | bytes 1572872 | tf_op jit(solution)/shard_map/ppermute | solution.py:410
  38.7 24.8 %all-to-all-start.1 = ((bf16[128,16,128]{2,1,0:T(8,128)(2,1)}), bf16[128,16,128]{2,1,0:T(8,128)(2,1)S(1)}, u32[]{:S(2)}, u32[]{:S(2)}) async-start(bf16[128,16,128]{2,1,0:T(8,128)(2,1)} %get-tuple-element.64), calls=%async_computation.1 | async-start | bytes 1048576 | tf_op jit(solution)/shard_map/all_to_all | solution.py:412
  49.6 0.8 copy-start
  50.4 1.0 copy-start.1
  67.1 9.4 %collective-permute-start.4 = (bf16[64,4096]{1,0:T(8,128)(2,1)S(1)}, bf16[64,4096]{1,0:T(8,128)(2,1)S(1)}, u32[]{:S(2)}, u32[]{:S(2)}) collective-permute-start(bf16[64,4096]{1,0:T(8,128)(2,1)S(1)} %get-tuple-element.75.refs_2_), channel_id=1, source_target_pairs={{0,1},{1,0},{2,3},{3,2},{4,5},{5,4},{6,7},{7,6},{8,9},{9,8},{10,11... | collective-permute-start | bytes 1572872 | tf_op jit(solution)/shard_map/ppermute | solution.py:411
  68.4 15.1 %collective-permute-start.5 = (bf16[64,4096]{1,0:T(8,128)(2,1)S(1)}, bf16[64,4096]{1,0:T(8,128)(2,1)S(1)}, u32[]{:S(2)}, u32[]{:S(2)}) collective-permute-start(bf16[64,4096]{1,0:T(8,128)(2,1)S(1)} %get-tuple-element.75.refs_2_), channel_id=1, source_target_pairs={{0,127},{1,2},{2,1},{3,4},{4,3},{5,6},{6,5},{7,8},{8,7},{9,10},{10... | collective-permute-start | bytes 1572872 | tf_op jit(solution)/shard_map/ppermute | solution.py:410
  68.4 21.9 %all-to-all-start.2 = ((bf16[128,16,128]{2,1,0:T(8,128)(2,1)}), bf16[128,16,128]{2,1,0:T(8,128)(2,1)S(1)}, u32[]{:S(2)}, u32[]{:S(2)}) async-start(bf16[128,16,128]{2,1,0:T(8,128)(2,1)} %get-tuple-element.74), calls=%async_computation.2 | async-start | bytes 1048576 | tf_op jit(solution)/shard_map/all_to_all | solution.py:412
  76.5 0.8 copy-start.2
  77.3 1.0 copy-start.3
  94.0 9.4 %collective-permute-start.6 = (bf16[64,4096]{1,0:T(8,128)(2,1)S(1)}, bf16[64,4096]{1,0:T(8,128)(2,1)S(1)}, u32[]{:S(2)}, u32[]{:S(2)}) collective-permute-start(bf16[64,4096]{1,0:T(8,128)(2,1)S(1)} %get-tuple-element.85.refs_2_), channel_id=1, source_target_pairs={{0,1},{1,0},{2,3},{3,2},{4,5},{5,4},{6,7},{7,6},{8,9},{9,8},{10,11... | collective-permute-start | bytes 1572872 | tf_op jit(solution)/shard_map/ppermute | solution.py:411
  95.2 15.1 %collective-permute-start.7 = (bf16[64,4096]{1,0:T(8,128)(2,1)S(1)}, bf16[64,4096]{1,0:T(8,128)(2,1)S(1)}, u32[]{:S(2)}, u32[]{:S(2)}) collective-permute-start(bf16[64,4096]{1,0:T(8,128)(2,1)S(1)} %get-tuple-element.85.refs_2_), channel_id=1, source_target_pairs={{0,127},{1,2},{2,1},{3,4},{4,3},{5,6},{6,5},{7,8},{8,7},{9,10},{10... | collective-permute-start | bytes 1572872 | tf_op jit(solution)/shard_map/ppermute | solution.py:410
  95.2 21.8 %all-to-all-start.3 = ((bf16[128,16,128]{2,1,0:T(8,128)(2,1)}), bf16[128,16,128]{2,1,0:T(8,128)(2,1)S(1)}, u32[]{:S(2)}, u32[]{:S(2)}) async-start(bf16[128,16,128]{2,1,0:T(8,128)(2,1)} %get-tuple-element.84), calls=%async_computation.3 | async-start | bytes 1048576 | tf_op jit(solution)/shard_map/all_to_all | solution.py:412
  103.4 0.8 copy-start.4
  104.2 1.0 copy-start.5
  120.8 9.4 %collective-permute-start.8 = (bf16[64,4096]{1,0:T(8,128)(2,1)S(1)}, bf16[64,4096]{1,0:T(8,128)(2,1)S(1)}, u32[]{:S(2)}, u32[]{:S(2)}) collective-permute-start(bf16[64,4096]{1,0:T(8,128)(2,1)S(1)} %get-tuple-element.95.refs_2_), channel_id=1, source_target_pairs={{0,1},{1,0},{2,3},{3,2},{4,5},{5,4},{6,7},{7,6},{8,9},{9,8},{10,11... | collective-permute-start | bytes 1572872 | tf_op jit(solution)/shard_map/ppermute | solution.py:411
  122.0 14.5 %collective-permute-start.9 = (bf16[64,4096]{1,0:T(8,128)(2,1)S(1)}, bf16[64,4096]{1,0:T(8,128)(2,1)S(1)}, u32[]{:S(2)}, u32[]{:S(2)}) collective-permute-start(bf16[64,4096]{1,0:T(8,128)(2,1)S(1)} %get-tuple-element.95.refs_2_), channel_id=1, source_target_pairs={{0,127},{1,2},{2,1},{3,4},{4,3},{5,6},{6,5},{7,8},{8,7},{9,10},{10... | collective-permute-start | bytes 1572872 | tf_op jit(solution)/shard_map/ppermute | solution.py:410
  122.0 21.8 %all-to-all-start.4 = ((bf16[128,16,128]{2,1,0:T(8,128)(2,1)}), bf16[128,16,128]{2,1,0:T(8,128)(2,1)S(1)}, u32[]{:S(2)}, u32[]{:S(2)}) async-start(bf16[128,16,128]{2,1,0:T(8,128)(2,1)} %get-tuple-element.94), calls=%async_computation.4 | async-start | bytes 1048576 | tf_op jit(solution)/shard_map/all_to_all | solution.py:412
  130.2 0.8 copy-start.6
  131.0 1.0 copy-start.7

commit v3 on v2

--- a/solution.py
+++ b/solution.py
@@ -162,6 +162,8 @@
     offset, count, field, mate, near, source_factor, target_factor,
     acc, others, source, gram, lists, counts, out, tiles, sems, osem, mate_here, msem, target, ssems, tsems,
 ):
+    start_halves(source_factor, source, ssems)
+    start_halves(target_factor, target, tsems)
     leaves = count.shape[0]
     slots = near.shape[0] // leaves
     odd = lax.axis_index("panels") % 2
@@ -195,18 +197,16 @@
         lax.fori_loop(filled[w], groups * BATCH, fill, 0)
         counts[w] = groups
 
-    def start_factors():
-        start_halves(source_factor, source, ssems)
-        start_halves(target_factor, target, tsems)
-
-    own_part(lists, counts, field, mate, near, acc, others, tiles, sems, osem, mate_here, msem, start_factors)
-    panels = source.shape[3]
-    for c in range(ssems.shape[0]):
-        wait_halves(source_factor, source, ssems, c)
-        wait_halves(target_factor, target, tsems, c)
-    for h in range(2):
-        for g in range(2):
-            gram[h, g] = nt(source[h].reshape(-1, panels), target[g].reshape(-1, panels)).astype(BF16)
+    def couple():
+        panels = source.shape[3]
+        for c in range(ssems.shape[0]):
+            wait_halves(source_factor, source, ssems, c)
+            wait_halves(target_factor, target, tsems, c)
+        for h in range(2):
+            for g in range(2):
+                gram[h, g] = nt(source[h].reshape(-1, panels), target[g].reshape(-1, panels)).astype(BF16)
+
+    own_part(lists, counts, field, mate, near, acc, others, tiles, sems, osem, mate_here, msem, couple)
 
 
 def store_tail(step, tail, out, sem):

time: 148 us -> 146 us (0.986)
  starting transfers between devices: 54.9 us -> 52.5 us
  waiting for transfers between devices: 20.5 us -> 18.8 us
  Pallas kernels: 63.8 us -> 65.3 us
    pallas_call x4, Pallas kernels: 19.8 us -> 21.6 us  [shards(): call(lambda *refs, step=step, last=last: (last_local_kernel if last else...]
    all_to_all x5, waiting for transfers between devices: 20.5 us -> 18.7 us  [shards(): lax.all_to_all(send, 'panels', split_axis=0, concat_axis=0, tiled=True)]
    all_to_all x5, starting transfers between devices: 45.9 us -> 44.4 us  [shards(): lax.all_to_all(send, 'panels', split_axis=0, concat_axis=0, tiled=True)]
  transfers between devices with their start and end apart: 15 -> 15, of which waited for: 5 -> 5; matrix products, arithmetic and copies ran while one was open for 0% -> 0% of each run, Pallas kernels for 28% -> 29%
where the time goes in v3:
time: 146 us; the launch traced here: 145 us
  Pallas kernels  65.3 us (45%)
  starting transfers between devices  52.5 us (36%)
  waiting for transfers between devices  18.8 us (13%)
  local copies, waits for them, and re-layouts  7.31 us (5%)
    all_to_all x5, starting transfers between devices, shards(): lax.all_to_all(send, 'panels', split_axis=0, concat_axis=0, tiled=True)  44.4 us
    pallas_call x4, Pallas kernels, shards(): call(lambda *refs, step=step, last=last: (last_local_kernel if last else...  21.6 us
    all_to_all x5, waiting for transfers between devices, shards(): lax.all_to_all(send, 'panels', split_axis=0, concat_axis=0, tiled=True)  18.7 us
    pallas_call x4, Pallas kernels, shards(): call(lambda *refs, step=step: far_kernel(step, *refs), (field_type, send_...  14.9 us
    pallas_call x1, Pallas kernels, shards(): call(setup_kernel, (acc_type, tiles_type, half_type, pltpu.HBM(gram_shape...  10.2 us
    pallas_call x4, Pallas kernels, shards(): call(others_kernel, (acc_type, x_type), [SMEM, SMEM, VMEM, VMEM, VMEM, VM...  9.42 us
    unnamed x24, local copies, waits for them, and re-layouts  7.31 us
    ppermute x5, starting transfers between devices, shards(): mate = lax.ppermute(field, 'panels', inward)  6.4 us
  transfers between devices with their start and end apart: 15, of which 5 were waited for; matrix products, arithmetic and copies ran while one was open for 0% of the time, Pallas kernels for 29%

profile of v3, /device:TPU:1, one launch (start us, length us, event | category | flops | bytes accessed | tf_op | source)
XLA Modules:
  0.0 145.3 jit_solution(876805873676279864)
XLA Ops:
  1.0 4.2 %first.1 = (bf16[128,16,128]{2,1,0:T(8,128)(2,1)}, bf16[64,4096]{1,0:T(8,128)(2,1)S(1)}) custom-call(s32[16]{0:T(128)S(1)} %select_reduce_fusion.dest.refs_2_, bf16[64,4096]{1,0:T(8,128)(2,1)} %field_in.1, bf16[16,32,4096]{2,1,0:T(8,128)(2,1)} %refs_5_.5), custom_call_target="tpu_custom_call" | custom-call | flops 268435456 | bytes 4194304 | tf_op jit(solution)/shard_map/first/pallas_call | solution.py:406
  5.2 1.5 %collective-permute-start = (bf16[64,4096]{1,0:T(8,128)(2,1)S(1)}, bf16[64,4096]{1,0:T(8,128)(2,1)S(1)}, u32[]{:S(2)}, u32[]{:S(2)}) collective-permute-start(bf16[64,4096]{1,0:T(8,128)(2,1)S(1)} %get-tuple-element.54.field), channel_id=1, source_target_pairs={{0,1},{1,0},{2,3},{3,2},{4,5},{5,4},{6,7},{7,6},{8,9},{9,8},{10,11... | collective-permute-start | bytes 1572872 | tf_op jit(solution)/shard_map/ppermute | solution.py:411
  6.7 1.7 %collective-permute-start.1 = (bf16[64,4096]{1,0:T(8,128)(2,1)S(1)}, bf16[64,4096]{1,0:T(8,128)(2,1)S(1)}, u32[]{:S(2)}, u32[]{:S(2)}) collective-permute-start(bf16[64,4096]{1,0:T(8,128)(2,1)S(1)} %get-tuple-element.54.field), channel_id=1, source_target_pairs={{0,127},{1,2},{2,1},{3,4},{4,3},{5,6},{6,5},{7,8},{8,7},{9,10},{10... | collective-permute-start | bytes 1572872 | tf_op jit(solution)/shard_map/ppermute | solution.py:410
  8.4 10.6 %all-to-all-start = ((bf16[128,16,128]{2,1,0:T(8,128)(2,1)}), bf16[128,16,128]{2,1,0:T(8,128)(2,1)S(1)}, u32[]{:S(2)}, u32[]{:S(2)}) async-start(bf16[128,16,128]{2,1,0:T(8,128)(2,1)} %get-tuple-element.53), calls=%async_computation | async-start | bytes 1048576 | tf_op jit(solution)/shard_map/all_to_all | solution.py:412
  19.0 10.2 %setup.1 = (f32[17,64,256]{2,1,0:T(8,128)S(1)}, bf16[88,256,256]{2,1,0:T(8,128)(2,1)S(1)}, bf16[2,16,16,4096]{3,2,1,0:T(8,128)(2,1)S(1)}, bf16[2,2,256,256]{3,2,...) custom-call(s32[5,16]{1,0:T(8,128)S(1)} %bitcast.8, s32[16]{0:T(128)S(1)} %copy-done.11, ...), custom_call_target="tpu_custom_call" | custom-call | flops 335544320 | bytes 4194304 | tf_op jit(solution)/shard_map/setup/pallas_call | solution.py:415
  29.3 2.4 %others.5 = (f32[17,64,256]{2,1,0:T(8,128)S(1)}, f32[256,128]{1,0:T(8,128)S(1)}) custom-call(s32[2,3,88]{2,1,0:T(4,128)S(1)} %get-tuple-element.56.lists.refs_0_, s32[2]{0:T(128)S(1)} %get-tuple-element.57.counts.refs_1_, bf16[88,256,256]{2,1,0:T(8,128)(2,1)S(1)} %get-tuple-element.58.tiles, ...), custom_call_target="tpu_custom_call", output_to_operand_aliasing={{0}: (5, {})} | custom-call | flops 335544320 | bytes 4194304 | tf_op jit(solution)/shard_map/others/pallas_call | solution.py:453
  31.6 1.2 all-to-all-done.refs_3_
  32.8 3.7 %far.4 = (bf16[64,4096]{1,0:T(8,128)(2,1)S(1)}, bf16[128,16,128]{2,1,0:T(8,128)(2,1)}, f32[5,64,4096]{2,1,0:T(8,128)}, f32[64,2048]{1,0:T(8,128)S(1)}) custom-call(s32[16,128]{1,0:T(8,128)S(1)} %bitcast.3, s32[128]{0:T(128)S(1)} %copy-done.9, s32[16]{0:T(128)S(1)} %select_reduce_fusion.dest.refs_2_, ...), custom_call_target="tpu_custom_call", output_to_operand_aliasing={{2}: (8, {})} | custom-call | flops 268435456 | bytes 4194304 | tf_op jit(solution)/shard_map/far/pallas_call | solution.py:458
  36.5 1.2 collective-permute-start.2
  37.8 9.4 %all-to-all-start.1 = ((bf16[128,16,128]{2,1,0:T(8,128)(2,1)}), bf16[128,16,128]{2,1,0:T(8,128)(2,1)S(1)}, u32[]{:S(2)}, u32[]{:S(2)}) async-start(bf16[128,16,128]{2,1,0:T(8,128)(2,1)} %get-tuple-element.64), calls=%async_computation.1 | async-start | bytes 1048576 | tf_op jit(solution)/shard_map/all_to_all | solution.py:412
  49.0 5.5 %local.4 = (f32[17,64,256]{2,1,0:T(8,128)S(1)}, bf16[88,256,256]{2,1,0:T(8,128)(2,1)S(1)}, bf16[2,16,16,4096]{3,2,1,0:T(8,128)(2,1)S(1)}, f32[5,64,4096]{2,1,0:T(8,128)}) custom-call(s32[2,3,88]{2,1,0:T(4,128)S(1)} %get-tuple-element.56.lists.refs_0_, s32[2]{0:T(128)S(1)} %get-tuple-element.57.counts.refs_1_, ...), custom_call_target="tpu_custom_call", output_to_operand_aliasing={{3}: (7, {})} | custom-call | flops 335544320 | bytes 4194304 | tf_op jit(solution)/shard_map/local/pallas_call | solution.py:429
  54.6 2.4 %others.6 = (f32[17,64,256]{2,1,0:T(8,128)S(1)}, f32[256,128]{1,0:T(8,128)S(1)}) custom-call(s32[2,3,88]{2,1,0:T(4,128)S(1)} %get-tuple-element.56.lists.refs_0_, s32[2]{0:T(128)S(1)} %get-tuple-element.57.counts.refs_1_, bf16[88,256,256]{2,1,0:T(8,128)(2,1)S(1)} %get-tuple-element.68.tiles, ...), custom_call_target="tpu_custom_call", output_to_operand_aliasing={{0}: (5, {})} | custom-call | flops 335544320 | bytes 4194304 | tf_op jit(solution)/shard_map/others/pallas_call | solution.py:453
  56.9 3.9 %all-to-all-done.1.refs_3_ = bf16[128,16,128]{2,1,0:T(8,128)(2,1)S(1)} async-done(((bf16[128,16,128]{2,1,0:T(8,128)(2,1)}), bf16[128,16,128]{2,1,0:T(8,128)(2,1)S(1)}, u32[]{:S(2)}, u32[]{:S(2)}) %all-to-all-start.1) | async-done | bytes 524320 | tf_op jit(solution)/shard_map/all_to_all | solution.py:412
  60.9 3.7 %far.5 = (bf16[64,4096]{1,0:T(8,128)(2,1)S(1)}, bf16[128,16,128]{2,1,0:T(8,128)(2,1)}, f32[5,64,4096]{2,1,0:T(8,128)}, f32[64,2048]{1,0:T(8,128)S(1)}) custom-call(s32[16,128]{1,0:T(8,128)S(1)} %bitcast.4, s32[128]{0:T(128)S(1)} %copy-done.9, s32[16]{0:T(128)S(1)} %select_reduce_fusion.dest.refs_2_, ...), custom_call_target="tpu_custom_call", output_to_operand_aliasing={{2}: (8, {})} | custom-call | flops 268435456 | bytes 4194304 | tf_op jit(solution)/shard_map/far/pallas_call | solution.py:458
  64.6 1.2 collective-permute-start.4
  65.8 8.1 %all-to-all-start.2 = ((bf16[128,16,128]{2,1,0:T(8,128)(2,1)}), bf16[128,16,128]{2,1,0:T(8,128)(2,1)S(1)}, u32[]{:S(2)}, u32[]{:S(2)}) async-start(bf16[128,16,128]{2,1,0:T(8,128)(2,1)} %get-tuple-element.74), calls=%async_computation.2 | async-start | bytes 1048576 | tf_op jit(solution)/shard_map/all_to_all | solution.py:412
  75.8 5.5 %local.5 = (f32[17,64,256]{2,1,0:T(8,128)S(1)}, bf16[88,256,256]{2,1,0:T(8,128)(2,1)S(1)}, bf16[2,16,16,4096]{3,2,1,0:T(8,128)(2,1)S(1)}, f32[5,64,4096]{2,1,0:T(8,128)}) custom-call(s32[2,3,88]{2,1,0:T(4,128)S(1)} %get-tuple-element.56.lists.refs_0_, s32[2]{0:T(128)S(1)} %get-tuple-element.57.counts.refs_1_, ...), custom_call_target="tpu_custom_call", output_to_operand_aliasing={{3}: (7, {})} | custom-call | flops 335544320 | bytes 4194304 | tf_op jit(solution)/shard_map/local/pallas_call | solution.py:429
  81.4 2.4 %others.7 = (f32[17,64,256]{2,1,0:T(8,128)S(1)}, f32[256,128]{1,0:T(8,128)S(1)}) custom-call(s32[2,3,88]{2,1,0:T(4,128)S(1)} %get-tuple-element.56.lists.refs_0_, s32[2]{0:T(128)S(1)} %get-tuple-element.57.counts.refs_1_, bf16[88,256,256]{2,1,0:T(8,128)(2,1)S(1)} %get-tuple-element.78.tiles, ...), custom_call_target="tpu_custom_call", output_to_operand_aliasing={{0}: (5, {})} | custom-call | flops 335544320 | bytes 4194304 | tf_op jit(solution)/shard_map/others/pallas_call | solution.py:453
  83.8 3.9 %all-to-all-done.2.refs_3_ = bf16[128,16,128]{2,1,0:T(8,128)(2,1)S(1)} async-done(((bf16[128,16,128]{2,1,0:T(8,128)(2,1)}), bf16[128,16,128]{2,1,0:T(8,128)(2,1)S(1)}, u32[]{:S(2)}, u32[]{:S(2)}) %all-to-all-start.2) | async-done | bytes 524320 | tf_op jit(solution)/shard_map/all_to_all | solution.py:412
  87.7 3.7 %far.6 = (bf16[64,4096]{1,0:T(8,128)(2,1)S(1)}, bf16[128,16,128]{2,1,0:T(8,128)(2,1)}, f32[5,64,4096]{2,1,0:T(8,128)}, f32[64,2048]{1,0:T(8,128)S(1)}) custom-call(s32[16,128]{1,0:T(8,128)S(1)} %bitcast.5, s32[128]{0:T(128)S(1)} %copy-done.9, s32[16]{0:T(128)S(1)} %select_reduce_fusion.dest.refs_2_, ...), custom_call_target="tpu_custom_call", output_to_operand_aliasing={{2}: (8, {})} | custom-call | flops 268435456 | bytes 4194304 | tf_op jit(solution)/shard_map/far/pallas_call | solution.py:458
  91.4 1.2 collective-permute-start.6
  92.6 8.1 %all-to-all-start.3 = ((bf16[128,16,128]{2,1,0:T(8,128)(2,1)}), bf16[128,16,128]{2,1,0:T(8,128)(2,1)S(1)}, u32[]{:S(2)}, u32[]{:S(2)}) async-start(bf16[128,16,128]{2,1,0:T(8,128)(2,1)} %get-tuple-element.84), calls=%async_computation.3 | async-start | bytes 1048576 | tf_op jit(solution)/shard_map/all_to_all | solution.py:412
  102.6 5.5 %local.6 = (f32[17,64,256]{2,1,0:T(8,128)S(1)}, bf16[88,256,256]{2,1,0:T(8,128)(2,1)S(1)}, bf16[2,16,16,4096]{3,2,1,0:T(8,128)(2,1)S(1)}, f32[5,64,4096]{2,1,0:T(8,128)}) custom-call(s32[2,3,88]{2,1,0:T(4,128)S(1)} %get-tuple-element.56.lists.refs_0_, s32[2]{0:T(128)S(1)} %get-tuple-element.57.counts.refs_1_, ...), custom_call_target="tpu_custom_call", output_to_operand_aliasing={{3}: (7, {})} | custom-call | flops 335544320 | bytes 4194304 | tf_op jit(solution)/shard_map/local/pallas_call | solution.py:429
  108.2 2.4 %others.8 = (f32[17,64,256]{2,1,0:T(8,128)S(1)}, f32[256,128]{1,0:T(8,128)S(1)}) custom-call(s32[2,3,88]{2,1,0:T(4,128)S(1)} %get-tuple-element.56.lists.refs_0_, s32[2]{0:T(128)S(1)} %get-tuple-element.57.counts.refs_1_, bf16[88,256,256]{2,1,0:T(8,128)(2,1)S(1)} %get-tuple-element.88.tiles, ...), custom_call_target="tpu_custom_call", output_to_operand_aliasing={{0}: (5, {})} | custom-call | flops 335544320 | bytes 4194304 | tf_op jit(solution)/shard_map/others/pallas_call | solution.py:453
  110.5 3.9 %all-to-all-done.3.refs_3_ = bf16[128,16,128]{2,1,0:T(8,128)(2,1)S(1)} async-done(((bf16[128,16,128]{2,1,0:T(8,128)(2,1)}), bf16[128,16,128]{2,1,0:T(8,128)(2,1)S(1)}, u32[]{:S(2)}, u32[]{:S(2)}) %all-to-all-start.3) | async-done | bytes 524320 | tf_op jit(solution)/shard_map/all_to_all | solution.py:412
  114.4 3.7 %far.7 = (bf16[64,4096]{1,0:T(8,128)(2,1)S(1)}, bf16[128,16,128]{2,1,0:T(8,128)(2,1)}, f32[5,64,4096]{2,1,0:T(8,128)}, f32[64,2048]{1,0:T(8,128)S(1)}) custom-call(s32[16,128]{1,0:T(8,128)S(1)} %bitcast.6, s32[128]{0:T(128)S(1)} %copy-done.9, s32[16]{0:T(128)S(1)} %select_reduce_fusion.dest.refs_2_, ...), custom_call_target="tpu_custom_call", output_to_operand_aliasing={{2}: (8, {})} | custom-call | flops 268435456 | bytes 4194304 | tf_op jit(solution)/shard_map/far/pallas_call | solution.py:458
  118.2 1.2 collective-permute-start.8
  119.4 8.1 %all-to-all-start.4 = ((bf16[128,16,128]{2,1,0:T(8,128)(2,1)}), bf16[128,16,128]{2,1,0:T(8,128)(2,1)S(1)}, u32[]{:S(2)}, u32[]{:S(2)}) async-start(bf16[128,16,128]{2,1,0:T(8,128)(2,1)} %get-tuple-element.94), calls=%async_computation.4 | async-start | bytes 1048576 | tf_op jit(solution)/shard_map/all_to_all | solution.py:412
  129.4 4.9 %local.7 = (f32[17,64,256]{2,1,0:T(8,128)S(1)}, bf16[88,256,256]{2,1,0:T(8,128)(2,1)S(1)}, f32[5,64,4096]{2,1,0:T(8,128)}) custom-call(s32[2,3,88]{2,1,0:T(4,128)S(1)} %get-tuple-element.56.lists.refs_0_, s32[2]{0:T(128)S(1)} %get-tuple-element.57.counts.refs_1_, bf16[64,4096]{1,0:T(8,128)(2,1)S(1)} %get-tuple-element.95.refs_2_, ...), custom_call_target="tpu_custom_call", output_to_operand_aliasing={{2}: (6, {})} | custom-call | flops 335544320 | bytes 4194304 | tf_op jit(solution)/shard_map/local/pallas_call | solution.py:429
  134.3 1.1 others.9.refs_4_
  135.4 5.8 %all-to-all-done.4.refs_2_ = bf16[128,16,128]{2,1,0:T(8,128)(2,1)S(1)} async-done(((bf16[128,16,128]{2,1,0:T(8,128)(2,1)}), bf16[128,16,128]{2,1,0:T(8,128)(2,1)S(1)}, u32[]{:S(2)}, u32[]{:S(2)}) %all-to-all-start.4) | async-done | bytes 524320 | tf_op jit(solution)/shard_map/all_to_all | solution.py:412
  141.2 3.9 %last.1 = f32[5,64,4096]{2,1,0:T(8,128)} custom-call(s32[16,128]{1,0:T(8,128)S(1)} %bitcast.7, s32[128]{0:T(128)S(1)} %copy-done.9, bf16[128,16,128]{2,1,0:T(8,128)(2,1)S(1)} %all-to-all-done.4.refs_2_, bf16[16,32,4096]{2,1,0:T(8,128)(2,1)} %refs_3_.1, f32[17,64,256]{2,1,0:T(8,128)S(1)} %others.9.refs_4_, ...), custom_call_target="tpu_custom_call", output_to_operand_aliasing={{}: (5, {})} | custom-call | flops 268435456 | bytes 4194304 | tf_op jit(solution)/shard_map/last/pallas_call | solution.py:447
  (41 shorter events, 8.3 us)
Async XLA Ops:
  0.0 19.0 %copy-start.10 = (s32[16,5]{0,1:T(8,128)S(1)}, s32[16,5]{0,1:T(8,128)}, u32[]{:S(2)}) copy-start(s32[16,5]{0,1:T(8,128)} %param.10) | copy-start | bytes 964
  0.0 19.0 %copy-start.11 = (s32[16]{0:T(128)S(1)}, s32[16]{0:T(128)}, u32[]{:S(2)}) copy-start(s32[16]{0:T(128)} %count.1) | copy-start | bytes 196
  5.2 13.8 %collective-permute-start = (bf16[64,4096]{1,0:T(8,128)(2,1)S(1)}, bf16[64,4096]{1,0:T(8,128)(2,1)S(1)}, u32[]{:S(2)}, u32[]{:S(2)}) collective-permute-start(bf16[64,4096]{1,0:T(8,128)(2,1)S(1)} %get-tuple-element.54.field), channel_id=1, source_target_pairs={{0,1},{1,0},{2,3},{3,2},{4,5},{5,4},{6,7},{7,6},{8,9},{9,8},{10,11... | collective-permute-start | bytes 1572872 | tf_op jit(solution)/shard_map/ppermute | solution.py:411
  6.7 22.6 %collective-permute-start.1 = (bf16[64,4096]{1,0:T(8,128)(2,1)S(1)}, bf16[64,4096]{1,0:T(8,128)(2,1)S(1)}, u32[]{:S(2)}, u32[]{:S(2)}) collective-permute-start(bf16[64,4096]{1,0:T(8,128)(2,1)S(1)} %get-tuple-element.54.field), channel_id=1, source_target_pairs={{0,127},{1,2},{2,1},{3,4},{4,3},{5,6},{6,5},{7,8},{8,7},{9,10},{10... | collective-permute-start | bytes 1572872 | tf_op jit(solution)/shard_map/ppermute | solution.py:410
  8.4 24.4 %all-to-all-start = ((bf16[128,16,128]{2,1,0:T(8,128)(2,1)}), bf16[128,16,128]{2,1,0:T(8,128)(2,1)S(1)}, u32[]{:S(2)}, u32[]{:S(2)}) async-start(bf16[128,16,128]{2,1,0:T(8,128)(2,1)} %get-tuple-element.53), calls=%async_computation | async-start | bytes 1048576 | tf_op jit(solution)/shard_map/all_to_all | solution.py:412
  29.3 3.5 %copy-start.8 = (s32[128,16]{0,1:T(8,128)S(1)}, s32[128,16]{0,1:T(8,128)}, u32[]{:S(2)}) copy-start(s32[128,16]{0,1:T(8,128)} %param.12) | copy-start | bytes 24580
  29.3 3.5 %copy-start.9 = (s32[128]{0:T(128)S(1)}, s32[128]{0:T(128)}, u32[]{:S(2)}) copy-start(s32[128]{0:T(128)} %refs_1_.9) | copy-start | bytes 1540
  36.5 10.6 %collective-permute-start.2 = (bf16[64,4096]{1,0:T(8,128)(2,1)S(1)}, bf16[64,4096]{1,0:T(8,128)(2,1)S(1)}, u32[]{:S(2)}, u32[]{:S(2)}) collective-permute-start(bf16[64,4096]{1,0:T(8,128)(2,1)S(1)} %get-tuple-element.65.refs_2_), channel_id=1, source_target_pairs={{0,1},{1,0},{2,3},{3,2},{4,5},{5,4},{6,7},{7,6},{8,9},{9,8},{10,11... | collective-permute-start | bytes 1572872 | tf_op jit(solution)/shard_map/ppermute | solution.py:411
  37.8 16.8 %collective-permute-start.3 = (bf16[64,4096]{1,0:T(8,128)(2,1)S(1)}, bf16[64,4096]{1,0:T(8,128)(2,1)S(1)}, u32[]{:S(2)}, u32[]{:S(2)}) collective-permute-start(bf16[64,4096]{1,0:T(8,128)(2,1)S(1)} %get-tuple-element.65.refs_2_), channel_id=1, source_target_pairs={{0,127},{1,2},{2,1},{3,4},{4,3},{5,6},{6,5},{7,8},{8,7},{9,10},{10... | collective-permute-start | bytes 1572872 | tf_op jit(solution)/shard_map/ppermute | solution.py:410
  37.8 23.1 %all-to-all-start.1 = ((bf16[128,16,128]{2,1,0:T(8,128)(2,1)}), bf16[128,16,128]{2,1,0:T(8,128)(2,1)S(1)}, u32[]{:S(2)}, u32[]{:S(2)}) async-start(bf16[128,16,128]{2,1,0:T(8,128)(2,1)} %get-tuple-element.64), calls=%async_computation.1 | async-start | bytes 1048576 | tf_op jit(solution)/shard_map/all_to_all | solution.py:412
  47.2 0.8 copy-start
  48.0 1.0 copy-start.1
  64.6 9.4 %collective-permute-start.4 = (bf16[64,4096]{1,0:T(8,128)(2,1)S(1)}, bf16[64,4096]{1,0:T(8,128)(2,1)S(1)}, u32[]{:S(2)}, u32[]{:S(2)}) collective-permute-start(bf16[64,4096]{1,0:T(8,128)(2,1)S(1)} %get-tuple-element.75.refs_2_), channel_id=1, source_target_pairs={{0,1},{1,0},{2,3},{3,2},{4,5},{5,4},{6,7},{7,6},{8,9},{9,8},{10,11... | collective-permute-start | bytes 1572872 | tf_op jit(solution)/shard_map/ppermute | solution.py:411
  65.8 15.5 %collective-permute-start.5 = (bf16[64,4096]{1,0:T(8,128)(2,1)S(1)}, bf16[64,4096]{1,0:T(8,128)(2,1)S(1)}, u32[]{:S(2)}, u32[]{:S(2)}) collective-permute-start(bf16[64,4096]{1,0:T(8,128)(2,1)S(1)} %get-tuple-element.75.refs_2_), channel_id=1, source_target_pairs={{0,127},{1,2},{2,1},{3,4},{4,3},{5,6},{6,5},{7,8},{8,7},{9,10},{10... | collective-permute-start | bytes 1572872 | tf_op jit(solution)/shard_map/ppermute | solution.py:410
  65.8 21.8 %all-to-all-start.2 = ((bf16[128,16,128]{2,1,0:T(8,128)(2,1)}), bf16[128,16,128]{2,1,0:T(8,128)(2,1)S(1)}, u32[]{:S(2)}, u32[]{:S(2)}) async-start(bf16[128,16,128]{2,1,0:T(8,128)(2,1)} %get-tuple-element.74), calls=%async_computation.2 | async-start | bytes 1048576 | tf_op jit(solution)/shard_map/all_to_all | solution.py:412
  74.0 0.8 copy-start.2
  74.8 1.0 copy-start.3
  91.4 9.4 %collective-permute-start.6 = (bf16[64,4096]{1,0:T(8,128)(2,1)S(1)}, bf16[64,4096]{1,0:T(8,128)(2,1)S(1)}, u32[]{:S(2)}, u32[]{:S(2)}) collective-permute-start(bf16[64,4096]{1,0:T(8,128)(2,1)S(1)} %get-tuple-element.85.refs_2_), channel_id=1, source_target_pairs={{0,1},{1,0},{2,3},{3,2},{4,5},{5,4},{6,7},{7,6},{8,9},{9,8},{10,11... | collective-permute-start | bytes 1572872 | tf_op jit(solution)/shard_map/ppermute | solution.py:411
  92.6 15.5 %collective-permute-start.7 = (bf16[64,4096]{1,0:T(8,128)(2,1)S(1)}, bf16[64,4096]{1,0:T(8,128)(2,1)S(1)}, u32[]{:S(2)}, u32[]{:S(2)}) collective-permute-start(bf16[64,4096]{1,0:T(8,128)(2,1)S(1)} %get-tuple-element.85.refs_2_), channel_id=1, source_target_pairs={{0,127},{1,2},{2,1},{3,4},{4,3},{5,6},{6,5},{7,8},{8,7},{9,10},{10... | collective-permute-start | bytes 1572872 | tf_op jit(solution)/shard_map/ppermute | solution.py:410
  92.6 21.8 %all-to-all-start.3 = ((bf16[128,16,128]{2,1,0:T(8,128)(2,1)}), bf16[128,16,128]{2,1,0:T(8,128)(2,1)S(1)}, u32[]{:S(2)}, u32[]{:S(2)}) async-start(bf16[128,16,128]{2,1,0:T(8,128)(2,1)} %get-tuple-element.84), calls=%async_computation.3 | async-start | bytes 1048576 | tf_op jit(solution)/shard_map/all_to_all | solution.py:412
  100.8 0.8 copy-start.4
  101.6 1.0 copy-start.5
  118.2 9.4 %collective-permute-start.8 = (bf16[64,4096]{1,0:T(8,128)(2,1)S(1)}, bf16[64,4096]{1,0:T(8,128)(2,1)S(1)}, u32[]{:S(2)}, u32[]{:S(2)}) collective-permute-start(bf16[64,4096]{1,0:T(8,128)(2,1)S(1)} %get-tuple-element.95.refs_2_), channel_id=1, source_target_pairs={{0,1},{1,0},{2,3},{3,2},{4,5},{5,4},{6,7},{7,6},{8,9},{9,8},{10,11... | collective-permute-start | bytes 1572872 | tf_op jit(solution)/shard_map/ppermute | solution.py:411
  119.4 14.9 %collective-permute-start.9 = (bf16[64,4096]{1,0:T(8,128)(2,1)S(1)}, bf16[64,4096]{1,0:T(8,128)(2,1)S(1)}, u32[]{:S(2)}, u32[]{:S(2)}) collective-permute-start(bf16[64,4096]{1,0:T(8,128)(2,1)S(1)} %get-tuple-element.95.refs_2_), channel_id=1, source_target_pairs={{0,127},{1,2},{2,1},{3,4},{4,3},{5,6},{6,5},{7,8},{8,7},{9,10},{10... | collective-permute-start | bytes 1572872 | tf_op jit(solution)/shard_map/ppermute | solution.py:410
  119.4 21.8 %all-to-all-start.4 = ((bf16[128,16,128]{2,1,0:T(8,128)(2,1)}), bf16[128,16,128]{2,1,0:T(8,128)(2,1)S(1)}, u32[]{:S(2)}, u32[]{:S(2)}) async-start(bf16[128,16,128]{2,1,0:T(8,128)(2,1)} %get-tuple-element.94), calls=%async_computation.4 | async-start | bytes 1048576 | tf_op jit(solution)/shard_map/all_to_all | solution.py:412
  127.5 0.8 copy-start.6
  128.3 1.0 copy-start.7

commit v4 on v3

--- a/solution.py
+++ b/solution.py
@@ -42,12 +42,12 @@
     slots = x.shape[0] // 16
 
     def copy(q):
-        return pltpu.make_async_copy(x.at[pl.ds(16 * q, 16)], send.at[dest[q]], sem.at[q])
+        return pltpu.make_async_copy(x.at[pl.ds(16 * q, 16)], send.at[dest[0, q]], sem.at[q])
 
     for act in ("start", "wait"):
         for q in range(slots):
 
-            @pl.when(dest[q] >= 0)
+            @pl.when(dest[0, q] >= 0)
             def _():
                 getattr(copy(q), act)()
 
@@ -82,10 +82,38 @@
         half_copy(factor, wide, sems, c, h).wait()
 
 
-def first_kernel(dest, field_in, factor, send, field, source, x, sems, psem, fsem):
+def destinations(far_src, far_count):
+    slots, rows = far_src.shape
+    live = lax.broadcasted_iota(jnp.int32, (slots, rows), 0) < far_count
+    hits = jnp.where((far_src == lax.axis_index("panels")) & live, 1.0, 0.0)
+    has = jnp.max(hits, axis=0, keepdims=True)
+    first = lax.broadcasted_iota(jnp.int32, (rows, rows), 0)
+    second = lax.broadcasted_iota(jnp.int32, (rows, rows), 1)
+    wide = jnp.broadcast_to(has, (8, rows))
+    rank = jnp.dot(wide, jnp.where(first < second, 1.0, 0.0), preferred_element_type=F32)[:1]
+    match = jnp.where((rank == first.astype(F32)) & (has > 0.5), 1.0, 0.0)
+    order = lax.broadcasted_iota(jnp.int32, (8, rows), 1).astype(F32) + 1.0
+    return nt(order, match)[:1].astype(jnp.int32) - 1
+
+
+def first_kernel(
+    far_src, far_count, field_in, factor, send, field, dest,
+    source, x, src_here, count_here, dest_here, sems, psem, fsem, lsems,
+):
+    plan = [
+        pltpu.make_async_copy(far_src, src_here, lsems.at[0]),
+        pltpu.make_async_copy(far_count, count_here.at[0], lsems.at[1]),
+    ]
+    for copy in plan:
+        copy.start()
     brought = pltpu.make_async_copy(field_in, field, fsem)
     brought.start()
     start_halves(factor, source, sems)
+    for copy in plan:
+        copy.wait()
+    dest_here[...] = destinations(src_here[...], count_here[...])
+    placed = pltpu.make_async_copy(dest_here, dest, lsems.at[2])
+    placed.start()
     brought.wait()
     parts = sems.shape[0]
     per = field.shape[1] // 256 // parts
@@ -95,6 +123,7 @@
         for i in range(c * per, c * per + per):
             accs = project(source, accs, i, field[:, 256 * i : 256 * i + 256])
     x[...] = jnp.concatenate(accs, axis=1).astype(BF16)
+    placed.wait()
     for _ in place(dest, x, send, psem):
         pass
 
@@ -344,17 +373,6 @@
         copy.wait()
 
 
-def far_lists(far_src, far_count, own):
-    rows, slots = far_src.shape
-    live = jnp.arange(slots, dtype=jnp.int32)[None, :] < far_count[:, None]
-    has = jnp.any((far_src == own) & live, axis=1)
-    order = jnp.arange(rows, dtype=jnp.int32)
-    rank = jnp.sum((has[None, :] & (order[None, :] < order[:, None])).astype(jnp.int32), axis=1)
-    hit = has[None, :] & (rank[None, :] == jnp.arange(slots, dtype=jnp.int32)[:, None])
-    dest = jnp.max(jnp.where(hit, order[None, :], -1), axis=1)
-    return dest
-
-
 def shards(
     excitation, near_tiles, near_offset, near_count, far_src, far_count, source_factor, target_factor
 ):
@@ -363,7 +381,6 @@
     rows, slots = far_src.shape
     rank = source_factor.shape[1]
     count = lax.axis_size("panels")
-    dest = far_lists(far_src, far_count, lax.axis_index("panels"))
 
     tile_total = leaves * near_slots
     near = streamed(near_tiles.reshape(tile_total, leaf, leaf))
@@ -403,10 +420,16 @@
     turned_src = far_src.T
     for step in range(ITERS):
         if step == 0:
-            send, field = call(
-                first_kernel, (send_type, field_type), [SMEM, ANY, ANY], (ANY, VMEM),
-                [half_type, picked_type, dma((PARTS, 2)), dma((slots,)), dma], far_flops, "first",
-            )(dest, streamed(excitation), source_factor)
+            row_type = jax.ShapeDtypeStruct((1, rows), jnp.int32)
+            send, field, dest = call(
+                first_kernel, (send_type, field_type, row_type), [ANY, ANY, ANY, ANY], (ANY, VMEM, SMEM),
+                [
+                    half_type, picked_type, pltpu.VMEM((slots, rows), jnp.int32),
+                    pltpu.VMEM((1, rows), jnp.int32), pltpu.VMEM((1, rows), jnp.int32),
+                    dma((PARTS, 2)), dma((slots,)), dma, dma((3,)),
+                ],
+                far_flops, "first",
+            )(streamed(turned_src), streamed(far_count), streamed(excitation), source_factor)
         outer = lax.ppermute(field, "panels", outward)
         mate = lax.ppermute(field, "panels", inward)
         received = lax.all_to_all(send, "panels", split_axis=0, concat_axis=0, tiled=True)

time: 146 us -> 146 us (level)
    pallas_call x4, Pallas kernels: 9.42 us -> 11.2 us  [shards(): call(others_kernel, (acc_type, x_type), [SMEM, SMEM, VMEM, VMEM, VMEM, VM...]
  transfers between devices with their start and end apart: 15 -> 15, of which waited for: 5 -> 5; matrix products, arithmetic and copies ran while one was open for 0% -> 0% of each run, Pallas kernels for 29% -> 30%
where the time goes in v4:
time: 146 us; the launch traced here: 145 us
  Pallas kernels  66.4 us (45%)
  starting transfers between devices  52.8 us (36%)
  waiting for transfers between devices  17.9 us (12%)
  local copies, waits for them, and re-layouts  7.35 us (5%)
    all_to_all x5, starting transfers between devices, shards(): lax.all_to_all(send, 'panels', split_axis=0, concat_axis=0, tiled=True)  44.7 us
    pallas_call x4, Pallas kernels, shards(): call(lambda *refs, step=step, last=last: (last_local_kernel if last else...  20.7 us
    all_to_all x5, waiting for transfers between devices, shards(): lax.all_to_all(send, 'panels', split_axis=0, concat_axis=0, tiled=True)  17.9 us
    pallas_call x4, Pallas kernels, shards(): call(lambda *refs, step=step: far_kernel(step, *refs), (field_type, send_...  14.9 us
    pallas_call x4, Pallas kernels, shards(): call(others_kernel, (acc_type, x_type), [SMEM, SMEM, VMEM, VMEM, VMEM, VM...  11.2 us
    pallas_call x1, Pallas kernels, shards(): call(setup_kernel, (acc_type, tiles_type, half_type, pltpu.HBM(gram_shape...  9.78 us
    unnamed x24, local copies, waits for them, and re-layouts  7.35 us
    ppermute x5, starting transfers between devices, shards(): mate = lax.ppermute(field, 'panels', inward)  6.43 us
  transfers between devices with their start and end apart: 15, of which 5 were waited for; matrix products, arithmetic and copies ran while one was open for 0% of the time, Pallas kernels for 30%

profile of v4, /device:TPU:1, one launch (start us, length us, event | category | flops | bytes accessed | tf_op | source)
XLA Modules:
  0.0 144.9 jit_solution(15695029657541410778)
XLA Ops:
  0.0 4.3 %first.1 = (bf16[128,16,128]{2,1,0:T(8,128)(2,1)}, bf16[64,4096]{1,0:T(8,128)(2,1)S(1)}, s32[1,128]{1,0:T(1,128)S(1)}) custom-call(s32[16,128]{1,0:T(8,128)} %bitcast.3, s32[128]{0:T(128)} %refs_1_.9, bf16[64,4096]{1,0:T(8,128)(2,1)} %field_in.1, bf16[16,32,4096]{2,1,0:T(8,128)(2,1)} %refs_5_.5), custom_call_target="tpu_custom_call" | custom-call | flops 268435456 | bytes 4194304 | tf_op jit(solution)/shard_map/first/pallas_call | solution.py:424
  4.4 1.5 %collective-permute-start = (bf16[64,4096]{1,0:T(8,128)(2,1)S(1)}, bf16[64,4096]{1,0:T(8,128)(2,1)S(1)}, u32[]{:S(2)}, u32[]{:S(2)}) collective-permute-start(bf16[64,4096]{1,0:T(8,128)(2,1)S(1)} %get-tuple-element.56.field), channel_id=1, source_target_pairs={{0,1},{1,0},{2,3},{3,2},{4,5},{5,4},{6,7},{7,6},{8,9},{9,8},{10,11... | collective-permute-start | bytes 1572872 | tf_op jit(solution)/shard_map/ppermute | solution.py:434
  5.9 1.7 %collective-permute-start.1 = (bf16[64,4096]{1,0:T(8,128)(2,1)S(1)}, bf16[64,4096]{1,0:T(8,128)(2,1)S(1)}, u32[]{:S(2)}, u32[]{:S(2)}) collective-permute-start(bf16[64,4096]{1,0:T(8,128)(2,1)S(1)} %get-tuple-element.56.field), channel_id=1, source_target_pairs={{0,127},{1,2},{2,1},{3,4},{4,3},{5,6},{6,5},{7,8},{8,7},{9,10},{10... | collective-permute-start | bytes 1572872 | tf_op jit(solution)/shard_map/ppermute | solution.py:433
  7.6 10.6 %all-to-all-start = ((bf16[128,16,128]{2,1,0:T(8,128)(2,1)}), bf16[128,16,128]{2,1,0:T(8,128)(2,1)S(1)}, u32[]{:S(2)}, u32[]{:S(2)}) async-start(bf16[128,16,128]{2,1,0:T(8,128)(2,1)} %get-tuple-element.55), calls=%async_computation | async-start | bytes 1048576 | tf_op jit(solution)/shard_map/all_to_all | solution.py:435
  18.2 9.8 %setup.1 = (f32[17,64,256]{2,1,0:T(8,128)S(1)}, bf16[88,256,256]{2,1,0:T(8,128)(2,1)S(1)}, bf16[2,16,16,4096]{3,2,1,0:T(8,128)(2,1)S(1)}, bf16[2,2,256,256]{3,2,...) custom-call(s32[5,16]{1,0:T(8,128)S(1)} %bitcast.9, s32[16]{0:T(128)S(1)} %copy-done.11, ...), custom_call_target="tpu_custom_call" | custom-call | flops 335544320 | bytes 4194304 | tf_op jit(solution)/shard_map/setup/pallas_call | solution.py:438
  28.0 2.8 %others.5 = (f32[17,64,256]{2,1,0:T(8,128)S(1)}, f32[256,128]{1,0:T(8,128)S(1)}) custom-call(s32[2,3,88]{2,1,0:T(4,128)S(1)} %get-tuple-element.58.lists.refs_0_, s32[2]{0:T(128)S(1)} %get-tuple-element.59.counts.refs_1_, bf16[88,256,256]{2,1,0:T(8,128)(2,1)S(1)} %get-tuple-element.60.tiles, ...), custom_call_target="tpu_custom_call", output_to_operand_aliasing={{0}: (5, {})} | custom-call | flops 335544320 | bytes 4194304 | tf_op jit(solution)/shard_map/others/pallas_call | solution.py:476
  30.8 1.2 all-to-all-done.refs_3_
  32.0 3.7 %far.4 = (bf16[64,4096]{1,0:T(8,128)(2,1)S(1)}, bf16[128,16,128]{2,1,0:T(8,128)(2,1)}, f32[5,64,4096]{2,1,0:T(8,128)}, f32[64,2048]{1,0:T(8,128)S(1)}) custom-call(s32[16,128]{1,0:T(8,128)S(1)} %bitcast.4, s32[128]{0:T(128)S(1)} %copy-done.9, s32[1,128]{1,0:T(1,128)S(1)} %get-tuple-element.54.refs_2_, ...), custom_call_target="tpu_custom_call", output_to_operand_aliasing={{2}: (8, {})} | custom-call | flops 268435456 | bytes 4194304 | tf_op jit(solution)/shard_map/far/pallas_call | solution.py:481
  35.7 1.2 collective-permute-start.2
  36.9 9.8 %all-to-all-start.1 = ((bf16[128,16,128]{2,1,0:T(8,128)(2,1)}), bf16[128,16,128]{2,1,0:T(8,128)(2,1)S(1)}, u32[]{:S(2)}, u32[]{:S(2)}) async-start(bf16[128,16,128]{2,1,0:T(8,128)(2,1)} %get-tuple-element.66), calls=%async_computation.1 | async-start | bytes 1048576 | tf_op jit(solution)/shard_map/all_to_all | solution.py:435
  48.5 5.4 %local.4 = (f32[17,64,256]{2,1,0:T(8,128)S(1)}, bf16[88,256,256]{2,1,0:T(8,128)(2,1)S(1)}, bf16[2,16,16,4096]{3,2,1,0:T(8,128)(2,1)S(1)}, f32[5,64,4096]{2,1,0:T(8,128)}) custom-call(s32[2,3,88]{2,1,0:T(4,128)S(1)} %get-tuple-element.58.lists.refs_0_, s32[2]{0:T(128)S(1)} %get-tuple-element.59.counts.refs_1_, ...), custom_call_target="tpu_custom_call", output_to_operand_aliasing={{3}: (7, {})} | custom-call | flops 335544320 | bytes 4194304 | tf_op jit(solution)/shard_map/local/pallas_call | solution.py:452
  54.0 2.8 %others.6 = (f32[17,64,256]{2,1,0:T(8,128)S(1)}, f32[256,128]{1,0:T(8,128)S(1)}) custom-call(s32[2,3,88]{2,1,0:T(4,128)S(1)} %get-tuple-element.58.lists.refs_0_, s32[2]{0:T(128)S(1)} %get-tuple-element.59.counts.refs_1_, bf16[88,256,256]{2,1,0:T(8,128)(2,1)S(1)} %get-tuple-element.70.tiles, ...), custom_call_target="tpu_custom_call", output_to_operand_aliasing={{0}: (5, {})} | custom-call | flops 335544320 | bytes 4194304 | tf_op jit(solution)/shard_map/others/pallas_call | solution.py:476
  56.8 3.7 %all-to-all-done.1.refs_3_ = bf16[128,16,128]{2,1,0:T(8,128)(2,1)S(1)} async-done(((bf16[128,16,128]{2,1,0:T(8,128)(2,1)}), bf16[128,16,128]{2,1,0:T(8,128)(2,1)S(1)}, u32[]{:S(2)}, u32[]{:S(2)}) %all-to-all-start.1) | async-done | bytes 524320 | tf_op jit(solution)/shard_map/all_to_all | solution.py:435
  60.5 3.7 %far.5 = (bf16[64,4096]{1,0:T(8,128)(2,1)S(1)}, bf16[128,16,128]{2,1,0:T(8,128)(2,1)}, f32[5,64,4096]{2,1,0:T(8,128)}, f32[64,2048]{1,0:T(8,128)S(1)}) custom-call(s32[16,128]{1,0:T(8,128)S(1)} %bitcast.5, s32[128]{0:T(128)S(1)} %copy-done.9, s32[1,128]{1,0:T(1,128)S(1)} %get-tuple-element.54.refs_2_, ...), custom_call_target="tpu_custom_call", output_to_operand_aliasing={{2}: (8, {})} | custom-call | flops 268435456 | bytes 4194304 | tf_op jit(solution)/shard_map/far/pallas_call | solution.py:481
  64.2 1.2 collective-permute-start.4
  65.5 8.1 %all-to-all-start.2 = ((bf16[128,16,128]{2,1,0:T(8,128)(2,1)}), bf16[128,16,128]{2,1,0:T(8,128)(2,1)S(1)}, u32[]{:S(2)}, u32[]{:S(2)}) async-start(bf16[128,16,128]{2,1,0:T(8,128)(2,1)} %get-tuple-element.76), calls=%async_computation.2 | async-start | bytes 1048576 | tf_op jit(solution)/shard_map/all_to_all | solution.py:435
  75.4 5.4 %local.5 = (f32[17,64,256]{2,1,0:T(8,128)S(1)}, bf16[88,256,256]{2,1,0:T(8,128)(2,1)S(1)}, bf16[2,16,16,4096]{3,2,1,0:T(8,128)(2,1)S(1)}, f32[5,64,4096]{2,1,0:T(8,128)}) custom-call(s32[2,3,88]{2,1,0:T(4,128)S(1)} %get-tuple-element.58.lists.refs_0_, s32[2]{0:T(128)S(1)} %get-tuple-element.59.counts.refs_1_, ...), custom_call_target="tpu_custom_call", output_to_operand_aliasing={{3}: (7, {})} | custom-call | flops 335544320 | bytes 4194304 | tf_op jit(solution)/shard_map/local/pallas_call | solution.py:452
  80.9 2.8 %others.7 = (f32[17,64,256]{2,1,0:T(8,128)S(1)}, f32[256,128]{1,0:T(8,128)S(1)}) custom-call(s32[2,3,88]{2,1,0:T(4,128)S(1)} %get-tuple-element.58.lists.refs_0_, s32[2]{0:T(128)S(1)} %get-tuple-element.59.counts.refs_1_, bf16[88,256,256]{2,1,0:T(8,128)(2,1)S(1)} %get-tuple-element.80.tiles, ...), custom_call_target="tpu_custom_call", output_to_operand_aliasing={{0}: (5, {})} | custom-call | flops 335544320 | bytes 4194304 | tf_op jit(solution)/shard_map/others/pallas_call | solution.py:476
  83.7 3.6 %all-to-all-done.2.refs_3_ = bf16[128,16,128]{2,1,0:T(8,128)(2,1)S(1)} async-done(((bf16[128,16,128]{2,1,0:T(8,128)(2,1)}), bf16[128,16,128]{2,1,0:T(8,128)(2,1)S(1)}, u32[]{:S(2)}, u32[]{:S(2)}) %all-to-all-start.2) | async-done | bytes 524320 | tf_op jit(solution)/shard_map/all_to_all | solution.py:435
  87.3 3.7 %far.6 = (bf16[64,4096]{1,0:T(8,128)(2,1)S(1)}, bf16[128,16,128]{2,1,0:T(8,128)(2,1)}, f32[5,64,4096]{2,1,0:T(8,128)}, f32[64,2048]{1,0:T(8,128)S(1)}) custom-call(s32[16,128]{1,0:T(8,128)S(1)} %bitcast.6, s32[128]{0:T(128)S(1)} %copy-done.9, s32[1,128]{1,0:T(1,128)S(1)} %get-tuple-element.54.refs_2_, ...), custom_call_target="tpu_custom_call", output_to_operand_aliasing={{2}: (8, {})} | custom-call | flops 268435456 | bytes 4194304 | tf_op jit(solution)/shard_map/far/pallas_call | solution.py:481
  91.0 1.2 collective-permute-start.6
  92.2 8.1 %all-to-all-start.3 = ((bf16[128,16,128]{2,1,0:T(8,128)(2,1)}), bf16[128,16,128]{2,1,0:T(8,128)(2,1)S(1)}, u32[]{:S(2)}, u32[]{:S(2)}) async-start(bf16[128,16,128]{2,1,0:T(8,128)(2,1)} %get-tuple-element.86), calls=%async_computation.3 | async-start | bytes 1048576 | tf_op jit(solution)/shard_map/all_to_all | solution.py:435
  102.2 5.4 %local.6 = (f32[17,64,256]{2,1,0:T(8,128)S(1)}, bf16[88,256,256]{2,1,0:T(8,128)(2,1)S(1)}, bf16[2,16,16,4096]{3,2,1,0:T(8,128)(2,1)S(1)}, f32[5,64,4096]{2,1,0:T(8,128)}) custom-call(s32[2,3,88]{2,1,0:T(4,128)S(1)} %get-tuple-element.58.lists.refs_0_, s32[2]{0:T(128)S(1)} %get-tuple-element.59.counts.refs_1_, ...), custom_call_target="tpu_custom_call", output_to_operand_aliasing={{3}: (7, {})} | custom-call | flops 335544320 | bytes 4194304 | tf_op jit(solution)/shard_map/local/pallas_call | solution.py:452
  107.6 2.8 %others.8 = (f32[17,64,256]{2,1,0:T(8,128)S(1)}, f32[256,128]{1,0:T(8,128)S(1)}) custom-call(s32[2,3,88]{2,1,0:T(4,128)S(1)} %get-tuple-element.58.lists.refs_0_, s32[2]{0:T(128)S(1)} %get-tuple-element.59.counts.refs_1_, bf16[88,256,256]{2,1,0:T(8,128)(2,1)S(1)} %get-tuple-element.90.tiles, ...), custom_call_target="tpu_custom_call", output_to_operand_aliasing={{0}: (5, {})} | custom-call | flops 335544320 | bytes 4194304 | tf_op jit(solution)/shard_map/others/pallas_call | solution.py:476
  110.5 3.6 %all-to-all-done.3.refs_3_ = bf16[128,16,128]{2,1,0:T(8,128)(2,1)S(1)} async-done(((bf16[128,16,128]{2,1,0:T(8,128)(2,1)}), bf16[128,16,128]{2,1,0:T(8,128)(2,1)S(1)}, u32[]{:S(2)}, u32[]{:S(2)}) %all-to-all-start.3) | async-done | bytes 524320 | tf_op jit(solution)/shard_map/all_to_all | solution.py:435
  114.0 3.7 %far.7 = (bf16[64,4096]{1,0:T(8,128)(2,1)S(1)}, bf16[128,16,128]{2,1,0:T(8,128)(2,1)}, f32[5,64,4096]{2,1,0:T(8,128)}, f32[64,2048]{1,0:T(8,128)S(1)}) custom-call(s32[16,128]{1,0:T(8,128)S(1)} %bitcast.7, s32[128]{0:T(128)S(1)} %copy-done.9, s32[1,128]{1,0:T(1,128)S(1)} %get-tuple-element.54.refs_2_, ...), custom_call_target="tpu_custom_call", output_to_operand_aliasing={{2}: (8, {})} | custom-call | flops 268435456 | bytes 4194304 | tf_op jit(solution)/shard_map/far/pallas_call | solution.py:481
  117.8 1.2 collective-permute-start.8
  119.0 8.1 %all-to-all-start.4 = ((bf16[128,16,128]{2,1,0:T(8,128)(2,1)}), bf16[128,16,128]{2,1,0:T(8,128)(2,1)S(1)}, u32[]{:S(2)}, u32[]{:S(2)}) async-start(bf16[128,16,128]{2,1,0:T(8,128)(2,1)} %get-tuple-element.96), calls=%async_computation.4 | async-start | bytes 1048576 | tf_op jit(solution)/shard_map/all_to_all | solution.py:435
  129.0 4.5 %local.7 = (f32[17,64,256]{2,1,0:T(8,128)S(1)}, bf16[88,256,256]{2,1,0:T(8,128)(2,1)S(1)}, f32[5,64,4096]{2,1,0:T(8,128)}) custom-call(s32[2,3,88]{2,1,0:T(4,128)S(1)} %get-tuple-element.58.lists.refs_0_, s32[2]{0:T(128)S(1)} %get-tuple-element.59.counts.refs_1_, bf16[64,4096]{1,0:T(8,128)(2,1)S(1)} %get-tuple-element.97.refs_2_, ...), custom_call_target="tpu_custom_call", output_to_operand_aliasing={{2}: (6, {})} | custom-call | flops 335544320 | bytes 4194304 | tf_op jit(solution)/shard_map/local/pallas_call | solution.py:452
  133.5 1.5 %others.9.refs_4_ = f32[17,64,256]{2,1,0:T(8,128)S(1)} custom-call(s32[2,3,88]{2,1,0:T(4,128)S(1)} %get-tuple-element.58.lists.refs_0_, s32[2]{0:T(128)S(1)} %get-tuple-element.59.counts.refs_1_, bf16[88,256,256]{2,1,0:T(8,128)(2,1)S(1)} %get-tuple-element.100.tiles, ...), custom_call_target="tpu_custom_call", output_to_operand_aliasing={{}: (4, {})} | custom-call | flops 335544320 | bytes 4194304 | tf_op jit(solution)/shard_map/others/pallas_call | solution.py:466
  135.0 5.8 %all-to-all-done.4.refs_2_ = bf16[128,16,128]{2,1,0:T(8,128)(2,1)S(1)} async-done(((bf16[128,16,128]{2,1,0:T(8,128)(2,1)}), bf16[128,16,128]{2,1,0:T(8,128)(2,1)S(1)}, u32[]{:S(2)}, u32[]{:S(2)}) %all-to-all-start.4) | async-done | bytes 524320 | tf_op jit(solution)/shard_map/all_to_all | solution.py:435
  140.8 3.9 %last.1 = f32[5,64,4096]{2,1,0:T(8,128)} custom-call(s32[16,128]{1,0:T(8,128)S(1)} %bitcast.8, s32[128]{0:T(128)S(1)} %copy-done.9, bf16[128,16,128]{2,1,0:T(8,128)(2,1)S(1)} %all-to-all-done.4.refs_2_, bf16[16,32,4096]{2,1,0:T(8,128)(2,1)} %refs_3_.1, f32[17,64,256]{2,1,0:T(8,128)S(1)} %others.9.refs_4_, ...), custom_call_target="tpu_custom_call", output_to_operand_aliasing={{}: (5, {})} | custom-call | flops 268435456 | bytes 4194304 | tf_op jit(solution)/shard_map/last/pallas_call | solution.py:470
  (38 shorter events, 7.4 us)
Async XLA Ops:
  0.0 18.1 %copy-start.10 = (s32[16,5]{0,1:T(8,128)S(1)}, s32[16,5]{0,1:T(8,128)}, u32[]{:S(2)}) copy-start(s32[16,5]{0,1:T(8,128)} %param.10) | copy-start | bytes 964
  0.0 18.2 %copy-start.11 = (s32[16]{0:T(128)S(1)}, s32[16]{0:T(128)}, u32[]{:S(2)}) copy-start(s32[16]{0:T(128)} %count.1) | copy-start | bytes 196
  4.4 13.8 %collective-permute-start = (bf16[64,4096]{1,0:T(8,128)(2,1)S(1)}, bf16[64,4096]{1,0:T(8,128)(2,1)S(1)}, u32[]{:S(2)}, u32[]{:S(2)}) collective-permute-start(bf16[64,4096]{1,0:T(8,128)(2,1)S(1)} %get-tuple-element.56.field), channel_id=1, source_target_pairs={{0,1},{1,0},{2,3},{3,2},{4,5},{5,4},{6,7},{7,6},{8,9},{9,8},{10,11... | collective-permute-start | bytes 1572872 | tf_op jit(solution)/shard_map/ppermute | solution.py:434
  5.9 22.1 %collective-permute-start.1 = (bf16[64,4096]{1,0:T(8,128)(2,1)S(1)}, bf16[64,4096]{1,0:T(8,128)(2,1)S(1)}, u32[]{:S(2)}, u32[]{:S(2)}) collective-permute-start(bf16[64,4096]{1,0:T(8,128)(2,1)S(1)} %get-tuple-element.56.field), channel_id=1, source_target_pairs={{0,127},{1,2},{2,1},{3,4},{4,3},{5,6},{6,5},{7,8},{8,7},{9,10},{10... | collective-permute-start | bytes 1572872 | tf_op jit(solution)/shard_map/ppermute | solution.py:433
  7.6 24.4 %all-to-all-start = ((bf16[128,16,128]{2,1,0:T(8,128)(2,1)}), bf16[128,16,128]{2,1,0:T(8,128)(2,1)S(1)}, u32[]{:S(2)}, u32[]{:S(2)}) async-start(bf16[128,16,128]{2,1,0:T(8,128)(2,1)} %get-tuple-element.55), calls=%async_computation | async-start | bytes 1048576 | tf_op jit(solution)/shard_map/all_to_all | solution.py:435
  28.0 4.0 %copy-start.8 = (s32[128,16]{0,1:T(8,128)S(1)}, s32[128,16]{0,1:T(8,128)}, u32[]{:S(2)}) copy-start(s32[128,16]{0,1:T(8,128)} %param.12) | copy-start | bytes 24580
  28.0 4.0 %copy-start.9 = (s32[128]{0:T(128)S(1)}, s32[128]{0:T(128)}, u32[]{:S(2)}) copy-start(s32[128]{0:T(128)} %refs_1_.9) | copy-start | bytes 1540
  35.7 11.0 %collective-permute-start.2 = (bf16[64,4096]{1,0:T(8,128)(2,1)S(1)}, bf16[64,4096]{1,0:T(8,128)(2,1)S(1)}, u32[]{:S(2)}, u32[]{:S(2)}) collective-permute-start(bf16[64,4096]{1,0:T(8,128)(2,1)S(1)} %get-tuple-element.67.refs_2_), channel_id=1, source_target_pairs={{0,1},{1,0},{2,3},{3,2},{4,5},{5,4},{6,7},{7,6},{8,9},{9,8},{10,11... | collective-permute-start | bytes 1572872 | tf_op jit(solution)/shard_map/ppermute | solution.py:434
  36.9 17.0 %collective-permute-start.3 = (bf16[64,4096]{1,0:T(8,128)(2,1)S(1)}, bf16[64,4096]{1,0:T(8,128)(2,1)S(1)}, u32[]{:S(2)}, u32[]{:S(2)}) collective-permute-start(bf16[64,4096]{1,0:T(8,128)(2,1)S(1)} %get-tuple-element.67.refs_2_), channel_id=1, source_target_pairs={{0,127},{1,2},{2,1},{3,4},{4,3},{5,6},{6,5},{7,8},{8,7},{9,10},{10... | collective-permute-start | bytes 1572872 | tf_op jit(solution)/shard_map/ppermute | solution.py:433
  36.9 23.6 %all-to-all-start.1 = ((bf16[128,16,128]{2,1,0:T(8,128)(2,1)}), bf16[128,16,128]{2,1,0:T(8,128)(2,1)S(1)}, u32[]{:S(2)}, u32[]{:S(2)}) async-start(bf16[128,16,128]{2,1,0:T(8,128)(2,1)} %get-tuple-element.66), calls=%async_computation.1 | async-start | bytes 1048576 | tf_op jit(solution)/shard_map/all_to_all | solution.py:435
  46.7 0.8 copy-start
  47.5 1.0 copy-start.1
  64.2 9.4 %collective-permute-start.4 = (bf16[64,4096]{1,0:T(8,128)(2,1)S(1)}, bf16[64,4096]{1,0:T(8,128)(2,1)S(1)}, u32[]{:S(2)}, u32[]{:S(2)}) collective-permute-start(bf16[64,4096]{1,0:T(8,128)(2,1)S(1)} %get-tuple-element.77.refs_2_), channel_id=1, source_target_pairs={{0,1},{1,0},{2,3},{3,2},{4,5},{5,4},{6,7},{7,6},{8,9},{9,8},{10,11... | collective-permute-start | bytes 1572872 | tf_op jit(solution)/shard_map/ppermute | solution.py:434
  65.5 15.4 %collective-permute-start.5 = (bf16[64,4096]{1,0:T(8,128)(2,1)S(1)}, bf16[64,4096]{1,0:T(8,128)(2,1)S(1)}, u32[]{:S(2)}, u32[]{:S(2)}) collective-permute-start(bf16[64,4096]{1,0:T(8,128)(2,1)S(1)} %get-tuple-element.77.refs_2_), channel_id=1, source_target_pairs={{0,127},{1,2},{2,1},{3,4},{4,3},{5,6},{6,5},{7,8},{8,7},{9,10},{10... | collective-permute-start | bytes 1572872 | tf_op jit(solution)/shard_map/ppermute | solution.py:433
  65.5 21.8 %all-to-all-start.2 = ((bf16[128,16,128]{2,1,0:T(8,128)(2,1)}), bf16[128,16,128]{2,1,0:T(8,128)(2,1)S(1)}, u32[]{:S(2)}, u32[]{:S(2)}) async-start(bf16[128,16,128]{2,1,0:T(8,128)(2,1)} %get-tuple-element.76), calls=%async_computation.2 | async-start | bytes 1048576 | tf_op jit(solution)/shard_map/all_to_all | solution.py:435
  73.6 0.8 copy-start.2
  74.4 1.0 copy-start.3
  91.0 9.4 %collective-permute-start.6 = (bf16[64,4096]{1,0:T(8,128)(2,1)S(1)}, bf16[64,4096]{1,0:T(8,128)(2,1)S(1)}, u32[]{:S(2)}, u32[]{:S(2)}) collective-permute-start(bf16[64,4096]{1,0:T(8,128)(2,1)S(1)} %get-tuple-element.87.refs_2_), channel_id=1, source_target_pairs={{0,1},{1,0},{2,3},{3,2},{4,5},{5,4},{6,7},{7,6},{8,9},{9,8},{10,11... | collective-permute-start | bytes 1572872 | tf_op jit(solution)/shard_map/ppermute | solution.py:434
  92.2 15.4 %collective-permute-start.7 = (bf16[64,4096]{1,0:T(8,128)(2,1)S(1)}, bf16[64,4096]{1,0:T(8,128)(2,1)S(1)}, u32[]{:S(2)}, u32[]{:S(2)}) collective-permute-start(bf16[64,4096]{1,0:T(8,128)(2,1)S(1)} %get-tuple-element.87.refs_2_), channel_id=1, source_target_pairs={{0,127},{1,2},{2,1},{3,4},{4,3},{5,6},{6,5},{7,8},{8,7},{9,10},{10... | collective-permute-start | bytes 1572872 | tf_op jit(solution)/shard_map/ppermute | solution.py:433
  92.2 21.8 %all-to-all-start.3 = ((bf16[128,16,128]{2,1,0:T(8,128)(2,1)}), bf16[128,16,128]{2,1,0:T(8,128)(2,1)S(1)}, u32[]{:S(2)}, u32[]{:S(2)}) async-start(bf16[128,16,128]{2,1,0:T(8,128)(2,1)} %get-tuple-element.86), calls=%async_computation.3 | async-start | bytes 1048576 | tf_op jit(solution)/shard_map/all_to_all | solution.py:435
  100.4 0.8 copy-start.4
  101.2 1.0 copy-start.5
  117.8 9.4 %collective-permute-start.8 = (bf16[64,4096]{1,0:T(8,128)(2,1)S(1)}, bf16[64,4096]{1,0:T(8,128)(2,1)S(1)}, u32[]{:S(2)}, u32[]{:S(2)}) collective-permute-start(bf16[64,4096]{1,0:T(8,128)(2,1)S(1)} %get-tuple-element.97.refs_2_), channel_id=1, source_target_pairs={{0,1},{1,0},{2,3},{3,2},{4,5},{5,4},{6,7},{7,6},{8,9},{9,8},{10,11... | collective-permute-start | bytes 1572872 | tf_op jit(solution)/shard_map/ppermute | solution.py:434
  119.0 14.5 %collective-permute-start.9 = (bf16[64,4096]{1,0:T(8,128)(2,1)S(1)}, bf16[64,4096]{1,0:T(8,128)(2,1)S(1)}, u32[]{:S(2)}, u32[]{:S(2)}) collective-permute-start(bf16[64,4096]{1,0:T(8,128)(2,1)S(1)} %get-tuple-element.97.refs_2_), channel_id=1, source_target_pairs={{0,127},{1,2},{2,1},{3,4},{4,3},{5,6},{6,5},{7,8},{8,7},{9,10},{10... | collective-permute-start | bytes 1572872 | tf_op jit(solution)/shard_map/ppermute | solution.py:433
  119.0 21.8 %all-to-all-start.4 = ((bf16[128,16,128]{2,1,0:T(8,128)(2,1)}), bf16[128,16,128]{2,1,0:T(8,128)(2,1)S(1)}, u32[]{:S(2)}, u32[]{:S(2)}) async-start(bf16[128,16,128]{2,1,0:T(8,128)(2,1)} %get-tuple-element.96), calls=%async_computation.4 | async-start | bytes 1048576 | tf_op jit(solution)/shard_map/all_to_all | solution.py:435
  127.2 0.8 copy-start.6
  127.9 1.0 copy-start.7

commit v5 on v4

--- a/solution.py
+++ b/solution.py
@@ -231,9 +231,10 @@
         for c in range(ssems.shape[0]):
             wait_halves(source_factor, source, ssems, c)
             wait_halves(target_factor, target, tsems, c)
-        for h in range(2):
-            for g in range(2):
-                gram[h, g] = nt(source[h].reshape(-1, panels), target[g].reshape(-1, panels)).astype(BF16)
+        for g in range(2):
+            both_halves = nt(source[...].reshape(-1, panels), target[g].reshape(-1, panels)).astype(BF16)
+            for h in range(2):
+                gram[h, g] = both_halves[256 * h : 256 * h + 256]
 
     own_part(lists, counts, field, mate, near, acc, others, tiles, sems, osem, mate_here, msem, couple)
 

time: 146 us -> 146 us (level)
  waiting for transfers between devices: 17.9 us -> 16 us
  Pallas kernels: 66.4 us -> 68.2 us
    all_to_all x5, waiting for transfers between devices: 17.9 us -> 16 us  [shards(): lax.all_to_all(send, 'panels', split_axis=0, concat_axis=0, tiled=True)]
  transfers between devices with their start and end apart: 15 -> 15, of which waited for: 5 -> 5; matrix products, arithmetic and copies ran while one was open for 0% -> 0% of each run, Pallas kernels for 30% -> 31%
where the time goes in v5:
time: 146 us; the launch traced here: 145 us
  Pallas kernels  68.2 us (47%)
  starting transfers between devices  52.8 us (36%)
  waiting for transfers between devices  16 us (11%)
  local copies, waits for them, and re-layouts  7.35 us (5%)
    all_to_all x5, starting transfers between devices, shards(): lax.all_to_all(send, 'panels', split_axis=0, concat_axis=0, tiled=True)  44.7 us
    pallas_call x4, Pallas kernels, shards(): call(lambda *refs, step=step, last=last: (last_local_kernel if last else...  22.1 us
    all_to_all x5, waiting for transfers between devices, shards(): lax.all_to_all(send, 'panels', split_axis=0, concat_axis=0, tiled=True)  16 us
    pallas_call x4, Pallas kernels, shards(): call(lambda *refs, step=step: far_kernel(step, *refs), (field_type, send_...  14.9 us
    pallas_call x4, Pallas kernels, shards(): call(others_kernel, (acc_type, x_type), [SMEM, SMEM, VMEM, VMEM, VMEM, VM...  11.2 us
    pallas_call x1, Pallas kernels, shards(): call(setup_kernel, (acc_type, tiles_type, half_type, pltpu.HBM(gram_shape...  10.2 us
    unnamed x24, local copies, waits for them, and re-layouts  7.35 us
    ppermute x5, starting transfers between devices, shards(): mate = lax.ppermute(field, 'panels', inward)  6.44 us
  transfers between devices with their start and end apart: 15, of which 5 were waited for; matrix products, arithmetic and copies ran while one was open for 0% of the time, Pallas kernels for 31%

profile of v5, /device:TPU:1, one launch (start us, length us, event | category | flops | bytes accessed | tf_op | source)
XLA Modules:
  0.0 144.9 jit_solution(17273051227786869731)
XLA Ops:
  0.0 4.3 %first.1 = (bf16[128,16,128]{2,1,0:T(8,128)(2,1)}, bf16[64,4096]{1,0:T(8,128)(2,1)S(1)}, s32[1,128]{1,0:T(1,128)S(1)}) custom-call(s32[16,128]{1,0:T(8,128)} %bitcast.3, s32[128]{0:T(128)} %refs_1_.9, bf16[64,4096]{1,0:T(8,128)(2,1)} %field_in.1, bf16[16,32,4096]{2,1,0:T(8,128)(2,1)} %refs_5_.5), custom_call_target="tpu_custom_call" | custom-call | flops 268435456 | bytes 4194304 | tf_op jit(solution)/shard_map/first/pallas_call | solution.py:425
  4.4 1.5 %collective-permute-start = (bf16[64,4096]{1,0:T(8,128)(2,1)S(1)}, bf16[64,4096]{1,0:T(8,128)(2,1)S(1)}, u32[]{:S(2)}, u32[]{:S(2)}) collective-permute-start(bf16[64,4096]{1,0:T(8,128)(2,1)S(1)} %get-tuple-element.56.field), channel_id=1, source_target_pairs={{0,1},{1,0},{2,3},{3,2},{4,5},{5,4},{6,7},{7,6},{8,9},{9,8},{10,11... | collective-permute-start | bytes 1572872 | tf_op jit(solution)/shard_map/ppermute | solution.py:435
  5.9 1.7 %collective-permute-start.1 = (bf16[64,4096]{1,0:T(8,128)(2,1)S(1)}, bf16[64,4096]{1,0:T(8,128)(2,1)S(1)}, u32[]{:S(2)}, u32[]{:S(2)}) collective-permute-start(bf16[64,4096]{1,0:T(8,128)(2,1)S(1)} %get-tuple-element.56.field), channel_id=1, source_target_pairs={{0,127},{1,2},{2,1},{3,4},{4,3},{5,6},{6,5},{7,8},{8,7},{9,10},{10... | collective-permute-start | bytes 1572872 | tf_op jit(solution)/shard_map/ppermute | solution.py:434
  7.6 10.6 %all-to-all-start = ((bf16[128,16,128]{2,1,0:T(8,128)(2,1)}), bf16[128,16,128]{2,1,0:T(8,128)(2,1)S(1)}, u32[]{:S(2)}, u32[]{:S(2)}) async-start(bf16[128,16,128]{2,1,0:T(8,128)(2,1)} %get-tuple-element.55), calls=%async_computation | async-start | bytes 1048576 | tf_op jit(solution)/shard_map/all_to_all | solution.py:436
  18.2 10.2 %setup.1 = (f32[17,64,256]{2,1,0:T(8,128)S(1)}, bf16[88,256,256]{2,1,0:T(8,128)(2,1)S(1)}, bf16[2,16,16,4096]{3,2,1,0:T(8,128)(2,1)S(1)}, bf16[2,2,256,256]{3,2,...) custom-call(s32[5,16]{1,0:T(8,128)S(1)} %bitcast.9, s32[16]{0:T(128)S(1)} %copy-done.11, ...), custom_call_target="tpu_custom_call" | custom-call | flops 335544320 | bytes 4194304 | tf_op jit(solution)/shard_map/setup/pallas_call | solution.py:439
  28.4 2.8 %others.5 = (f32[17,64,256]{2,1,0:T(8,128)S(1)}, f32[256,128]{1,0:T(8,128)S(1)}) custom-call(s32[2,3,88]{2,1,0:T(4,128)S(1)} %get-tuple-element.58.lists.refs_0_, s32[2]{0:T(128)S(1)} %get-tuple-element.59.counts.refs_1_, bf16[88,256,256]{2,1,0:T(8,128)(2,1)S(1)} %get-tuple-element.60.tiles, ...), custom_call_target="tpu_custom_call", output_to_operand_aliasing={{0}: (5, {})} | custom-call | flops 335544320 | bytes 4194304 | tf_op jit(solution)/shard_map/others/pallas_call | solution.py:477
  32.0 3.7 %far.4 = (bf16[64,4096]{1,0:T(8,128)(2,1)S(1)}, bf16[128,16,128]{2,1,0:T(8,128)(2,1)}, f32[5,64,4096]{2,1,0:T(8,128)}, f32[64,2048]{1,0:T(8,128)S(1)}) custom-call(s32[16,128]{1,0:T(8,128)S(1)} %bitcast.4, s32[128]{0:T(128)S(1)} %copy-done.9, s32[1,128]{1,0:T(1,128)S(1)} %get-tuple-element.54.refs_2_, ...), custom_call_target="tpu_custom_call", output_to_operand_aliasing={{2}: (8, {})} | custom-call | flops 268435456 | bytes 4194304 | tf_op jit(solution)/shard_map/far/pallas_call | solution.py:482
  35.7 1.2 collective-permute-start.2
  36.9 9.8 %all-to-all-start.1 = ((bf16[128,16,128]{2,1,0:T(8,128)(2,1)}), bf16[128,16,128]{2,1,0:T(8,128)(2,1)S(1)}, u32[]{:S(2)}, u32[]{:S(2)}) async-start(bf16[128,16,128]{2,1,0:T(8,128)(2,1)} %get-tuple-element.66), calls=%async_computation.1 | async-start | bytes 1048576 | tf_op jit(solution)/shard_map/all_to_all | solution.py:436
  48.5 5.7 %local.4 = (f32[17,64,256]{2,1,0:T(8,128)S(1)}, bf16[88,256,256]{2,1,0:T(8,128)(2,1)S(1)}, bf16[2,16,16,4096]{3,2,1,0:T(8,128)(2,1)S(1)}, f32[5,64,4096]{2,1,0:T(8,128)}) custom-call(s32[2,3,88]{2,1,0:T(4,128)S(1)} %get-tuple-element.58.lists.refs_0_, s32[2]{0:T(128)S(1)} %get-tuple-element.59.counts.refs_1_, ...), custom_call_target="tpu_custom_call", output_to_operand_aliasing={{3}: (7, {})} | custom-call | flops 335544320 | bytes 4194304 | tf_op jit(solution)/shard_map/local/pallas_call | solution.py:453
  54.3 2.8 %others.6 = (f32[17,64,256]{2,1,0:T(8,128)S(1)}, f32[256,128]{1,0:T(8,128)S(1)}) custom-call(s32[2,3,88]{2,1,0:T(4,128)S(1)} %get-tuple-element.58.lists.refs_0_, s32[2]{0:T(128)S(1)} %get-tuple-element.59.counts.refs_1_, bf16[88,256,256]{2,1,0:T(8,128)(2,1)S(1)} %get-tuple-element.70.tiles, ...), custom_call_target="tpu_custom_call", output_to_operand_aliasing={{0}: (5, {})} | custom-call | flops 335544320 | bytes 4194304 | tf_op jit(solution)/shard_map/others/pallas_call | solution.py:477
  57.1 3.4 %all-to-all-done.1.refs_3_ = bf16[128,16,128]{2,1,0:T(8,128)(2,1)S(1)} async-done(((bf16[128,16,128]{2,1,0:T(8,128)(2,1)}), bf16[128,16,128]{2,1,0:T(8,128)(2,1)S(1)}, u32[]{:S(2)}, u32[]{:S(2)}) %all-to-all-start.1) | async-done | bytes 524320 | tf_op jit(solution)/shard_map/all_to_all | solution.py:436
  60.5 3.7 %far.5 = (bf16[64,4096]{1,0:T(8,128)(2,1)S(1)}, bf16[128,16,128]{2,1,0:T(8,128)(2,1)}, f32[5,64,4096]{2,1,0:T(8,128)}, f32[64,2048]{1,0:T(8,128)S(1)}) custom-call(s32[16,128]{1,0:T(8,128)S(1)} %bitcast.5, s32[128]{0:T(128)S(1)} %copy-done.9, s32[1,128]{1,0:T(1,128)S(1)} %get-tuple-element.54.refs_2_, ...), custom_call_target="tpu_custom_call", output_to_operand_aliasing={{2}: (8, {})} | custom-call | flops 268435456 | bytes 4194304 | tf_op jit(solution)/shard_map/far/pallas_call | solution.py:482
  64.2 1.2 collective-permute-start.4
  65.5 8.1 %all-to-all-start.2 = ((bf16[128,16,128]{2,1,0:T(8,128)(2,1)}), bf16[128,16,128]{2,1,0:T(8,128)(2,1)S(1)}, u32[]{:S(2)}, u32[]{:S(2)}) async-start(bf16[128,16,128]{2,1,0:T(8,128)(2,1)} %get-tuple-element.76), calls=%async_computation.2 | async-start | bytes 1048576 | tf_op jit(solution)/shard_map/all_to_all | solution.py:436
  75.4 5.7 %local.5 = (f32[17,64,256]{2,1,0:T(8,128)S(1)}, bf16[88,256,256]{2,1,0:T(8,128)(2,1)S(1)}, bf16[2,16,16,4096]{3,2,1,0:T(8,128)(2,1)S(1)}, f32[5,64,4096]{2,1,0:T(8,128)}) custom-call(s32[2,3,88]{2,1,0:T(4,128)S(1)} %get-tuple-element.58.lists.refs_0_, s32[2]{0:T(128)S(1)} %get-tuple-element.59.counts.refs_1_, ...), custom_call_target="tpu_custom_call", output_to_operand_aliasing={{3}: (7, {})} | custom-call | flops 335544320 | bytes 4194304 | tf_op jit(solution)/shard_map/local/pallas_call | solution.py:453
  81.2 2.8 %others.7 = (f32[17,64,256]{2,1,0:T(8,128)S(1)}, f32[256,128]{1,0:T(8,128)S(1)}) custom-call(s32[2,3,88]{2,1,0:T(4,128)S(1)} %get-tuple-element.58.lists.refs_0_, s32[2]{0:T(128)S(1)} %get-tuple-element.59.counts.refs_1_, bf16[88,256,256]{2,1,0:T(8,128)(2,1)S(1)} %get-tuple-element.80.tiles, ...), custom_call_target="tpu_custom_call", output_to_operand_aliasing={{0}: (5, {})} | custom-call | flops 335544320 | bytes 4194304 | tf_op jit(solution)/shard_map/others/pallas_call | solution.py:477
  84.0 3.2 %all-to-all-done.2.refs_3_ = bf16[128,16,128]{2,1,0:T(8,128)(2,1)S(1)} async-done(((bf16[128,16,128]{2,1,0:T(8,128)(2,1)}), bf16[128,16,128]{2,1,0:T(8,128)(2,1)S(1)}, u32[]{:S(2)}, u32[]{:S(2)}) %all-to-all-start.2) | async-done | bytes 524320 | tf_op jit(solution)/shard_map/all_to_all | solution.py:436
  87.3 3.7 %far.6 = (bf16[64,4096]{1,0:T(8,128)(2,1)S(1)}, bf16[128,16,128]{2,1,0:T(8,128)(2,1)}, f32[5,64,4096]{2,1,0:T(8,128)}, f32[64,2048]{1,0:T(8,128)S(1)}) custom-call(s32[16,128]{1,0:T(8,128)S(1)} %bitcast.6, s32[128]{0:T(128)S(1)} %copy-done.9, s32[1,128]{1,0:T(1,128)S(1)} %get-tuple-element.54.refs_2_, ...), custom_call_target="tpu_custom_call", output_to_operand_aliasing={{2}: (8, {})} | custom-call | flops 268435456 | bytes 4194304 | tf_op jit(solution)/shard_map/far/pallas_call | solution.py:482
  91.0 1.2 collective-permute-start.6
  92.2 8.1 %all-to-all-start.3 = ((bf16[128,16,128]{2,1,0:T(8,128)(2,1)}), bf16[128,16,128]{2,1,0:T(8,128)(2,1)S(1)}, u32[]{:S(2)}, u32[]{:S(2)}) async-start(bf16[128,16,128]{2,1,0:T(8,128)(2,1)} %get-tuple-element.86), calls=%async_computation.3 | async-start | bytes 1048576 | tf_op jit(solution)/shard_map/all_to_all | solution.py:436
  101.2 1.0 copy-done.5
  102.2 5.7 %local.6 = (f32[17,64,256]{2,1,0:T(8,128)S(1)}, bf16[88,256,256]{2,1,0:T(8,128)(2,1)S(1)}, bf16[2,16,16,4096]{3,2,1,0:T(8,128)(2,1)S(1)}, f32[5,64,4096]{2,1,0:T(8,128)}) custom-call(s32[2,3,88]{2,1,0:T(4,128)S(1)} %get-tuple-element.58.lists.refs_0_, s32[2]{0:T(128)S(1)} %get-tuple-element.59.counts.refs_1_, ...), custom_call_target="tpu_custom_call", output_to_operand_aliasing={{3}: (7, {})} | custom-call | flops 335544320 | bytes 4194304 | tf_op jit(solution)/shard_map/local/pallas_call | solution.py:453
  107.9 2.8 %others.8 = (f32[17,64,256]{2,1,0:T(8,128)S(1)}, f32[256,128]{1,0:T(8,128)S(1)}) custom-call(s32[2,3,88]{2,1,0:T(4,128)S(1)} %get-tuple-element.58.lists.refs_0_, s32[2]{0:T(128)S(1)} %get-tuple-element.59.counts.refs_1_, bf16[88,256,256]{2,1,0:T(8,128)(2,1)S(1)} %get-tuple-element.90.tiles, ...), custom_call_target="tpu_custom_call", output_to_operand_aliasing={{0}: (5, {})} | custom-call | flops 335544320 | bytes 4194304 | tf_op jit(solution)/shard_map/others/pallas_call | solution.py:477
  110.8 3.3 %all-to-all-done.3.refs_3_ = bf16[128,16,128]{2,1,0:T(8,128)(2,1)S(1)} async-done(((bf16[128,16,128]{2,1,0:T(8,128)(2,1)}), bf16[128,16,128]{2,1,0:T(8,128)(2,1)S(1)}, u32[]{:S(2)}, u32[]{:S(2)}) %all-to-all-start.3) | async-done | bytes 524320 | tf_op jit(solution)/shard_map/all_to_all | solution.py:436
  114.0 3.7 %far.7 = (bf16[64,4096]{1,0:T(8,128)(2,1)S(1)}, bf16[128,16,128]{2,1,0:T(8,128)(2,1)}, f32[5,64,4096]{2,1,0:T(8,128)}, f32[64,2048]{1,0:T(8,128)S(1)}) custom-call(s32[16,128]{1,0:T(8,128)S(1)} %bitcast.7, s32[128]{0:T(128)S(1)} %copy-done.9, s32[1,128]{1,0:T(1,128)S(1)} %get-tuple-element.54.refs_2_, ...), custom_call_target="tpu_custom_call", output_to_operand_aliasing={{2}: (8, {})} | custom-call | flops 268435456 | bytes 4194304 | tf_op jit(solution)/shard_map/far/pallas_call | solution.py:482
  117.8 1.2 collective-permute-start.8
  119.0 8.1 %all-to-all-start.4 = ((bf16[128,16,128]{2,1,0:T(8,128)(2,1)}), bf16[128,16,128]{2,1,0:T(8,128)(2,1)S(1)}, u32[]{:S(2)}, u32[]{:S(2)}) async-start(bf16[128,16,128]{2,1,0:T(8,128)(2,1)} %get-tuple-element.96), calls=%async_computation.4 | async-start | bytes 1048576 | tf_op jit(solution)/shard_map/all_to_all | solution.py:436
  129.0 4.9 %local.7 = (f32[17,64,256]{2,1,0:T(8,128)S(1)}, bf16[88,256,256]{2,1,0:T(8,128)(2,1)S(1)}, f32[5,64,4096]{2,1,0:T(8,128)}) custom-call(s32[2,3,88]{2,1,0:T(4,128)S(1)} %get-tuple-element.58.lists.refs_0_, s32[2]{0:T(128)S(1)} %get-tuple-element.59.counts.refs_1_, bf16[64,4096]{1,0:T(8,128)(2,1)S(1)} %get-tuple-element.97.refs_2_, ...), custom_call_target="tpu_custom_call", output_to_operand_aliasing={{2}: (6, {})} | custom-call | flops 335544320 | bytes 4194304 | tf_op jit(solution)/shard_map/local/pallas_call | solution.py:453
  133.9 1.5 %others.9.refs_4_ = f32[17,64,256]{2,1,0:T(8,128)S(1)} custom-call(s32[2,3,88]{2,1,0:T(4,128)S(1)} %get-tuple-element.58.lists.refs_0_, s32[2]{0:T(128)S(1)} %get-tuple-element.59.counts.refs_1_, bf16[88,256,256]{2,1,0:T(8,128)(2,1)S(1)} %get-tuple-element.100.tiles, ...), custom_call_target="tpu_custom_call", output_to_operand_aliasing={{}: (4, {})} | custom-call | flops 335544320 | bytes 4194304 | tf_op jit(solution)/shard_map/others/pallas_call | solution.py:467
  135.5 5.4 %all-to-all-done.4.refs_2_ = bf16[128,16,128]{2,1,0:T(8,128)(2,1)S(1)} async-done(((bf16[128,16,128]{2,1,0:T(8,128)(2,1)}), bf16[128,16,128]{2,1,0:T(8,128)(2,1)S(1)}, u32[]{:S(2)}, u32[]{:S(2)}) %all-to-all-start.4) | async-done | bytes 524320 | tf_op jit(solution)/shard_map/all_to_all | solution.py:436
  140.8 3.9 %last.1 = f32[5,64,4096]{2,1,0:T(8,128)} custom-call(s32[16,128]{1,0:T(8,128)S(1)} %bitcast.8, s32[128]{0:T(128)S(1)} %copy-done.9, bf16[128,16,128]{2,1,0:T(8,128)(2,1)S(1)} %all-to-all-done.4.refs_2_, bf16[16,32,4096]{2,1,0:T(8,128)(2,1)} %refs_3_.1, f32[17,64,256]{2,1,0:T(8,128)S(1)} %others.9.refs_4_, ...), custom_call_target="tpu_custom_call", output_to_operand_aliasing={{}: (5, {})} | custom-call | flops 268435456 | bytes 4194304 | tf_op jit(solution)/shard_map/last/pallas_call | solution.py:471
  (38 shorter events, 7.1 us)
Async XLA Ops:
  0.0 18.2 %copy-start.10 = (s32[16,5]{0,1:T(8,128)S(1)}, s32[16,5]{0,1:T(8,128)}, u32[]{:S(2)}) copy-start(s32[16,5]{0,1:T(8,128)} %param.10) | copy-start | bytes 964
  0.0 18.2 %copy-start.11 = (s32[16]{0:T(128)S(1)}, s32[16]{0:T(128)}, u32[]{:S(2)}) copy-start(s32[16]{0:T(128)} %count.1) | copy-start | bytes 196
  4.4 13.8 %collective-permute-start = (bf16[64,4096]{1,0:T(8,128)(2,1)S(1)}, bf16[64,4096]{1,0:T(8,128)(2,1)S(1)}, u32[]{:S(2)}, u32[]{:S(2)}) collective-permute-start(bf16[64,4096]{1,0:T(8,128)(2,1)S(1)} %get-tuple-element.56.field), channel_id=1, source_target_pairs={{0,1},{1,0},{2,3},{3,2},{4,5},{5,4},{6,7},{7,6},{8,9},{9,8},{10,11... | collective-permute-start | bytes 1572872 | tf_op jit(solution)/shard_map/ppermute | solution.py:435
  5.9 22.5 %collective-permute-start.1 = (bf16[64,4096]{1,0:T(8,128)(2,1)S(1)}, bf16[64,4096]{1,0:T(8,128)(2,1)S(1)}, u32[]{:S(2)}, u32[]{:S(2)}) collective-permute-start(bf16[64,4096]{1,0:T(8,128)(2,1)S(1)} %get-tuple-element.56.field), channel_id=1, source_target_pairs={{0,127},{1,2},{2,1},{3,4},{4,3},{5,6},{6,5},{7,8},{8,7},{9,10},{10... | collective-permute-start | bytes 1572872 | tf_op jit(solution)/shard_map/ppermute | solution.py:434
  7.6 24.4 %all-to-all-start = ((bf16[128,16,128]{2,1,0:T(8,128)(2,1)}), bf16[128,16,128]{2,1,0:T(8,128)(2,1)S(1)}, u32[]{:S(2)}, u32[]{:S(2)}) async-start(bf16[128,16,128]{2,1,0:T(8,128)(2,1)} %get-tuple-element.55), calls=%async_computation | async-start | bytes 1048576 | tf_op jit(solution)/shard_map/all_to_all | solution.py:436
  28.4 3.5 %copy-start.8 = (s32[128,16]{0,1:T(8,128)S(1)}, s32[128,16]{0,1:T(8,128)}, u32[]{:S(2)}) copy-start(s32[128,16]{0,1:T(8,128)} %param.12) | copy-start | bytes 24580
  28.4 3.5 %copy-start.9 = (s32[128]{0:T(128)S(1)}, s32[128]{0:T(128)}, u32[]{:S(2)}) copy-start(s32[128]{0:T(128)} %refs_1_.9) | copy-start | bytes 1540
  35.7 11.0 %collective-permute-start.2 = (bf16[64,4096]{1,0:T(8,128)(2,1)S(1)}, bf16[64,4096]{1,0:T(8,128)(2,1)S(1)}, u32[]{:S(2)}, u32[]{:S(2)}) collective-permute-start(bf16[64,4096]{1,0:T(8,128)(2,1)S(1)} %get-tuple-element.67.refs_2_), channel_id=1, source_target_pairs={{0,1},{1,0},{2,3},{3,2},{4,5},{5,4},{6,7},{7,6},{8,9},{9,8},{10,11... | collective-permute-start | bytes 1572872 | tf_op jit(solution)/shard_map/ppermute | solution.py:435
  36.9 17.3 %collective-permute-start.3 = (bf16[64,4096]{1,0:T(8,128)(2,1)S(1)}, bf16[64,4096]{1,0:T(8,128)(2,1)S(1)}, u32[]{:S(2)}, u32[]{:S(2)}) collective-permute-start(bf16[64,4096]{1,0:T(8,128)(2,1)S(1)} %get-tuple-element.67.refs_2_), channel_id=1, source_target_pairs={{0,127},{1,2},{2,1},{3,4},{4,3},{5,6},{6,5},{7,8},{8,7},{9,10},{10... | collective-permute-start | bytes 1572872 | tf_op jit(solution)/shard_map/ppermute | solution.py:434
  36.9 23.6 %all-to-all-start.1 = ((bf16[128,16,128]{2,1,0:T(8,128)(2,1)}), bf16[128,16,128]{2,1,0:T(8,128)(2,1)S(1)}, u32[]{:S(2)}, u32[]{:S(2)}) async-start(bf16[128,16,128]{2,1,0:T(8,128)(2,1)} %get-tuple-element.66), calls=%async_computation.1 | async-start | bytes 1048576 | tf_op jit(solution)/shard_map/all_to_all | solution.py:436
  46.7 0.8 copy-start
  47.5 1.0 copy-start.1
  64.2 9.4 %collective-permute-start.4 = (bf16[64,4096]{1,0:T(8,128)(2,1)S(1)}, bf16[64,4096]{1,0:T(8,128)(2,1)S(1)}, u32[]{:S(2)}, u32[]{:S(2)}) collective-permute-start(bf16[64,4096]{1,0:T(8,128)(2,1)S(1)} %get-tuple-element.77.refs_2_), channel_id=1, source_target_pairs={{0,1},{1,0},{2,3},{3,2},{4,5},{5,4},{6,7},{7,6},{8,9},{9,8},{10,11... | collective-permute-start | bytes 1572872 | tf_op jit(solution)/shard_map/ppermute | solution.py:435
  65.5 15.8 %collective-permute-start.5 = (bf16[64,4096]{1,0:T(8,128)(2,1)S(1)}, bf16[64,4096]{1,0:T(8,128)(2,1)S(1)}, u32[]{:S(2)}, u32[]{:S(2)}) collective-permute-start(bf16[64,4096]{1,0:T(8,128)(2,1)S(1)} %get-tuple-element.77.refs_2_), channel_id=1, source_target_pairs={{0,127},{1,2},{2,1},{3,4},{4,3},{5,6},{6,5},{7,8},{8,7},{9,10},{10... | collective-permute-start | bytes 1572872 | tf_op jit(solution)/shard_map/ppermute | solution.py:434
  65.5 21.8 %all-to-all-start.2 = ((bf16[128,16,128]{2,1,0:T(8,128)(2,1)}), bf16[128,16,128]{2,1,0:T(8,128)(2,1)S(1)}, u32[]{:S(2)}, u32[]{:S(2)}) async-start(bf16[128,16,128]{2,1,0:T(8,128)(2,1)} %get-tuple-element.76), calls=%async_computation.2 | async-start | bytes 1048576 | tf_op jit(solution)/shard_map/all_to_all | solution.py:436
  73.6 0.8 copy-start.2
  74.4 1.0 copy-start.3
  91.0 9.4 %collective-permute-start.6 = (bf16[64,4096]{1,0:T(8,128)(2,1)S(1)}, bf16[64,4096]{1,0:T(8,128)(2,1)S(1)}, u32[]{:S(2)}, u32[]{:S(2)}) collective-permute-start(bf16[64,4096]{1,0:T(8,128)(2,1)S(1)} %get-tuple-element.87.refs_2_), channel_id=1, source_target_pairs={{0,1},{1,0},{2,3},{3,2},{4,5},{5,4},{6,7},{7,6},{8,9},{9,8},{10,11... | collective-permute-start | bytes 1572872 | tf_op jit(solution)/shard_map/ppermute | solution.py:435
  92.2 15.7 %collective-permute-start.7 = (bf16[64,4096]{1,0:T(8,128)(2,1)S(1)}, bf16[64,4096]{1,0:T(8,128)(2,1)S(1)}, u32[]{:S(2)}, u32[]{:S(2)}) collective-permute-start(bf16[64,4096]{1,0:T(8,128)(2,1)S(1)} %get-tuple-element.87.refs_2_), channel_id=1, source_target_pairs={{0,127},{1,2},{2,1},{3,4},{4,3},{5,6},{6,5},{7,8},{8,7},{9,10},{10... | collective-permute-start | bytes 1572872 | tf_op jit(solution)/shard_map/ppermute | solution.py:434
  92.2 21.8 %all-to-all-start.3 = ((bf16[128,16,128]{2,1,0:T(8,128)(2,1)}), bf16[128,16,128]{2,1,0:T(8,128)(2,1)S(1)}, u32[]{:S(2)}, u32[]{:S(2)}) async-start(bf16[128,16,128]{2,1,0:T(8,128)(2,1)} %get-tuple-element.86), calls=%async_computation.3 | async-start | bytes 1048576 | tf_op jit(solution)/shard_map/all_to_all | solution.py:436
  100.4 0.8 copy-start.4
  101.2 1.0 copy-start.5
  117.8 9.4 %collective-permute-start.8 = (bf16[64,4096]{1,0:T(8,128)(2,1)S(1)}, bf16[64,4096]{1,0:T(8,128)(2,1)S(1)}, u32[]{:S(2)}, u32[]{:S(2)}) collective-permute-start(bf16[64,4096]{1,0:T(8,128)(2,1)S(1)} %get-tuple-element.97.refs_2_), channel_id=1, source_target_pairs={{0,1},{1,0},{2,3},{3,2},{4,5},{5,4},{6,7},{7,6},{8,9},{9,8},{10,11... | collective-permute-start | bytes 1572872 | tf_op jit(solution)/shard_map/ppermute | solution.py:435
  119.0 14.9 %collective-permute-start.9 = (bf16[64,4096]{1,0:T(8,128)(2,1)S(1)}, bf16[64,4096]{1,0:T(8,128)(2,1)S(1)}, u32[]{:S(2)}, u32[]{:S(2)}) collective-permute-start(bf16[64,4096]{1,0:T(8,128)(2,1)S(1)} %get-tuple-element.97.refs_2_), channel_id=1, source_target_pairs={{0,127},{1,2},{2,1},{3,4},{4,3},{5,6},{6,5},{7,8},{8,7},{9,10},{10... | collective-permute-start | bytes 1572872 | tf_op jit(solution)/shard_map/ppermute | solution.py:434
  119.0 21.8 %all-to-all-start.4 = ((bf16[128,16,128]{2,1,0:T(8,128)(2,1)}), bf16[128,16,128]{2,1,0:T(8,128)(2,1)S(1)}, u32[]{:S(2)}, u32[]{:S(2)}) async-start(bf16[128,16,128]{2,1,0:T(8,128)(2,1)} %get-tuple-element.96), calls=%async_computation.4 | async-start | bytes 1048576 | tf_op jit(solution)/shard_map/all_to_all | solution.py:436
  127.2 0.8 copy-start.6
  127.9 1.0 copy-start.7
